TPU v7x, 32 devices: a whole 2x2x4 slice. The times are simulated.
32 devices in a mesh: grp: 2 (over y), dim: 4 (over z), ex: 4 (over x, core).
Axes of the slice: x: 2, y: 2, z: 4, core: 2. Of those that a mesh axis runs over, the one named last changes fastest.
Arguments:
- store: bfloat16 [2048, 32768], P(('grp', 'ex'), 'dim'), parts along dimension 0, may hold values from -1000 to 1000
- queries: bfloat16 [256, 32768], P(('grp', 'ex'), 'dim'), parts along dimension 0, may hold values from -24 to 24
- eig_left: float32 [16, 64, 64], P(('grp', 'dim')), parts along dimension 0, may hold values from -1 to 1
- eig_right: float32 [16, 64, 64], P(('grp', 'dim')), parts along dimension 0, may hold values from -1 to 1
- val_left: float32 [16, 64], P(('grp', 'dim')), parts along dimension 0, may hold values from 0.01 to 10
- val_right: float32 [16, 64], P(('grp', 'dim')), parts along dimension 0, may hold values from 0.01 to 10
Outputs:
- scores: float32 [2048, 128], P(('grp', 'ex'), 'dim'), parts along dimension 0
There are 2 independent parts, one for each index of `grp`. A program takes and returns all parts, laid end to end along the dimension named above; each array names one. Nothing has to cross between parts.
All inputs are finite; a program needn't handle non-finite values.
Results may differ from a plain program's by a relative error of at most 0.0029.
Values may be sent and summed in bfloat16 or wider, within the bound.
No kernel may reach another device: no remote copies, remote signals or barrier semaphores. Data moves between devices by JAX's collectives and lax.ppermute only.
A program may use at most 64 MiB of HBM per device.

v0:
```python
import jax
import jax.numpy as jnp
from jax import lax
from jax.sharding import PartitionSpec as P

damping = 0.1


def precondition(queries, eig_left, eig_right, val_left, val_right):
    count = queries.shape[0]
    layers = eig_left.shape[0]
    side_a = eig_left.shape[1]
    side_b = eig_right.shape[1]
    block = queries.astype(jnp.float32).reshape(count, layers, side_a, side_b)
    high = lax.Precision.HIGHEST
    rotated = jnp.einsum("lai,nlab->nlib", eig_left, block, precision=high)
    rotated = jnp.einsum("nlib,lbj->nlij", rotated, eig_right, precision=high)
    scaled = rotated / (val_left[None, :, :, None] * val_right[None, :, None, :] + damping)
    back = jnp.einsum("lai,nlij->nlaj", eig_left, scaled, precision=high)
    back = jnp.einsum("nlaj,lbj->nlab", back, eig_right, precision=high)
    return back.reshape(count, layers * side_a * side_b).astype(jnp.bfloat16)


def local(store, queries, eig_left, eig_right, val_left, val_right):
    precond = precondition(queries, eig_left, eig_right, val_left, val_right)
    squares = jnp.sum(jnp.square(store.astype(jnp.float32)), axis=1)
    total_sq = lax.psum(squares, "dim")
    norm = jnp.sqrt(total_sq + 1e-06)
    partial_value = lax.dot_general(
        store,
        lax.all_gather(precond, "ex", axis=0, tiled=True),
        (((1,), (1,)), ((), ())),
        preferred_element_type=jnp.float32,
    )
    summed = lax.psum_scatter(partial_value, "dim", scatter_dimension=1, tiled=True)
    return summed / norm[:, None]


def solution(mesh):
    in_specs = (
        P(("grp", "ex"), "dim"),
        P(("grp", "ex"), "dim"),
        P(("grp", "dim"), None, None),
        P(("grp", "dim"), None, None),
        P(("grp", "dim"), None),
        P(("grp", "dim"), None),
    )
    out_specs = P(("grp", "ex"), "dim")
    return jax.shard_map(local, mesh=mesh, in_specs=in_specs, out_specs=out_specs, check_vma=False)
```

profile of v0, /device:TPU:0, one launch (start us, length us, event | category | flops | bytes accessed | tf_op | source)
XLA Modules:
  0.0 77.2 jit_solution(4166741185874226652)
XLA Ops:
  6.5 0.0 copy-start
  6.5 0.0 copy-start.1
  6.5 0.0 all-gather.2.cloned.1.call-start
  6.5 2.1 %reshape.16 = bf16[32,2,64,64]{3,2,1,0:T(8,128)(2,1)S(1)} reshape(bf16[32,8192]{1,0:T(8,128)(2,1)} %param.7) | data formatting | bytes 1048576 | tf_op jit(solution)/shard_map/reshape | solution.py:14
  8.6 0.0 copy-done
  8.6 1.2 %fusion.13 = f32[2,32,64,64]{3,2,1,0:T(8,128)S(1)} fusion(bf16[32,2,64,64]{3,2,1,0:T(8,128)(2,1)S(1)} %reshape.16, f32[2,64,64]{2,1,0:T(8,128)S(1)} %copy-done), kind=kOutput, calls=%fused_computation.11 | convolution fusion | flops 201326592 | bytes 1605632 | tf_op jit(solution)/shard_map/lai,nlab->nlib/dot_general | solution.py:16
  9.8 0.0 copy-done.1
  9.8 0.0 copy-start.2
  9.8 0.0 copy-start.3
  9.8 3.4 %fusion.4 = f32[2,32,64,64]{3,2,1,0:T(8,128)S(1)} fusion(f32[2,32,64,64]{3,2,1,0:T(8,128)S(1)} %fusion.13, f32[2,64,64]{2,1,0:T(8,128)S(1)} %copy-done.1), kind=kOutput, calls=%fused_computation.5 | convolution fusion | flops 201326592 | bytes 2129920 | tf_op jit(solution)/shard_map/nlib,lbj->nlij/dot_general | solution.py:17
  13.3 0.0 copy-done.2
  13.3 0.0 copy-done.3
  13.3 0.1 multiply_add_fusion
  13.4 2.1 %fusion.2 = f32[2,32,64,64]{2,3,1,0:T(8,128)S(1)} fusion(f32[2,32,64,64]{3,2,1,0:T(8,128)S(1)} %fusion.4, f32[2,64,64]{2,1,0:T(8,128)S(1)} %multiply_add_fusion, f32[2,64,64]{2,1,0:T(8,128)S(1)} %copy-done), kind=kOutput, calls=%fused_computation.3 | convolution fusion | flops 201588736 | bytes 2162688 | tf_op jit(solution)/shard_map/lai,nlij->nlaj/dot_general | solution.py:19
  15.5 1.9 %fusion.10 = bf16[32,2,64,64]{3,2,0,1:T(8,128)(2,1)S(1)} fusion(f32[2,32,64,64]{2,3,1,0:T(8,128)S(1)} %fusion.2, f32[2,64,64]{2,1,0:T(8,128)S(1)} %copy-done.1), kind=kOutput, calls=%fused_computation.9 | convolution fusion | flops 201588736 | bytes 1605632 | tf_op jit(solution)/shard_map/nlaj,lbj->nlab/dot_general | solution.py:20
  17.4 0.1 copy.7
  17.5 1.6 %convert_element_type.15 = bf16[32,8192]{1,0:T(8,128)(2,1)} reshape(bf16[32,2,64,64]{3,2,1,0:T(8,128)(2,1)S(1)} %copy.7) | data formatting | bytes 1048576 | tf_op jit(solution)/shard_map/convert_element_type | solution.py:21
  19.2 0.0 all-gather.2.cloned.1.call-update
  19.2 0.0 reduce-scatter.2.cloned.1.call-start
  19.2 25.4 %all-gather.2.cloned.1.call-done = bf16[128,8192]{1,0:T(8,128)(2,1)} async-done(((bf16[32,8192]{1,0:T(8,128)(2,1)}), bf16[128,8192]{1,0:T(8,128)(2,1)}) %all-gather.2.cloned.1.call-update) | async-done | bytes 2097168 | tf_op jit(solution)/shard_map/all_gather | solution.py:31
  44.6 5.0 %convolution_bitcast_fusion = f32[256,128]{0,1:T(8,128)} fusion(bf16[128,8192]{1,0:T(8,128)(2,1)} %all-gather.2.cloned.1.call-done, bf16[256,8192]{1,0:T(8,128)(2,1)} %param.6), kind=kOutput, calls=%fused_computation.10 | convolution fusion | flops 536870912 | bytes 6422528 | tf_op jit(solution)/shard_map/dot_general | solution.py:29
  49.6 0.0 reduce-scatter.2.cloned.1.call-update
  49.7 3.1 %multiply_reduce_fusion = f32[256]{0:T(256)S(1)} fusion(bf16[256,8192]{1,0:T(8,128)(2,1)} %param.6), kind=kLoop, calls=%fused_computation | loop fusion | flops 6291200 | bytes 4195328 | tf_op jit(solution)/shard_map/reduce_sum | solution.py:26
  52.8 11.7 %psum.7 = f32[256]{0:T(256)S(1)} all-reduce(f32[256]{0:T(256)S(1)} %multiply_reduce_fusion), channel_id=1, replica_groups=mesh['grp'=2,'dim'=4,'ex'=4] {'dim'}, use_global_device_ids=true, to_apply=%region_2.0 | all-reduce | flops 256 | bytes 2048 | tf_op jit(solution)/shard_map/psum | solution.py:27
  64.5 4.5 %reduce-scatter.2.cloned.1.call-done = f32[256,32]{0,1:T(8,128)} async-done(((f32[256,128]{0,1:T(8,128)}), f32[256,32]{0,1:T(8,128)}) %reduce-scatter.2.cloned.1.call-update) | async-done | bytes 32784 | tf_op jit(solution)/shard_map/reduce_scatter | solution.py:35
  69.0 1.4 %broadcast_divide_fusion = f32[256,32]{0,1:T(8,128)} fusion(f32[256,32]{0,1:T(8,128)} %reduce-scatter.2.cloned.1.call-done, f32[256]{0:T(256)S(1)} %add_sqrt_fusion), kind=kLoop, calls=%fused_computation.19 | loop fusion | flops 8192 | bytes 66560 | tf_op jit(solution)/shard_map/div | solution.py:36
  (1 shorter events, 0.0 us)
Async XLA Ops:
  6.5 2.1 %copy-start = (f32[2,64,64]{2,1,0:T(8,128)S(1)}, f32[2,64,64]{2,1,0:T(8,128)}, u32[]{:S(2)}) copy-start(f32[2,64,64]{2,1,0:T(8,128)} %param.8) | copy-start | bytes 98308
  6.5 3.3 %copy-start.1 = (f32[2,64,64]{2,1,0:T(8,128)S(1)}, f32[2,64,64]{2,1,0:T(8,128)}, u32[]{:S(2)}) copy-start(f32[2,64,64]{2,1,0:T(8,128)} %param.9) | copy-start | bytes 98308
  6.5 38.1 %all-gather.2.cloned.1.call-start = ((), (), s32[]{:S(2)}) async-start(), calls=%async_computation.1 | async-start | bytes 2621440 | tf_op jit(solution)/shard_map/all_gather | solution.py:31
  9.8 3.5 %copy-start.2 = (f32[2,64]{1,0:T(2,128)S(1)}, f32[2,64]{1,0:T(2,128)}, u32[]{:S(2)}) copy-start(f32[2,64]{1,0:T(2,128)} %param.11) | copy-start | bytes 1540
  9.8 3.4 %copy-start.3 = (f32[2,64]{1,0:T(2,128)S(1)}, f32[2,64]{1,0:T(2,128)}, u32[]{:S(2)}) copy-start(f32[2,64]{1,0:T(2,128)} %param.10) | copy-start | bytes 1540
  19.2 49.8 %reduce-scatter.2.cloned.1.call-start = ((), (), s32[]{:S(2)}) async-start(), calls=%async_computation.2 | async-start | bytes 163840 | tf_op jit(solution)/shard_map/reduce_scatter | solution.py:35
Sparse Core Ops, SparseCore 0:
  19.3 25.2 all-gather.1
  49.8 19.1 reduce-scatter.1
where the time goes:
time: 77.5 us; the launch traced here: 77.2 us
  waiting for transfers between devices  29.9 us (39%)
  matrix products  13.6 us (18%)
  between operations  13.5 us (17%)
  blocking collectives  11.7 us (15%)
  other arithmetic  4.57 us (6%)
  local copies, waits for them, and re-layouts  3.81 us (5%)
    all_gather x1, waiting for transfers between devices, local(): lax.all_gather(precond, 'ex', axis=0, tiled=True)  25.4 us
    psum x1, blocking collectives, local(): total_sq = lax.psum(squares, 'dim')  11.7 us
    dot_general x1, matrix products, local(): lax.dot_general(store, lax.all_gather(precond, 'ex', axis=0, tiled=True),...  5.02 us
    reduce_scatter x1, waiting for transfers between devices, local(): lax.psum_scatter(partial_value, 'dim', scatter_dimension=1, tiled=True)  4.5 us
    dot_general x1, matrix products, precondition(): rotated = jnp.einsum('nlib,lbj->nlij', rotated, eig_right, precision=high)  3.42 us
    reduce_sum x1, other arithmetic, local(): squares = jnp.sum(jnp.square(store.astype(jnp.float32)), axis=1)  3.1 us
    dot_general x1, matrix products, precondition(): back = jnp.einsum('lai,nlij->nlaj', eig_left, scaled, precision=high)  2.13 us
    reshape x1, local copies, waits for them, and re-layouts, precondition(): block = queries.astype(jnp.float32).reshape(count, layers, side_a, side_b)  2.09 us
  transfers between devices with their start and end apart: 2, of which 2 were waited for; matrix products, arithmetic and copies ran while one was open for 4% of the time, Pallas kernels for 0%

commit v1 on v0

v1 whole, which is shorter than its diff:
```python
import functools

import jax
import jax.numpy as jnp
from jax import lax
from jax.experimental import pallas as pl
from jax.experimental.pallas import tpu as pltpu
from jax.sharding import PartitionSpec as P

damping = 0.1
f32, bf16 = jnp.float32, jnp.bfloat16
WHOLE = pl.BlockSpec(memory_space=pltpu.VMEM)
HBM = pl.BlockSpec(memory_space=pl.ANY)
SIDE = 64
LANES = 128
QUAD = 4
PAIRS = SIDE // 2
FLAT = SIDE * SIDE


def near(x):
    return pltpu.with_memory_space_constraint(x, pltpu.VMEM)


def call(body, name, outs, ins, scratch=(), flops=0, moved=0, specs=None):
    return pl.pallas_call(
        body,
        out_shape=outs,
        in_specs=specs or [WHOLE] * len(ins),
        out_specs=jax.tree.map(lambda _: WHOLE, outs, is_leaf=lambda o: hasattr(o, "shape")),
        scratch_shapes=scratch,
        cost_estimate=pl.CostEstimate(flops=flops, bytes_accessed=moved, transcendentals=0),
        compiler_params=pltpu.CompilerParams(vmem_limit_bytes=40 * 2**20),
        name=name,
    )(*ins)


def split(x):
    high = x.astype(bf16)
    return high, (x - high.astype(f32)).astype(bf16)


def mm(a, b):
    return jnp.dot(a, b, preferred_element_type=f32)


def factors_body(queries, left, right, val_left, val_right, *refs):
    to_high, to_low, back_high, back_low, turn, unturn, unturn_low, inverse = refs[:8]
    copies = []
    for layer, here in enumerate(refs[8:-1]):
        part = pl.ds(layer * FLAT, FLAT)
        copies.append(pltpu.make_async_copy(queries.at[:, part], here, refs[-1].at[layer]))
        copies[-1].start()
    for layer in range(left.shape[0]):
        block = lax.broadcasted_iota(jnp.int32, (PAIRS, QUAD * SIDE), 1) // SIDE
        rows = []
        for low in range(2):
            part = left[layer, pl.ds(low, PAIRS, stride=2), :]
            wide = jnp.concatenate([part] * QUAD, axis=1)
            rows += [jnp.where(block == quad, wide, 0.0) for quad in range(QUAD)]
        table = jnp.concatenate(rows, axis=0)
        to_high[layer], to_low[layer] = split(table)
        back_high[layer], back_low[layer] = split(table.T)
        twice = jnp.concatenate([right[layer]] * 2, axis=1)
        half = lax.broadcasted_iota(jnp.int32, (SIDE, LANES), 1) // SIDE
        table = jnp.concatenate([jnp.where(half == low, twice, 0.0) for low in range(2)], axis=0)
        turn[layer] = jnp.concatenate(split(table), axis=0)
        high, rest = split(table.T)
        unturn[layer] = jnp.concatenate([high, high], axis=0)
        unturn_low[layer] = rest
        along = jnp.concatenate([val_left[layer : layer + 1, :]] * QUAD, axis=1)
        down = jnp.broadcast_to(val_right[layer : layer + 1, :], (SIDE, SIDE)).T
        inverse[layer] = 1.0 / (along * jnp.concatenate([down] * QUAD, axis=1) + damping)
    for copy in copies:
        copy.wait()


def factors(queries, left, right, val_left, val_right):
    layers = left.shape[0]
    shapes = [((256, 256), bf16)] * 4 + [((256, 128), bf16)] * 2 + [((128, 128), bf16), ((64, 256), f32)]
    outs = [pltpu.VMEM((layers, *shape), kind) for shape, kind in shapes]
    outs += [pltpu.VMEM((queries.shape[0], FLAT), bf16)] * layers
    outs = call(
        factors_body,
        "factors",
        outs,
        (queries, left, right, val_left, val_right),
        [pltpu.SemaphoreType.DMA((layers,))],
        flops=10**6,
        moved=2**20,
        specs=[HBM] + [WHOLE] * 4,
    )
    return outs[:8], outs[8:]


def precondition_body(layer, queries, *refs):
    tables, outs, buffer = refs[:8], refs[8:-1], refs[-1]
    to_high, to_low, back_high, back_low, turn, unturn, unturn_low, inverse = [r[layer] for r in tables]
    count = queries.shape[0]
    groups = count // QUAD
    x = jnp.concatenate([queries[:, a * LANES : (a + 1) * LANES] for a in range(PAIRS)], axis=0)
    buffer[...] = mm(jnp.concatenate([x, x], axis=1), turn)
    turned = []
    for group in range(groups):
        t = jnp.concatenate([buffer[pl.ds(QUAD * group + k, PAIRS, stride=count), :] for k in range(QUAD)], axis=0).T
        turned.append(jnp.concatenate([t[:SIDE], t[SIDE:]], axis=1))
    high, low = split(jnp.concatenate(turned, axis=0))
    t = mm(high, to_high) + (mm(low, to_high) + mm(high, to_low))
    high, low = split(t * jnp.concatenate([inverse] * groups, axis=0))
    t = mm(high, back_high) + (mm(low, back_high) + mm(high, back_low))
    rows = []
    for group in range(groups):
        u = t[SIDE * group : SIDE * (group + 1)]
        rows.append(jnp.concatenate([u[:, :LANES], u[:, LANES:]], axis=0).T)
    high, low = split(jnp.concatenate(rows, axis=0))
    buffer[...] = mm(jnp.concatenate([high, low], axis=1), unturn) + mm(high, unturn_low)
    a = 0
    for out in outs:
        for column in range(0, out.shape[1], LANES):
            out[:, column : column + LANES] = buffer[pl.ds(a, count, stride=PAIRS), :].astype(bf16)
            a += 1


def precondition(queries, tables, layer, widths):
    count = queries.shape[0]
    outs = [pltpu.VMEM((count, width), bf16) for width in widths]
    return call(
        functools.partial(precondition_body, layer),
        f"precondition_{layer}",
        outs,
        [near(x) for x in (queries, *tables)],
        [pltpu.VMEM((count * PAIRS, LANES), f32)],
        flops=count * FLAT * SIDE * 8 * 3,
        moved=2 * 2**20,
    )


def squares_body(store, held, out, sems):
    rows, columns = store.shape
    width = min(columns, 1024)
    copies = []
    for index in range(columns // width):
        part = pl.ds(index * width, width)
        copies.append(pltpu.make_async_copy(store.at[:, part], held.at[:, part], sems.at[index]))
        copies[-1].start()
    total = jnp.zeros((rows, LANES), f32)
    for index, copy in enumerate(copies):
        copy.wait()
        for column in range(index * width, (index + 1) * width, LANES):
            x = held[:, column : column + LANES].astype(f32)
            total += x * x
    out[...] = jnp.broadcast_to(jnp.sum(total.T, axis=0, keepdims=True), out.shape)


def squares(store):
    rows, columns = store.shape
    return call(
        squares_body,
        "squares",
        [pltpu.VMEM((rows, columns), bf16), pltpu.VMEM((8, rows), f32)],
        (store,),
        [pltpu.SemaphoreType.DMA((max(1, columns // 1024),))],
        flops=2 * rows * columns,
        moved=8 * 2**20,
        specs=[HBM],
    )


def dot_rows(pieces, held, first):
    x = jnp.concatenate([p[...] for p in pieces], axis=0)
    return lax.dot_general(x, held[:, first : first + x.shape[1]], (((1,), (1,)), ((), ())), preferred_element_type=f32)


def partial_body(first, started, *refs):
    held, pieces, out = refs[0], refs[1 + started : -1], refs[-1]
    value = dot_rows(pieces, held, first)
    out[...] = refs[1][...] + value if started else value


def last_body(first, partners, *refs):
    held, before, sq, pieces = refs[0], refs[1], refs[2], refs[3 : -len(partners) - 1]
    outs, total = refs[-len(partners) - 1 : -1], refs[-1]
    total[...] = before[...] + dot_rows(pieces, held, first)
    count = pieces[0].shape[0]
    ex, dim = lax.axis_index("ex"), lax.axis_index("dim")
    chips = len(pieces) // 2
    for out, partner in zip(outs, partners):
        block = partner(dim)
        apart = lax.rem(ex // 2 - block // 2 + chips, chips)
        place = 2 * apart + (ex % 2 + block % 2) % 2
        out[:count] = total[pl.ds(pl.multiple_of(place * count, count), count), :]
        out[count:] = sq[...]


def finish_body(*refs):
    out = refs[-1]
    total = refs[0][...]
    for r in refs[1:-1]:
        total = total + r[...]
    count = out.shape[1]
    scores = total[:count] / jnp.sqrt(total[count : count + 1] + 1e-06)
    out[...] = scores.T


def local(dims, exs, store, queries, eig_left, eig_right, val_left, val_right):
    layers = eig_left.shape[0]
    count, rows = queries.shape[0], store.shape[0]
    chips = exs // 2
    across = [(e, e ^ 1) for e in range(exs)]

    tables, here = factors(queries, eig_left, eig_right, val_left, val_right)
    pieces = []
    for layer in range(layers):
        widths = (FLAT,) if layer < layers - 1 else (FLAT // 2, FLAT // 2)
        pieces += precondition(here[layer], tables, layer, widths)
    held, sq = squares(store)

    total, first = None, 0
    for index, piece in enumerate(pieces):
        parts = [piece, lax.ppermute(piece, "ex", across)]
        for step in range(1, chips):
            came = lax.ppermute(piece, "ex", [(e, (e + 2 * step) % exs) for e in range(exs)])
            parts += [came, lax.ppermute(came, "ex", across)]
        width = piece.shape[1]
        ins = (held, *(() if total is None else (total,)), *((sq,) if index == len(pieces) - 1 else ()), *parts)
        ins = [near(x) for x in ins]
        cost = dict(flops=2 * count * exs * rows * width, moved=2 * 2**20)
        if index < len(pieces) - 1:
            body = functools.partial(partial_body, first, int(index > 0))
            total = call(body, f"scores_{index}", pltpu.VMEM((count * exs, rows), f32), ins, **cost)
        else:
            if dims & (dims - 1):
                links = [[(z, (z + k) % dims) for z in range(dims)] for k in range(dims)]
                partners = [lambda z, k=k: lax.rem(z + k, dims) for k in range(dims)]
            else:
                links = [[(z, z ^ k) for z in range(dims)] for k in range(dims)]
                partners = [lambda z, k=k: lax.bitwise_xor(z, k) for k in range(dims)]
            body = functools.partial(last_body, first, partners)
            outs = [pltpu.VMEM((count + 8, rows), f32) for _ in range(dims)]
            sent = call(body, "scores_last", outs, ins, [pltpu.VMEM((count * exs, rows), f32)], **cost)
        first += width
    came = [sent[0]] + [lax.ppermute(sent[k], "dim", links[k]) for k in reversed(range(1, dims))]
    return call(
        finish_body, "finish", jax.ShapeDtypeStruct((rows, count), f32), [near(c) for c in came], flops=10**6, moved=2**20
    )


def solution(mesh):
    in_specs = (
        P(("grp", "ex"), "dim"),
        P(("grp", "ex"), "dim"),
        P(("grp", "dim"), None, None),
        P(("grp", "dim"), None, None),
        P(("grp", "dim"), None),
        P(("grp", "dim"), None),
    )
    out_specs = P(("grp", "ex"), "dim")
    body = functools.partial(local, mesh.shape["dim"], mesh.shape["ex"])
    return jax.shard_map(body, mesh=mesh, in_specs=in_specs, out_specs=out_specs, check_vma=False)
```

time: 77.5 us -> 42.6 us (0.55)
  matrix products: 13.6 us -> 0 us
  between operations: 13.5 us -> 0.12 us
  blocking collectives: 11.7 us -> 0 us
  waiting for transfers between devices: 29.9 us -> 18.8 us
  starting transfers between devices: 0.04 us -> 10.1 us
  Pallas kernels: 0 us -> 8.51 us
  other arithmetic: 4.57 us -> 0 us
  local copies, waits for them, and re-layouts: 3.81 us -> 4.77 us
    all_gather x1 -> x0, waiting for transfers between devices: 25.4 us -> none  [local(): lax.all_gather(precond, 'ex', axis=0, tiled=True)]
    ppermute x0 -> x12, waiting for transfers between devices: none -> 18.8 us  [the longest x3 13 us: local(): lax.ppermute(piece, 'ex', [(e, (e + 2 * step) % exs) for e in range(exs)])]
    dot_general x5 -> x0, matrix products: 13.6 us -> none  [the longest x1 5.02 us: local(): lax.dot_general(store, lax.all_gather(precond, 'ex', axis=0, tiled=True),...]
    psum x1 -> x0, blocking collectives: 11.7 us -> none  [local(): total_sq = lax.psum(squares, 'dim')]
    ppermute x0 -> x12, starting transfers between devices: none -> 10.1 us  [the longest x3 5.1 us: local(): lax.ppermute(piece, 'ex', [(e, (e + 2 * step) % exs) for e in range(exs)])]
    pallas_call x0 -> x8, Pallas kernels: none -> 8.51 us  [call(): pl.pallas_call(body, out_shape=outs, in_specs=specs or [WHOLE] * len(ins)...]
    reduce_scatter x1 -> x0, waiting for transfers between devices: 4.5 us -> none  [local(): lax.psum_scatter(partial_value, 'dim', scatter_dimension=1, tiled=True)]
    unnamed x8 -> x12, local copies, waits for them, and re-layouts: 0.02 us -> 4.08 us
  transfers between devices with their start and end apart: 2 -> 12, of which waited for: 2 -> 6; matrix products, arithmetic and copies ran while one was open for 4% -> 0% of each run, Pallas kernels for 0% -> 12%
where the time goes in v1:
time: 42.6 us; the launch traced here: 42.3 us
  waiting for transfers between devices  18.8 us (44%)
  starting transfers between devices  10.1 us (24%)
  Pallas kernels  8.51 us (20%)
  local copies, waits for them, and re-layouts  4.77 us (11%)
    ppermute x3, waiting for transfers between devices, local(): lax.ppermute(piece, 'ex', [(e, (e + 2 * step) % exs) for e in range(exs)])  13 us
    pallas_call x8, Pallas kernels, call(): pl.pallas_call(body, out_shape=outs, in_specs=specs or [WHOLE] * len(ins)...  8.51 us
    ppermute x3, waiting for transfers between devices, local(): lax.ppermute(sent[k], 'dim', links[k])  5.8 us
    ppermute x3, starting transfers between devices, local(): lax.ppermute(piece, 'ex', [(e, (e + 2 * step) % exs) for e in range(exs)])  5.1 us
    ppermute x3, starting transfers between devices, local(): lax.ppermute(sent[k], 'dim', links[k])  4.48 us
    unnamed x12, local copies, waits for them, and re-layouts  4.08 us
  transfers between devices with their start and end apart: 12, of which 6 were waited for; matrix products, arithmetic and copies ran while one was open for 0% of the time, Pallas kernels for 12%

profile of v1, /device:TPU:0, one launch (start us, length us, event | category | flops | bytes accessed | tf_op | source)
XLA Modules:
  0.0 42.3 jit_solution(5765680449774645276)
XLA Ops:
  0.0 0.0 copy-start.1
  0.0 1.0 %copy-done.1 = bf16[32,8192]{1,0:T(8,128)(2,1)S(1)} copy-done((bf16[32,8192]{1,0:T(8,128)(2,1)S(1)}, bf16[32,8192]{1,0:T(8,128)(2,1)}, u32[]{:S(2)}) %copy-start.1) | copy-done | bytes 524312
  1.0 0.0 copy-start.2
  1.0 0.8 %copy-done.2 = f32[2,64,64]{2,1,0:T(8,128)S(1)} copy-done((f32[2,64,64]{2,1,0:T(8,128)S(1)}, f32[2,64,64]{2,1,0:T(8,128)}, u32[]{:S(2)}) %copy-start.2) | copy-done | bytes 32792
  1.9 0.0 copy-start.3
  1.9 0.8 %copy-done.3 = f32[2,64,64]{2,1,0:T(8,128)S(1)} copy-done((f32[2,64,64]{2,1,0:T(8,128)S(1)}, f32[2,64,64]{2,1,0:T(8,128)}, u32[]{:S(2)}) %copy-start.3) | copy-done | bytes 32792
  2.7 0.0 copy-start.4
  2.7 0.7 %copy-done.4 = f32[2,64]{1,0:T(2,128)S(1)} copy-done((f32[2,64]{1,0:T(2,128)S(1)}, f32[2,64]{1,0:T(2,128)}, u32[]{:S(2)}) %copy-start.4) | copy-done | bytes 536
  3.4 0.0 copy-start.5
  3.4 0.7 %copy-done.5 = f32[2,64]{1,0:T(2,128)S(1)} copy-done((f32[2,64]{1,0:T(2,128)S(1)}, f32[2,64]{1,0:T(2,128)}, u32[]{:S(2)}) %copy-start.5) | copy-done | bytes 536
  4.1 0.0 copy-start
  4.1 0.6 %factors.1 = (bf16[2,256,256]{2,1,0:T(8,128)(2,1)S(1)}, bf16[2,256,256]{2,1,0:T(8,128)(2,1)S(1)}, bf16[2,256,256]{2,1,0:T(8,128)(2,1)S(1)}, bf16[2,256,256]{2,1,...) custom-call(bf16[32,8192]{1,0:T(8,128)(2,1)S(1)} %copy-done.1, ...), custom_call_target="tpu_custom_call" | custom-call | flops 1000000 | bytes 1048576 | tf_op jit(solution)/shard_map/factors/pallas_call | solution.py:26
  4.7 2.1 %precondition_0.1.refs_1_ = bf16[32,4096]{1,0:T(8,128)(2,1)S(1)} custom-call(bf16[32,4096]{1,0:T(8,128)(2,1)S(1)} %get-tuple-element.24.queries, bf16[2,256,256]{2,1,0:T(8,128)(2,1)S(1)} %get-tuple-element.25.refs_0_, bf16[2,256,256]{2,1,0:T(8,128)(2,1)S(1)} %get-tuple-element.26.refs_1_, bf16[2,256,256]{2,1,0:T(8,128)(2,1)S(1)} %get-tuple-element.27.refs_2_, ...), custom_call_target="tpu_custom_call" | custom-call | flops 201326592 | bytes 2097152 | tf_op jit(solution)/shard_map/precondition_0/pallas_call | solution.py:26
  6.8 3.0 %collective-permute-start.1 = (bf16[32,4096]{1,0:T(8,128)(2,1)S(1)}, bf16[32,4096]{1,0:T(8,128)(2,1)S(1)}, u32[]{:S(2)}, u32[]{:S(2)}) collective-permute-start(bf16[32,4096]{1,0:T(8,128)(2,1)S(1)} %precondition_0.1.refs_1_), channel_id=1, source_target_pairs={{0,2},{1,3},{2,0},{3,1},{4,6},{5,7},{6,4},{7,5},{8,10},{9,11},{10,... | collective-permute-start | bytes 786440 | tf_op jit(solution)/shard_map/ppermute | solution.py:222
  9.8 0.0 collective-permute-start
  9.8 6.3 %collective-permute-done.1.refs_3_ = bf16[32,4096]{1,0:T(8,128)(2,1)S(1)} collective-permute-done((bf16[32,4096]{1,0:T(8,128)(2,1)S(1)}, bf16[32,4096]{1,0:T(8,128)(2,1)S(1)}, u32[]{:S(2)}, u32[]{:S(2)}) %collective-permute-start.1) | collective-permute-done | bytes 262176 | tf_op jit(solution)/shard_map/ppermute | solution.py:222
  16.1 0.0 collective-permute-start.2
  16.1 2.1 %precondition_1.1 = (bf16[32,2048]{1,0:T(8,128)(2,1)S(1)}, bf16[32,2048]{1,0:T(8,128)(2,1)S(1)}) custom-call(bf16[32,4096]{1,0:T(8,128)(2,1)S(1)} %get-tuple-element.33.queries, bf16[2,256,256]{2,1,0:T(8,128)(2,1)S(1)} %get-tuple-element.25.refs_0_, bf16[2,256,256]{2,1,0:T(8,128)(2,1)S(1)} %get-tuple-element.26.refs_1_, ...), custom_call_target="tpu_custom_call" | custom-call | flops 201326592 | bytes 2097152 | tf_op jit(solution)/shard_map/precondition_1/pallas_call | solution.py:26
  18.3 1.8 %collective-permute-start.4 = (bf16[32,2048]{1,0:T(8,128)(2,1)S(1)}, bf16[32,2048]{1,0:T(8,128)(2,1)S(1)}, u32[]{:S(2)}, u32[]{:S(2)}) collective-permute-start(bf16[32,2048]{1,0:T(8,128)(2,1)S(1)} %get-tuple-element.34.refs_2_), channel_id=1, source_target_pairs={{0,2},{1,3},{2,0},{3,1},{4,6},{5,7},{6,4},{7,5},{8,10},{9,11},{10,... | collective-permute-start | bytes 393224 | tf_op jit(solution)/shard_map/ppermute | solution.py:222
  20.1 0.3 collective-permute-start.7
  20.4 0.0 collective-permute-start.3
  20.4 4.2 %collective-permute-done.4.refs_4_ = bf16[32,2048]{1,0:T(8,128)(2,1)S(1)} collective-permute-done((bf16[32,2048]{1,0:T(8,128)(2,1)S(1)}, bf16[32,2048]{1,0:T(8,128)(2,1)S(1)}, u32[]{:S(2)}, u32[]{:S(2)}) %collective-permute-start.4) | collective-permute-done | bytes 131104 | tf_op jit(solution)/shard_map/ppermute | solution.py:222
  24.6 0.0 collective-permute-start.5
  24.6 2.4 %collective-permute-done.7.refs_5_ = bf16[32,2048]{1,0:T(8,128)(2,1)S(1)} collective-permute-done((bf16[32,2048]{1,0:T(8,128)(2,1)S(1)}, bf16[32,2048]{1,0:T(8,128)(2,1)S(1)}, u32[]{:S(2)}, u32[]{:S(2)}) %collective-permute-start.7) | collective-permute-done | bytes 131104 | tf_op jit(solution)/shard_map/ppermute | solution.py:222
  27.1 0.0 collective-permute-start.6
  27.1 0.0 collective-permute-done.refs_2_
  27.1 0.5 %collective-permute-start.8 = (bf16[32,2048]{1,0:T(8,128)(2,1)S(1)}, bf16[32,2048]{1,0:T(8,128)(2,1)S(1)}, u32[]{:S(2)}, u32[]{:S(2)}) collective-permute-start(bf16[32,2048]{1,0:T(8,128)(2,1)S(1)} %collective-permute-done.7.refs_5_), channel_id=1, source_target_pairs={{0,1},{1,0},{2,3},{3,2},{4,5},{5,4},{6,7},{7,6},{8,9},{9,8},{10,11... | collective-permute-start | bytes 393224 | tf_op jit(solution)/shard_map/ppermute | solution.py:223
  27.6 0.0 copy-done
  27.6 1.7 %squares.1 = (bf16[256,8192]{1,0:T(8,128)(2,1)S(1)}, f32[8,256]{1,0:T(8,128)S(1)}) custom-call(bf16[256,8192]{1,0:T(8,128)(2,1)S(1)} %copy-done), custom_call_target="tpu_custom_call" | custom-call | flops 4194304 | bytes 8388608 | tf_op jit(solution)/shard_map/squares/pallas_call | solution.py:26
  29.3 0.0 collective-permute-done.2.refs_4_
  29.3 0.8 %scores_0.1.refs_1_ = f32[128,256]{1,0:T(8,128)S(1)} custom-call(bf16[256,8192]{1,0:T(8,128)(2,1)S(1)} %get-tuple-element.23.refs_0_, bf16[32,4096]{1,0:T(8,128)(2,1)S(1)} %precondition_0.1.refs_1_, bf16[32,4096]{1,0:T(8,128)(2,1)S(1)} %collective-permute-done.refs_2_, bf16[32,4096]{1,0:T(8,128)(2,1)S(1)} %collective-permute-done.1.refs_3_, ...), custom_call_target="tpu_custom_call" | custom-call | flops 268435456 | bytes 2097152 | tf_op jit(solution)/shard_map/scores_0/pallas_call | solution.py:26
  30.2 0.0 collective-permute-done.3.refs_3_
  30.2 0.0 collective-permute-done.5.refs_5_
  30.2 0.5 %scores_1.1.refs_1_ = f32[128,256]{1,0:T(8,128)S(1)} custom-call(bf16[256,8192]{1,0:T(8,128)(2,1)S(1)} %get-tuple-element.23.refs_0_, f32[128,256]{1,0:T(8,128)S(1)} %scores_0.1.refs_1_, bf16[32,2048]{1,0:T(8,128)(2,1)S(1)} %get-tuple-element.34.refs_2_, bf16[32,2048]{1,0:T(8,128)(2,1)S(1)} %collective-permute-done.3.refs_3_, ...), custom_call_target="tpu_custom_call" | custom-call | flops 134217728 | bytes 2097152 | tf_op jit(solution)/shard_map/scores_1/pallas_call | solution.py:26
  30.7 0.0 collective-permute-done.6.refs_4_
  30.7 0.0 collective-permute-done.8.refs_6_
  30.7 0.5 %scores_last.1 = (f32[40,256]{1,0:T(8,128)S(1)}, f32[40,256]{1,0:T(8,128)S(1)}, f32[40,256]{1,0:T(8,128)S(1)}, f32[40,256]{1,0:T(8,128)S(1)}) custom-call(bf16[256,8192]{1,0:T(8,128)(2,1)S(1)} %get-tuple-element.23.refs_0_, f32[128,256]{1,0:T(8,128)S(1)} %scores_1.1.refs_1_, f32[8,256]{1,0:T(8,128)S(1)} %get-tuple-element.35.refs_2_, ...), custom_call_target="tpu_custom_call" | custom-call | flops 134217728 | bytes 2097152 | tf_op jit(solution)/shard_map/scores_last/pallas_call | solution.py:26
  31.2 2.9 %collective-permute-start.10 = (f32[40,256]{1,0:T(8,128)S(1)}, f32[40,256]{1,0:T(8,128)S(1)}, u32[]{:S(2)}, u32[]{:S(2)}) collective-permute-start(f32[40,256]{1,0:T(8,128)S(1)} %get-tuple-element.39), channel_id=1, source_target_pairs={{0,8},{4,12},{8,0},{12,4},{1,9},{5,13},{9,1},{13,5},{2,10},{6,14},... | collective-permute-start | bytes 122888 | tf_op jit(solution)/shard_map/ppermute | solution.py:242
  34.1 1.6 %collective-permute-start.11 = (f32[40,256]{1,0:T(8,128)S(1)}, f32[40,256]{1,0:T(8,128)S(1)}, u32[]{:S(2)}, u32[]{:S(2)}) collective-permute-start(f32[40,256]{1,0:T(8,128)S(1)} %get-tuple-element.40), channel_id=1, source_target_pairs={{0,4},{4,0},{8,12},{12,8},{1,5},{5,1},{9,13},{13,9},{2,6},{6,2},{1... | collective-permute-start | bytes 122888 | tf_op jit(solution)/shard_map/ppermute | solution.py:242
  35.7 0.0 collective-permute-start.9
  35.7 1.0 %collective-permute-done.10.refs_2_ = f32[40,256]{1,0:T(8,128)S(1)} collective-permute-done((f32[40,256]{1,0:T(8,128)S(1)}, f32[40,256]{1,0:T(8,128)S(1)}, u32[]{:S(2)}, u32[]{:S(2)}) %collective-permute-start.10) | collective-permute-done | bytes 40992 | tf_op jit(solution)/shard_map/ppermute | solution.py:242
  36.7 1.4 %collective-permute-done.11.refs_3_ = f32[40,256]{1,0:T(8,128)S(1)} collective-permute-done((f32[40,256]{1,0:T(8,128)S(1)}, f32[40,256]{1,0:T(8,128)S(1)}, u32[]{:S(2)}, u32[]{:S(2)}) %collective-permute-start.11) | collective-permute-done | bytes 40992 | tf_op jit(solution)/shard_map/ppermute | solution.py:242
  38.1 3.4 %collective-permute-done.9.refs_1_ = f32[40,256]{1,0:T(8,128)S(1)} collective-permute-done((f32[40,256]{1,0:T(8,128)S(1)}, f32[40,256]{1,0:T(8,128)S(1)}, u32[]{:S(2)}, u32[]{:S(2)}) %collective-permute-start.9) | collective-permute-done | bytes 40992 | tf_op jit(solution)/shard_map/ppermute | solution.py:242
  41.5 0.1 finish.1
  41.6 0.7 %copy.7 = f32[256,32]{0,1:T(8,128)} copy(f32[256,32]{1,0:T(8,128)S(1)} %finish.1) | data formatting | bytes 65536 | tf_op jit(solution)/shard_map/finish/pallas_call | solution.py:26
Async XLA Ops:
  0.0 1.0 %copy-start.1 = (bf16[32,8192]{1,0:T(8,128)(2,1)S(1)}, bf16[32,8192]{1,0:T(8,128)(2,1)}, u32[]{:S(2)}) copy-start(bf16[32,8192]{1,0:T(8,128)(2,1)} %queries.1) | copy-start | bytes 1572868
  1.0 0.8 %copy-start.2 = (f32[2,64,64]{2,1,0:T(8,128)S(1)}, f32[2,64,64]{2,1,0:T(8,128)}, u32[]{:S(2)}) copy-start(f32[2,64,64]{2,1,0:T(8,128)} %left.1) | copy-start | bytes 98308
  1.9 0.8 %copy-start.3 = (f32[2,64,64]{2,1,0:T(8,128)S(1)}, f32[2,64,64]{2,1,0:T(8,128)}, u32[]{:S(2)}) copy-start(f32[2,64,64]{2,1,0:T(8,128)} %right.1) | copy-start | bytes 98308
  2.7 0.7 %copy-start.4 = (f32[2,64]{1,0:T(2,128)S(1)}, f32[2,64]{1,0:T(2,128)}, u32[]{:S(2)}) copy-start(f32[2,64]{1,0:T(2,128)} %val_left.1) | copy-start | bytes 1540
  3.4 0.7 %copy-start.5 = (f32[2,64]{1,0:T(2,128)S(1)}, f32[2,64]{1,0:T(2,128)}, u32[]{:S(2)}) copy-start(f32[2,64]{1,0:T(2,128)} %val_right.1) | copy-start | bytes 1540
  4.1 23.5 %copy-start = (bf16[256,8192]{1,0:T(8,128)(2,1)S(1)}, bf16[256,8192]{1,0:T(8,128)(2,1)}, u32[]{:S(2)}) copy-start(bf16[256,8192]{1,0:T(8,128)(2,1)} %store.1) | copy-start | bytes 12582916
  6.8 9.3 %collective-permute-start.1 = (bf16[32,4096]{1,0:T(8,128)(2,1)S(1)}, bf16[32,4096]{1,0:T(8,128)(2,1)S(1)}, u32[]{:S(2)}, u32[]{:S(2)}) collective-permute-start(bf16[32,4096]{1,0:T(8,128)(2,1)S(1)} %precondition_0.1.refs_1_), channel_id=1, source_target_pairs={{0,2},{1,3},{2,0},{3,1},{4,6},{5,7},{6,4},{7,5},{8,10},{9,11},{10,... | collective-permute-start | bytes 786440 | tf_op jit(solution)/shard_map/ppermute | solution.py:222
  9.8 17.2 %collective-permute-start = (bf16[32,4096]{1,0:T(8,128)(2,1)S(1)}, bf16[32,4096]{1,0:T(8,128)(2,1)S(1)}, u32[]{:S(2)}, u32[]{:S(2)}) collective-permute-start(bf16[32,4096]{1,0:T(8,128)(2,1)S(1)} %precondition_0.1.refs_1_), channel_id=1, source_target_pairs={{0,1},{1,0},{2,3},{3,2},{4,5},{5,4},{6,7},{7,6},{8,9},{9,8},{10,11... | collective-permute-start | bytes 786440 | tf_op jit(solution)/shard_map/ppermute | solution.py:220
  16.1 13.2 %collective-permute-start.2 = (bf16[32,4096]{1,0:T(8,128)(2,1)S(1)}, bf16[32,4096]{1,0:T(8,128)(2,1)S(1)}, u32[]{:S(2)}, u32[]{:S(2)}) collective-permute-start(bf16[32,4096]{1,0:T(8,128)(2,1)S(1)} %collective-permute-done.1.refs_3_), channel_id=1, source_target_pairs={{0,1},{1,0},{2,3},{3,2},{4,5},{5,4},{6,7},{7,6},{8,9},{9,8},{10,11... | collective-permute-start | bytes 786440 | tf_op jit(solution)/shard_map/ppermute | solution.py:223
  18.3 6.4 %collective-permute-start.4 = (bf16[32,2048]{1,0:T(8,128)(2,1)S(1)}, bf16[32,2048]{1,0:T(8,128)(2,1)S(1)}, u32[]{:S(2)}, u32[]{:S(2)}) collective-permute-start(bf16[32,2048]{1,0:T(8,128)(2,1)S(1)} %get-tuple-element.34.refs_2_), channel_id=1, source_target_pairs={{0,2},{1,3},{2,0},{3,1},{4,6},{5,7},{6,4},{7,5},{8,10},{9,11},{10,... | collective-permute-start | bytes 393224 | tf_op jit(solution)/shard_map/ppermute | solution.py:222
  20.1 7.0 %collective-permute-start.7 = (bf16[32,2048]{1,0:T(8,128)(2,1)S(1)}, bf16[32,2048]{1,0:T(8,128)(2,1)S(1)}, u32[]{:S(2)}, u32[]{:S(2)}) collective-permute-start(bf16[32,2048]{1,0:T(8,128)(2,1)S(1)} %get-tuple-element.36.refs_3_), channel_id=1, source_target_pairs={{0,2},{1,3},{2,0},{3,1},{4,6},{5,7},{6,4},{7,5},{8,10},{9,11},{10,... | collective-permute-start | bytes 393224 | tf_op jit(solution)/shard_map/ppermute | solution.py:222
  20.4 9.8 %collective-permute-start.3 = (bf16[32,2048]{1,0:T(8,128)(2,1)S(1)}, bf16[32,2048]{1,0:T(8,128)(2,1)S(1)}, u32[]{:S(2)}, u32[]{:S(2)}) collective-permute-start(bf16[32,2048]{1,0:T(8,128)(2,1)S(1)} %get-tuple-element.34.refs_2_), channel_id=1, source_target_pairs={{0,1},{1,0},{2,3},{3,2},{4,5},{5,4},{6,7},{7,6},{8,9},{9,8},{10,11... | collective-permute-start | bytes 393224 | tf_op jit(solution)/shard_map/ppermute | solution.py:220
  24.6 5.5 %collective-permute-start.5 = (bf16[32,2048]{1,0:T(8,128)(2,1)S(1)}, bf16[32,2048]{1,0:T(8,128)(2,1)S(1)}, u32[]{:S(2)}, u32[]{:S(2)}) collective-permute-start(bf16[32,2048]{1,0:T(8,128)(2,1)S(1)} %collective-permute-done.4.refs_4_), channel_id=1, source_target_pairs={{0,1},{1,0},{2,3},{3,2},{4,5},{5,4},{6,7},{7,6},{8,9},{9,8},{10,11... | collective-permute-start | bytes 393224 | tf_op jit(solution)/shard_map/ppermute | solution.py:223
  27.1 3.6 %collective-permute-start.6 = (bf16[32,2048]{1,0:T(8,128)(2,1)S(1)}, bf16[32,2048]{1,0:T(8,128)(2,1)S(1)}, u32[]{:S(2)}, u32[]{:S(2)}) collective-permute-start(bf16[32,2048]{1,0:T(8,128)(2,1)S(1)} %get-tuple-element.36.refs_3_), channel_id=1, source_target_pairs={{0,1},{1,0},{2,3},{3,2},{4,5},{5,4},{6,7},{7,6},{8,9},{9,8},{10,11... | collective-permute-start | bytes 393224 | tf_op jit(solution)/shard_map/ppermute | solution.py:220
  27.1 3.6 %collective-permute-start.8 = (bf16[32,2048]{1,0:T(8,128)(2,1)S(1)}, bf16[32,2048]{1,0:T(8,128)(2,1)S(1)}, u32[]{:S(2)}, u32[]{:S(2)}) collective-permute-start(bf16[32,2048]{1,0:T(8,128)(2,1)S(1)} %collective-permute-done.7.refs_5_), channel_id=1, source_target_pairs={{0,1},{1,0},{2,3},{3,2},{4,5},{5,4},{6,7},{7,6},{8,9},{9,8},{10,11... | collective-permute-start | bytes 393224 | tf_op jit(solution)/shard_map/ppermute | solution.py:223
  31.2 5.5 %collective-permute-start.10 = (f32[40,256]{1,0:T(8,128)S(1)}, f32[40,256]{1,0:T(8,128)S(1)}, u32[]{:S(2)}, u32[]{:S(2)}) collective-permute-start(f32[40,256]{1,0:T(8,128)S(1)} %get-tuple-element.39), channel_id=1, source_target_pairs={{0,8},{4,12},{8,0},{12,4},{1,9},{5,13},{9,1},{13,5},{2,10},{6,14},... | collective-permute-start | bytes 122888 | tf_op jit(solution)/shard_map/ppermute | solution.py:242
  34.1 4.0 %collective-permute-start.11 = (f32[40,256]{1,0:T(8,128)S(1)}, f32[40,256]{1,0:T(8,128)S(1)}, u32[]{:S(2)}, u32[]{:S(2)}) collective-permute-start(f32[40,256]{1,0:T(8,128)S(1)} %get-tuple-element.40), channel_id=1, source_target_pairs={{0,4},{4,0},{8,12},{12,8},{1,5},{5,1},{9,13},{13,9},{2,6},{6,2},{1... | collective-permute-start | bytes 122888 | tf_op jit(solution)/shard_map/ppermute | solution.py:242
  35.7 5.8 %collective-permute-start.9 = (f32[40,256]{1,0:T(8,128)S(1)}, f32[40,256]{1,0:T(8,128)S(1)}, u32[]{:S(2)}, u32[]{:S(2)}) collective-permute-start(f32[40,256]{1,0:T(8,128)S(1)} %get-tuple-element.38), channel_id=1, source_target_pairs={{0,12},{4,8},{8,4},{12,0},{1,13},{5,9},{9,5},{13,1},{2,14},{6,10},... | collective-permute-start | bytes 122888 | tf_op jit(solution)/shard_map/ppermute | solution.py:242

commit v2 on v0

v2 whole, which is shorter than its diff:
```python
import functools

import jax
import jax.numpy as jnp
from jax import lax
from jax.experimental import pallas as pl
from jax.experimental.pallas import tpu as pltpu
from jax.sharding import PartitionSpec as P

damping = 0.1
f32, bf16 = jnp.float32, jnp.bfloat16
WHOLE = pl.BlockSpec(memory_space=pltpu.VMEM)
HBM = pl.BlockSpec(memory_space=pltpu.HBM)
SIDE = 64
SCALE = 0.02
LANES = 128
QUAD = 4
PAIRS = SIDE // 2
FLAT = SIDE * SIDE
PAD = 8
ROWS = 16


def near(x):
    return pltpu.with_memory_space_constraint(x, pltpu.VMEM)


def far(x):
    return pltpu.with_memory_space_constraint(x, pltpu.HBM)


def after(x, *others):
    return lax.optimization_barrier((x, *others))[0]


def call(body, name, outs, ins, scratch=(), us=1.0, specs=None, to=WHOLE):
    return pl.pallas_call(
        body,
        out_shape=outs,
        in_specs=specs or [WHOLE] * len(ins),
        out_specs=jax.tree.map(lambda _: to, outs, is_leaf=lambda o: hasattr(o, "shape")),
        scratch_shapes=scratch,
        cost_estimate=pl.CostEstimate(flops=int(us * 1.15e9 * SCALE), bytes_accessed=0, transcendentals=0),
        compiler_params=pltpu.CompilerParams(vmem_limit_bytes=40 * 2**20),
        name=name,
    )(*ins)


def split(x):
    high = x.astype(bf16)
    return high, (x - high.astype(f32)).astype(bf16)


def mm(a, b):
    return jnp.dot(a, b, preferred_element_type=f32)


def position():
    ex, dim = lax.axis_index("ex"), lax.axis_index("dim")
    return ex // 2, ex % 2, dim


def three(x):
    high, low = split(x)
    return jnp.concatenate([high, low, high], axis=1)


def stacked(table):
    high, low = split(table)
    return jnp.concatenate([high, high, low], axis=0)


def factors_body(*refs):
    given, (left, right, val_left, val_right), sems = refs[:5], refs[-5:-1], refs[-1]
    forth, back, turn, unturn, inverse, own = refs[5:11]
    layer = position()[1]
    copies = []
    for k, (g, h) in enumerate(zip(given, [left, right, val_left, val_right, own])):
        copies.append(pltpu.make_async_copy(g.at[layer] if k < 2 else g, h, sems.at[k]))
        copies[-1].start()
    for copy in copies[:4]:
        copy.wait()
    block = lax.broadcasted_iota(jnp.int32, (PAIRS, QUAD * SIDE), 1) // SIDE
    rows = []
    for low in range(2):
        part = left[pl.ds(low, PAIRS, stride=2), :]
        wide = jnp.concatenate([part] * QUAD, axis=1)
        rows += [jnp.where(block == quad, wide, 0.0) for quad in range(QUAD)]
    table = jnp.concatenate(rows, axis=0)
    forth[...] = stacked(table)
    back[...] = stacked(table.T)
    twice = jnp.concatenate([right[...]] * 2, axis=1)
    half = lax.broadcasted_iota(jnp.int32, (SIDE, LANES), 1) // SIDE
    table = jnp.concatenate([jnp.where(half == low, twice, 0.0) for low in range(2)], axis=0)
    turn[...] = jnp.concatenate(split(table), axis=0)
    unturn[...] = stacked(table.T)
    along = jnp.concatenate([val_left[pl.ds(layer, 1), :]] * QUAD, axis=1)
    down = jnp.broadcast_to(val_right[pl.ds(layer, 1), :], (SIDE, SIDE)).T
    inverse[...] = 1.0 / (along * jnp.concatenate([down] * QUAD, axis=1) + damping)
    copies[4].wait()


def factors(queries, left, right, val_left, val_right):
    shapes = [((768, 256), bf16)] * 2 + [((256, 128), bf16), ((384, 128), bf16), ((64, 256), f32), (queries.shape, bf16)]
    given = (left, right, val_left, val_right, queries)
    *tables, own = call(
        factors_body,
        "factors",
        [pltpu.VMEM(shape, kind) for shape, kind in shapes],
        [far(x) for x in given],
        [pltpu.VMEM(x.shape[1:] if x.ndim == 3 else x.shape, f32) for x in given[:4]] + [pltpu.SemaphoreType.DMA((5,))],
        us=1.2,
        specs=[HBM] * 5,
    )
    return tables, own


def precondition_body(parity, first, joined, own, other, *refs):
    forth, back, turn, unturn, inverse = refs[:5]
    outs, buffer = refs[5:-1], refs[-1]
    outs, union = (outs[:-1], outs[-1]) if joined else (outs, None)
    _, core, dim = position()
    count = outs[0].shape[0]
    groups = count // QUAD
    pitch, pitch_back = count + PAD, PAIRS + PAD
    mine = (core + dim) % 2 == parity
    x = []
    for a in range(PAIRS):
        part = pl.ds(pl.multiple_of(core * FLAT + a * LANES, LANES), LANES)
        x.append(jnp.where(mine, own[first : first + count, part], other[first : first + count, part]))
    x = jnp.concatenate(x, axis=0)
    t = mm(jnp.concatenate([x, x], axis=1), turn[...])
    for a in range(PAIRS):
        buffer[a * pitch : a * pitch + count] = t[a * count : (a + 1) * count]
    turned = []
    for group in range(groups):
        t = jnp.concatenate([buffer[pl.ds(QUAD * group + k, PAIRS, stride=pitch), :] for k in range(QUAD)], axis=0).T
        turned.append(jnp.concatenate([t[:SIDE], t[SIDE:]], axis=1))
    t = mm(three(jnp.concatenate(turned, axis=0)), forth[...])
    t = mm(three(t * jnp.concatenate([inverse[...]] * groups, axis=0)), back[...])
    rows = []
    for group in range(groups):
        u = t[SIDE * group : SIDE * (group + 1)]
        rows.append(jnp.concatenate([u[:, :LANES], u[:, LANES:]], axis=0).T)
    t = mm(three(jnp.concatenate(rows, axis=0)), unturn[...])
    for n in range(count):
        buffer[n * pitch_back : n * pitch_back + PAIRS] = t[n * PAIRS : (n + 1) * PAIRS]
    a = 0
    for out in outs:
        for column in range(0, out.shape[1], LANES):
            part = buffer[pl.ds(a, count, stride=pitch_back), :].astype(bf16)
            out[:, column : column + LANES] = part
            if joined:
                union[:, a * LANES : (a + 1) * LANES] = part
            a += 1


def precondition(own, other, tables, parity, first, count, widths, joined=False):
    widths = widths + [FLAT] * joined
    return call(
        functools.partial(precondition_body, parity, first, joined),
        f"precondition_{parity}_{first}",
        [pltpu.VMEM((count, width), bf16) for width in widths],
        [near(x) for x in (own, other, *tables)],
        [pltpu.VMEM((max(PAIRS * (count + PAD), count * (PAIRS + PAD)), LANES), f32)],
        us=1.8 * count / 32,
    )


def dot_cores(core, ours, theirs, store, first):
    value = 0.0
    for layer, x in ((core, ours), (1 - core, theirs)):
        value = value + mm(x, store[pl.ds(pl.multiple_of(layer * FLAT + first, LANES), x.shape[1]), :])
    return value


def store_body(store, turned, out):
    rows, columns = store.shape
    squares = jnp.zeros((8, rows), f32)
    for column in range(0, columns, rows):
        part = store[:, column : column + rows].T
        turned[column : column + rows] = part
        part = part.astype(f32)
        squares += jnp.sum((part * part).reshape(-1, 8, rows), axis=0)
    out[...] = jnp.broadcast_to(jnp.sum(squares, axis=0, keepdims=True), out.shape)


def gathered(core, widths, first, refs, chips, store):
    ours, theirs, pairs = refs[0], refs[1], refs[2:]
    value, away = 0.0, chips - 1
    for index, width in enumerate(widths):
        sides = []
        for k, mine in enumerate((ours, theirs)):
            came = pairs[2 * away * index + away * k : 2 * away * index + away * (k + 1)]
            sides.append(jnp.concatenate([mine[:, first : first + width], *[r[...] for r in came]], axis=0))
        value = value + dot_cores(core, *sides, store, first)
        first += width
    return value


def odd_body(chips, store, sq, *refs):
    pieces, (message, total) = refs[:-2], refs[-2:]
    x, core, _ = position()
    half = len(pieces) // 2
    sides = [jnp.concatenate([r[...] for r in pieces[k * half : (k + 1) * half]], axis=0) for k in range(2)]
    total[...] = dot_cores(core, *sides, store, 0)
    count = total.shape[0] // chips
    for block in range(chips):
        apart = lax.rem(x - block + chips, chips)
        message[block * count : (block + 1) * count] = total[pl.ds(pl.multiple_of(apart * count, count), count), :]
    message[chips * count :] = sq[...]


def even_body(chips, widths, store, *refs):
    _, core, _ = position()
    refs[-1][...] = gathered(core, widths, 0, refs[:-1], chips, store)


def send_body(chips, widths, first, partners, store, sq, got, before, *refs):
    refs, messages, total = refs[: -1 - len(partners)], refs[-1 - len(partners) : -1], refs[-1]
    x, core, dim = position()
    total[...] = before[...] + gathered(core, widths, first, refs, chips, store)
    count = refs[0].shape[0]
    for message, partner in zip(messages, partners):
        block = partner(dim) // 2
        apart = lax.rem(x - block + chips, chips)
        message[:count] = (
            got[pl.ds(pl.multiple_of(block * count, count), count), :]
            + total[pl.ds(pl.multiple_of(apart * count, count), count), :]
        )
        message[count:] = sq[...] + got[chips * count :]


def finish_body(*refs):
    out, here, sem = refs[-3:]
    total = refs[0][...]
    for r in refs[1:-3]:
        total = total + r[...]
    count = out.shape[0]
    here[...] = total[:count] / jnp.sqrt(total[count : count + 1] + 1e-06)
    copy = pltpu.make_async_copy(here, out, sem)
    copy.start()
    copy.wait()


def local(dims, exs, store, queries, eig_left, eig_right, val_left, val_right):
    count, rows = queries.shape[0], store.shape[0]
    chips = exs // 2
    across = [(e, e ^ 1) for e in range(exs)]

    def swap(x):
        return lax.ppermute(x, "ex", across)

    def hop(x, step):
        return lax.ppermute(x, "ex", [(e, (e + 2 * step) % exs) for e in range(exs)])

    other = swap(queries)
    tables, own = factors(queries, eig_left, eig_right, val_left, val_right)
    odd, odd_came, theirs_odd = [], [], []
    for first in range(0, count, ROWS):
        given = after(own, *theirs_odd)
        odd += precondition(given, other, tables, 1, first, ROWS, [FLAT])
        odd_came.append([hop(odd[-1], step) for step in range(1, chips)])
        theirs_odd.append(swap(odd[-1]))
    widths = [FLAT * 5 // 8, FLAT * 3 // 8]
    *even, ours = precondition(after(own, odd[-1]), other, tables, 0, 0, count, widths, True)
    outs = [pltpu.VMEM((store.shape[1], rows), bf16), pltpu.VMEM((8, rows), f32)]
    store, sq = call(store_body, "store", outs, [near(after(store, *even))], us=1.5)
    even_came = [[hop(p, step) for step in range(1, chips)] for p in even]
    theirs = swap(ours)

    odd_came = [[after(x, *even, sq) for x in xs] for xs in odd_came]
    came = [x for step in zip(*odd_came) for x in step]
    ins = [store, sq, *odd, *came, *theirs_odd, *[swap(x) for x in came]]
    body = functools.partial(odd_body, chips)
    out = pltpu.VMEM((chips * count + 8, rows), f32)
    scratch = [pltpu.VMEM((count * chips, rows), f32)]
    message = call(body, "odd", out, [near(x) for x in ins], scratch, us=1.4)
    got = lax.ppermute(message, "dim", [(z, z ^ 1) for z in range(dims)])

    even_came = [[after(x, message) for x in xs] for xs in even_came]
    even_came[1] = [after(x, got) for x in even_came[1]]
    pairs = [[*xs, *[swap(x) for x in xs]] for xs in even_came]
    body = functools.partial(even_body, chips, widths[:1])
    ins = [store, ours, theirs, *pairs[0]]
    total = call(body, "even", pltpu.VMEM((count * chips, rows), f32), [near(x) for x in ins], us=0.9)

    partners = [lambda z, k=k: lax.bitwise_xor(z, k) for k in range(0, dims, 2)]
    ins = [store, sq, got, total, ours, theirs, *pairs[1]]
    body = functools.partial(send_body, chips, widths[1:], widths[0], partners)
    outs = [pltpu.VMEM((count + 8, rows), f32)] * (dims // 2)
    messages = call(body, "send", outs, [near(x) for x in ins], scratch, us=0.6)
    sums = [messages[0]]
    for k in range(2, dims, 2):
        sums.append(lax.ppermute(messages[k // 2], "dim", [(z, z ^ k) for z in range(dims)]))
    turned = call(
        finish_body,
        "finish",
        jax.ShapeDtypeStruct((count, rows), f32),
        [near(x) for x in sums],
        [pltpu.VMEM((count, rows), f32), pltpu.SemaphoreType.DMA],
        us=0.6,
        to=HBM,
    )
    return turned.T


def solution(mesh):
    in_specs = (
        P(("grp", "ex"), "dim"),
        P(("grp", "ex"), "dim"),
        P(("grp", "dim"), None, None),
        P(("grp", "dim"), None, None),
        P(("grp", "dim"), None),
        P(("grp", "dim"), None),
    )
    out_specs = P(("grp", "ex"), "dim")
    body = functools.partial(local, mesh.shape["dim"], mesh.shape["ex"])
    return jax.shard_map(body, mesh=mesh, in_specs=in_specs, out_specs=out_specs, check_vma=False)
```

time: 77.5 us -> 29.3 us (0.38)
  waiting for transfers between devices: 29.9 us -> 6.92 us
  matrix products: 13.6 us -> 0 us
  between operations: 13.5 us -> 0.09 us
  starting transfers between devices: 0.04 us -> 12.8 us
  blocking collectives: 11.7 us -> 0 us
  Pallas kernels: 0 us -> 9.3 us
  other arithmetic: 4.57 us -> 0 us
  local copies, waits for them, and re-layouts: 3.81 us -> 0.01 us
    all_gather x1 -> x0, waiting for transfers between devices: 25.4 us -> none  [local(): lax.all_gather(precond, 'ex', axis=0, tiled=True)]
    dot_general x5 -> x0, matrix products: 13.6 us -> none  [the longest x1 5.02 us: local(): lax.dot_general(store, lax.all_gather(precond, 'ex', axis=0, tiled=True),...]
    ppermute x0 -> x14, starting transfers between devices: none -> 12.8 us  [the longest x4 6.54 us: hop(): lax.ppermute(x, 'ex', [(e, (e + 2 * step) % exs) for e in range(exs)])]
    psum x1 -> x0, blocking collectives: 11.7 us -> none  [local(): total_sq = lax.psum(squares, 'dim')]
    pallas_call x0 -> x9, Pallas kernels: none -> 9.3 us  [call(): pl.pallas_call(body, out_shape=outs, in_specs=specs or [WHOLE] * len(ins)...]
    ppermute x0 -> x14, waiting for transfers between devices: none -> 6.92 us  [the longest x1 2.75 us: local(): lax.ppermute(messages[k // 2], 'dim', [(z, z ^ k) for z in range(dims)])]
    reduce_scatter x1 -> x0, waiting for transfers between devices: 4.5 us -> none  [local(): lax.psum_scatter(partial_value, 'dim', scatter_dimension=1, tiled=True)]
    reduce_sum x1 -> x0, other arithmetic: 3.1 us -> none  [local(): squares = jnp.sum(jnp.square(store.astype(jnp.float32)), axis=1)]
  transfers between devices with their start and end apart: 2 -> 14, of which waited for: 2 -> 6; matrix products, arithmetic and copies ran while one was open for 4% -> 0% of each run, Pallas kernels for 0% -> 24%
where the time goes in v2:
time: 29.3 us; the launch traced here: 29.1 us
  starting transfers between devices  12.8 us (44%)
  Pallas kernels  9.3 us (32%)
  waiting for transfers between devices  6.92 us (24%)
    pallas_call x9, Pallas kernels, call(): pl.pallas_call(body, out_shape=outs, in_specs=specs or [WHOLE] * len(ins)...  9.3 us
    ppermute x4, starting transfers between devices, hop(): lax.ppermute(x, 'ex', [(e, (e + 2 * step) % exs) for e in range(exs)])  6.54 us
    ppermute x1, waiting for transfers between devices, local(): lax.ppermute(messages[k // 2], 'dim', [(z, z ^ k) for z in range(dims)])  2.75 us
    ppermute x1, starting transfers between devices, local(): lax.ppermute(messages[k // 2], 'dim', [(z, z ^ k) for z in range(dims)])  2.66 us
    ppermute x1, waiting for transfers between devices, local(): got = lax.ppermute(message, 'dim', [(z, z ^ 1) for z in range(dims)])  2.2 us
    ppermute x8, starting transfers between devices, swap(): return lax.ppermute(x, 'ex', across)  1.98 us
    ppermute x1, starting transfers between devices, local(): got = lax.ppermute(message, 'dim', [(z, z ^ 1) for z in range(dims)])  1.64 us
    ppermute x8, waiting for transfers between devices, swap(): return lax.ppermute(x, 'ex', across)  1.39 us
  transfers between devices with their start and end apart: 14, of which 6 were waited for; matrix products, arithmetic and copies ran while one was open for 0% of the time, Pallas kernels for 24%

profile of v2, /device:TPU:0, one launch (start us, length us, event | category | flops | bytes accessed | tf_op | source)
XLA Modules:
  0.0 29.1 jit_solution(13289192546474457324)
XLA Ops:
  0.0 0.0 copy-start
  0.0 0.5 %collective-permute-start = (bf16[32,8192]{1,0:T(8,128)(2,1)}, bf16[32,8192]{1,0:T(8,128)(2,1)S(1)}, u32[]{:S(2)}, u32[]{:S(2)}) collective-permute-start(bf16[32,8192]{1,0:T(8,128)(2,1)} %refs_4_.1), channel_id=1, source_target_pairs={{0,1},{1,0},{2,3},{3,2},{4,5},{5,4},{6,7},{7,6},{8,9},{9,8},{10,11... | collective-permute-start | bytes 1572872 | tf_op jit(solution)/shard_map/ppermute | solution.py:252
  0.5 1.4 %factors.1 = (bf16[768,256]{1,0:T(8,128)(2,1)S(1)}, bf16[768,256]{1,0:T(8,128)(2,1)S(1)}, bf16[256,128]{1,0:T(8,128)(2,1)S(1)}, bf16[384,128]{1,0:T(8,128)(2,1)S...) custom-call(f32[2,64,64]{2,1,0:T(8,128)} %refs_0_.1, f32[2,64,64]{2,1,0:T(8,128)} %refs_1_.1, f32[2,64]{1,0:T(2,128)} %refs_2_.1, ...), custom_call_target="tpu_custom_call" | custom-call | flops 27600000 | tf_op jit(solution)/shard_map/factors/pallas_call | solution.py:37
  1.8 0.4 %collective-permute-done.other = bf16[32,8192]{1,0:T(8,128)(2,1)S(1)} collective-permute-done((bf16[32,8192]{1,0:T(8,128)(2,1)}, bf16[32,8192]{1,0:T(8,128)(2,1)S(1)}, u32[]{:S(2)}, u32[]{:S(2)}) %collective-permute-start) | collective-permute-done | bytes 524320 | tf_op jit(solution)/shard_map/ppermute | solution.py:252
  2.2 1.2 %precondition_1_0.1.refs_0_ = bf16[16,4096]{1,0:T(8,128)(2,1)S(1)} custom-call(bf16[32,8192]{1,0:T(8,128)(2,1)S(1)} %get-tuple-element.33.own, bf16[32,8192]{1,0:T(8,128)(2,1)S(1)} %collective-permute-done.other, bf16[768,256]{1,0:T(8,128)(2,1)S(1)} %get-tuple-element.27.refs_0_, bf16[768,256]{1,0:T(8,128)(2,1)S(1)} %get-tuple-element.28.refs_1_, ...), custom_call_target="tpu_custom_call" | custom-call | flops 20700000 | tf_op jit(solution)/shard_map/precondition_1_0/pallas_call | solution.py:37
  3.4 0.4 %collective-permute-start.1 = (bf16[16,4096]{1,0:T(8,128)(2,1)S(1)}, bf16[16,4096]{1,0:T(8,128)(2,1)S(1)}, u32[]{:S(2)}, u32[]{:S(2)}) collective-permute-start(bf16[16,4096]{1,0:T(8,128)(2,1)S(1)} %precondition_1_0.1.refs_0_), channel_id=1, source_target_pairs={{0,1},{1,0},{2,3},{3,2},{4,5},{5,4},{6,7},{7,6},{8,9},{9,8},{10,11... | collective-permute-start | bytes 393224 | tf_op jit(solution)/shard_map/ppermute | solution.py:252
  3.9 2.6 %collective-permute-start.2 = (bf16[16,4096]{1,0:T(8,128)(2,1)S(1)}, bf16[16,4096]{1,0:T(8,128)(2,1)S(1)}, u32[]{:S(2)}, u32[]{:S(2)}) collective-permute-start(bf16[16,4096]{1,0:T(8,128)(2,1)S(1)} %precondition_1_0.1.refs_0_), channel_id=1, source_target_pairs={{0,2},{1,3},{2,0},{3,1},{4,6},{5,7},{6,4},{7,5},{8,10},{9,11},{10,... | collective-permute-start | bytes 393224 | tf_op jit(solution)/shard_map/ppermute | solution.py:255
  6.5 0.0 collective-permute-done.1.refs_4_
  6.5 1.2 %precondition_1_16.1.refs_1_ = bf16[16,4096]{1,0:T(8,128)(2,1)S(1)} custom-call(bf16[32,8192]{1,0:T(8,128)(2,1)S(1)} %get-tuple-element.33.own, bf16[32,8192]{1,0:T(8,128)(2,1)S(1)} %collective-permute-done.other, bf16[768,256]{1,0:T(8,128)(2,1)S(1)} %get-tuple-element.27.refs_0_, bf16[768,256]{1,0:T(8,128)(2,1)S(1)} %get-tuple-element.28.refs_1_, ...), custom_call_target="tpu_custom_call" | custom-call | flops 20700000 | tf_op jit(solution)/shard_map/precondition_1_16/pallas_call | solution.py:37
  7.7 1.3 %collective-permute-start.3 = (bf16[16,4096]{1,0:T(8,128)(2,1)S(1)}, bf16[16,4096]{1,0:T(8,128)(2,1)S(1)}, u32[]{:S(2)}, u32[]{:S(2)}) collective-permute-start(bf16[16,4096]{1,0:T(8,128)(2,1)S(1)} %precondition_1_16.1.refs_1_), channel_id=1, source_target_pairs={{0,2},{1,3},{2,0},{3,1},{4,6},{5,7},{6,4},{7,5},{8,10},{9,11},{10,... | collective-permute-start | bytes 393224 | tf_op jit(solution)/shard_map/ppermute | solution.py:255
  9.0 1.8 %precondition_0_0.1 = (bf16[32,2560]{1,0:T(8,128)(2,1)S(1)}, bf16[32,1536]{1,0:T(8,128)(2,1)S(1)}, bf16[32,4096]{1,0:T(8,128)(2,1)S(1)}) custom-call(bf16[32,8192]{1,0:T(8,128)(2,1)S(1)} %get-tuple-element.33.own, bf16[32,8192]{1,0:T(8,128)(2,1)S(1)} %collective-permute-done.other, bf16[768,256]{1,0:T(8,128)(2,1)S(1)} %get-tuple-element.27.refs_0_, ...), custom_call_target="tpu_custom_call" | custom-call | flops 41400000 | tf_op jit(solution)/shard_map/precondition_0_0/pallas_call | solution.py:37
  10.8 0.9 %collective-permute-start.9 = (bf16[32,2560]{1,0:T(8,128)(2,1)S(1)}, bf16[32,2560]{1,0:T(8,128)(2,1)S(1)}, u32[]{:S(2)}, u32[]{:S(2)}) collective-permute-start(bf16[32,2560]{1,0:T(8,128)(2,1)S(1)} %get-tuple-element.34), channel_id=1, source_target_pairs={{0,2},{1,3},{2,0},{3,1},{4,6},{5,7},{6,4},{7,5},{8,10},{9,11},{10,... | collective-permute-start | bytes 491528 | tf_op jit(solution)/shard_map/ppermute | solution.py:255
  11.7 0.0 copy-done
  11.7 1.2 %store.1 = (bf16[8192,256]{1,0:T(8,128)(2,1)S(1)}, f32[8,256]{1,0:T(8,128)S(1)}) custom-call(bf16[256,8192]{1,0:T(8,128)(2,1)S(1)} %copy-done), custom_call_target="tpu_custom_call" | custom-call | flops 34500000 | tf_op jit(solution)/shard_map/store/pallas_call | solution.py:37
  12.9 0.0 collective-permute-done.2.refs_2_
  12.9 0.1 collective-permute-start.5
  13.0 0.5 %collective-permute-start.4 = (bf16[16,4096]{1,0:T(8,128)(2,1)S(1)}, bf16[16,4096]{1,0:T(8,128)(2,1)S(1)}, u32[]{:S(2)}, u32[]{:S(2)}) collective-permute-start(bf16[16,4096]{1,0:T(8,128)(2,1)S(1)} %precondition_1_16.1.refs_1_), channel_id=1, source_target_pairs={{0,1},{1,0},{2,3},{3,2},{4,5},{5,4},{6,7},{7,6},{8,9},{9,8},{10,11... | collective-permute-start | bytes 393224 | tf_op jit(solution)/shard_map/ppermute | solution.py:252
  13.5 0.0 collective-permute-done.3.refs_3_
  13.5 0.1 collective-permute-start.6
  13.6 0.4 %collective-permute-start.8 = (bf16[32,4096]{1,0:T(8,128)(2,1)S(1)}, bf16[32,4096]{1,0:T(8,128)(2,1)S(1)}, u32[]{:S(2)}, u32[]{:S(2)}) collective-permute-start(bf16[32,4096]{1,0:T(8,128)(2,1)S(1)} %get-tuple-element.41.refs_0_), channel_id=1, source_target_pairs={{0,1},{1,0},{2,3},{3,2},{4,5},{5,4},{6,7},{7,6},{8,9},{9,8},{10,11... | collective-permute-start | bytes 786440 | tf_op jit(solution)/shard_map/ppermute | solution.py:252
  14.0 0.3 %collective-permute-done.5.refs_6_ = bf16[16,4096]{1,0:T(8,128)(2,1)S(1)} collective-permute-done((bf16[16,4096]{1,0:T(8,128)(2,1)S(1)}, bf16[16,4096]{1,0:T(8,128)(2,1)S(1)}, u32[]{:S(2)}, u32[]{:S(2)}) %collective-permute-start.5) | collective-permute-done | bytes 131104 | tf_op jit(solution)/shard_map/ppermute | solution.py:252
  14.3 1.7 %collective-permute-start.11 = (bf16[32,1536]{1,0:T(8,128)(2,1)S(1)}, bf16[32,1536]{1,0:T(8,128)(2,1)S(1)}, u32[]{:S(2)}, u32[]{:S(2)}) collective-permute-start(bf16[32,1536]{1,0:T(8,128)(2,1)S(1)} %get-tuple-element.35), channel_id=1, source_target_pairs={{0,2},{1,3},{2,0},{3,1},{4,6},{5,7},{6,4},{7,5},{8,10},{9,11},{10,... | collective-permute-start | bytes 294920 | tf_op jit(solution)/shard_map/ppermute | solution.py:255
  16.1 0.0 collective-permute-done.4.refs_5_
  16.1 0.0 collective-permute-done.6.refs_7_
  16.1 0.9 %odd.1 = f32[72,256]{1,0:T(8,128)S(1)} custom-call(bf16[8192,256]{1,0:T(8,128)(2,1)S(1)} %get-tuple-element.37.store, f32[8,256]{1,0:T(8,128)S(1)} %get-tuple-element.38.sq, bf16[16,4096]{1,0:T(8,128)(2,1)S(1)} %precondition_1_0.1.refs_0_, bf16[16,4096]{1,0:T(8,128)(2,1)S(1)} %precondition_1_16.1.refs_1_, ...), custom_call_target="tpu_custom_call" | custom-call | flops 32200000 | tf_op jit(solution)/shard_map/odd/pallas_call | solution.py:37
  16.9 1.6 %collective-permute-start.7 = (f32[72,256]{1,0:T(8,128)S(1)}, f32[72,256]{1,0:T(8,128)S(1)}, u32[]{:S(2)}, u32[]{:S(2)}) collective-permute-start(f32[72,256]{1,0:T(8,128)S(1)} %odd.1), channel_id=1, source_target_pairs={{0,4},{4,0},{8,12},{12,8},{1,5},{5,1},{9,13},{13,9},{2,6},{6,2},{1... | collective-permute-start | bytes 221192 | tf_op jit(solution)/shard_map/ppermute | solution.py:279
  18.6 0.0 collective-permute-done.9.refs_2_
  18.6 0.0 collective-permute-start.10
  18.6 0.6 %collective-permute-done.11.refs_2_ = bf16[32,1536]{1,0:T(8,128)(2,1)S(1)} collective-permute-done((bf16[32,1536]{1,0:T(8,128)(2,1)S(1)}, bf16[32,1536]{1,0:T(8,128)(2,1)S(1)}, u32[]{:S(2)}, u32[]{:S(2)}) %collective-permute-start.11) | collective-permute-done | bytes 98336 | tf_op jit(solution)/shard_map/ppermute | solution.py:255
  19.2 2.2 %collective-permute-done.7.got = f32[72,256]{1,0:T(8,128)S(1)} collective-permute-done((f32[72,256]{1,0:T(8,128)S(1)}, f32[72,256]{1,0:T(8,128)S(1)}, u32[]{:S(2)}, u32[]{:S(2)}) %collective-permute-start.7) | collective-permute-done | bytes 73760 | tf_op jit(solution)/shard_map/ppermute | solution.py:279
  21.4 0.0 collective-permute-start.12
  21.4 0.0 collective-permute-done.8.refs_1_
  21.4 0.0 collective-permute-done.10.refs_3_
  21.4 0.6 %even.1.before = f32[64,256]{1,0:T(8,128)S(1)} custom-call(bf16[8192,256]{1,0:T(8,128)(2,1)S(1)} %get-tuple-element.37.store, bf16[32,4096]{1,0:T(8,128)(2,1)S(1)} %get-tuple-element.41.refs_0_, bf16[32,4096]{1,0:T(8,128)(2,1)S(1)} %collective-permute-done.8.refs_1_, bf16[32,2560]{1,0:T(8,128)(2,1)S(1)} %collective-permute-done.9.refs_2_, ...), custom_call_target="tpu_custom_call" | custom-call | flops 20700000 | tf_op jit(solution)/shard_map/even/pallas_call | solution.py:37
  22.0 0.7 %collective-permute-done.12.refs_3_ = bf16[32,1536]{1,0:T(8,128)(2,1)S(1)} collective-permute-done((bf16[32,1536]{1,0:T(8,128)(2,1)S(1)}, bf16[32,1536]{1,0:T(8,128)(2,1)S(1)}, u32[]{:S(2)}, u32[]{:S(2)}) %collective-permute-start.12) | collective-permute-done | bytes 98336 | tf_op jit(solution)/shard_map/ppermute | solution.py:252
  22.7 0.4 %send.1 = (f32[40,256]{1,0:T(8,128)S(1)}, f32[40,256]{1,0:T(8,128)S(1)}) custom-call(bf16[8192,256]{1,0:T(8,128)(2,1)S(1)} %get-tuple-element.37.store, f32[8,256]{1,0:T(8,128)S(1)} %get-tuple-element.38.sq, f32[72,256]{1,0:T(8,128)S(1)} %collective-permute-done.7.got, f32[64,256]{1,0:T(8,128)S(1)} %even.1.before, ...), custom_call_target="tpu_custom_call" | custom-call | flops 13800000 | tf_op jit(solution)/shard_map/send/pallas_call | solution.py:37
  23.1 2.7 %collective-permute-start.13 = (f32[40,256]{1,0:T(8,128)S(1)}, f32[40,256]{1,0:T(8,128)S(1)}, u32[]{:S(2)}, u32[]{:S(2)}) collective-permute-start(f32[40,256]{1,0:T(8,128)S(1)} %get-tuple-element.46), channel_id=1, source_target_pairs={{0,8},{4,12},{8,0},{12,4},{1,9},{5,13},{9,1},{13,5},{2,10},{6,14},... | collective-permute-start | bytes 122888 | tf_op jit(solution)/shard_map/ppermute | solution.py:295
  25.7 2.7 %collective-permute-done.13.refs_1_ = f32[40,256]{1,0:T(8,128)S(1)} collective-permute-done((f32[40,256]{1,0:T(8,128)S(1)}, f32[40,256]{1,0:T(8,128)S(1)}, u32[]{:S(2)}, u32[]{:S(2)}) %collective-permute-start.13) | collective-permute-done | bytes 40992 | tf_op jit(solution)/shard_map/ppermute | solution.py:295
  28.5 0.6 %finish.1 = f32[32,256]{1,0:T(8,128)} custom-call(f32[40,256]{1,0:T(8,128)S(1)} %get-tuple-element.45.refs_0_, f32[40,256]{1,0:T(8,128)S(1)} %collective-permute-done.13.refs_1_), custom_call_target="tpu_custom_call" | custom-call | flops 13800000 | tf_op jit(solution)/shard_map/finish/pallas_call | solution.py:37
Async XLA Ops:
  0.0 11.7 %copy-start = (bf16[256,8192]{1,0:T(8,128)(2,1)S(1)}, bf16[256,8192]{1,0:T(8,128)(2,1)}, u32[]{:S(2)}) copy-start(bf16[256,8192]{1,0:T(8,128)(2,1)} %store.2) | copy-start | bytes 12582916
  0.0 2.2 %collective-permute-start = (bf16[32,8192]{1,0:T(8,128)(2,1)}, bf16[32,8192]{1,0:T(8,128)(2,1)S(1)}, u32[]{:S(2)}, u32[]{:S(2)}) collective-permute-start(bf16[32,8192]{1,0:T(8,128)(2,1)} %refs_4_.1), channel_id=1, source_target_pairs={{0,1},{1,0},{2,3},{3,2},{4,5},{5,4},{6,7},{7,6},{8,9},{9,8},{10,11... | collective-permute-start | bytes 1572872 | tf_op jit(solution)/shard_map/ppermute | solution.py:252
  3.4 3.1 %collective-permute-start.1 = (bf16[16,4096]{1,0:T(8,128)(2,1)S(1)}, bf16[16,4096]{1,0:T(8,128)(2,1)S(1)}, u32[]{:S(2)}, u32[]{:S(2)}) collective-permute-start(bf16[16,4096]{1,0:T(8,128)(2,1)S(1)} %precondition_1_0.1.refs_0_), channel_id=1, source_target_pairs={{0,1},{1,0},{2,3},{3,2},{4,5},{5,4},{6,7},{7,6},{8,9},{9,8},{10,11... | collective-permute-start | bytes 393224 | tf_op jit(solution)/shard_map/ppermute | solution.py:252
  3.9 9.0 %collective-permute-start.2 = (bf16[16,4096]{1,0:T(8,128)(2,1)S(1)}, bf16[16,4096]{1,0:T(8,128)(2,1)S(1)}, u32[]{:S(2)}, u32[]{:S(2)}) collective-permute-start(bf16[16,4096]{1,0:T(8,128)(2,1)S(1)} %precondition_1_0.1.refs_0_), channel_id=1, source_target_pairs={{0,2},{1,3},{2,0},{3,1},{4,6},{5,7},{6,4},{7,5},{8,10},{9,11},{10,... | collective-permute-start | bytes 393224 | tf_op jit(solution)/shard_map/ppermute | solution.py:255
  7.7 5.7 %collective-permute-start.3 = (bf16[16,4096]{1,0:T(8,128)(2,1)S(1)}, bf16[16,4096]{1,0:T(8,128)(2,1)S(1)}, u32[]{:S(2)}, u32[]{:S(2)}) collective-permute-start(bf16[16,4096]{1,0:T(8,128)(2,1)S(1)} %precondition_1_16.1.refs_1_), channel_id=1, source_target_pairs={{0,2},{1,3},{2,0},{3,1},{4,6},{5,7},{6,4},{7,5},{8,10},{9,11},{10,... | collective-permute-start | bytes 393224 | tf_op jit(solution)/shard_map/ppermute | solution.py:255
  10.8 7.8 %collective-permute-start.9 = (bf16[32,2560]{1,0:T(8,128)(2,1)S(1)}, bf16[32,2560]{1,0:T(8,128)(2,1)S(1)}, u32[]{:S(2)}, u32[]{:S(2)}) collective-permute-start(bf16[32,2560]{1,0:T(8,128)(2,1)S(1)} %get-tuple-element.34), channel_id=1, source_target_pairs={{0,2},{1,3},{2,0},{3,1},{4,6},{5,7},{6,4},{7,5},{8,10},{9,11},{10,... | collective-permute-start | bytes 491528 | tf_op jit(solution)/shard_map/ppermute | solution.py:255
  12.9 1.4 %collective-permute-start.5 = (bf16[16,4096]{1,0:T(8,128)(2,1)S(1)}, bf16[16,4096]{1,0:T(8,128)(2,1)S(1)}, u32[]{:S(2)}, u32[]{:S(2)}) collective-permute-start(bf16[16,4096]{1,0:T(8,128)(2,1)S(1)} %collective-permute-done.2.refs_2_), channel_id=1, source_target_pairs={{0,1},{1,0},{2,3},{3,2},{4,5},{5,4},{6,7},{7,6},{8,9},{9,8},{10,11... | collective-permute-start | bytes 393224 | tf_op jit(solution)/shard_map/ppermute | solution.py:252
  13.0 3.1 %collective-permute-start.4 = (bf16[16,4096]{1,0:T(8,128)(2,1)S(1)}, bf16[16,4096]{1,0:T(8,128)(2,1)S(1)}, u32[]{:S(2)}, u32[]{:S(2)}) collective-permute-start(bf16[16,4096]{1,0:T(8,128)(2,1)S(1)} %precondition_1_16.1.refs_1_), channel_id=1, source_target_pairs={{0,1},{1,0},{2,3},{3,2},{4,5},{5,4},{6,7},{7,6},{8,9},{9,8},{10,11... | collective-permute-start | bytes 393224 | tf_op jit(solution)/shard_map/ppermute | solution.py:252
  13.5 2.6 %collective-permute-start.6 = (bf16[16,4096]{1,0:T(8,128)(2,1)S(1)}, bf16[16,4096]{1,0:T(8,128)(2,1)S(1)}, u32[]{:S(2)}, u32[]{:S(2)}) collective-permute-start(bf16[16,4096]{1,0:T(8,128)(2,1)S(1)} %collective-permute-done.3.refs_3_), channel_id=1, source_target_pairs={{0,1},{1,0},{2,3},{3,2},{4,5},{5,4},{6,7},{7,6},{8,9},{9,8},{10,11... | collective-permute-start | bytes 393224 | tf_op jit(solution)/shard_map/ppermute | solution.py:252
  13.6 7.8 %collective-permute-start.8 = (bf16[32,4096]{1,0:T(8,128)(2,1)S(1)}, bf16[32,4096]{1,0:T(8,128)(2,1)S(1)}, u32[]{:S(2)}, u32[]{:S(2)}) collective-permute-start(bf16[32,4096]{1,0:T(8,128)(2,1)S(1)} %get-tuple-element.41.refs_0_), channel_id=1, source_target_pairs={{0,1},{1,0},{2,3},{3,2},{4,5},{5,4},{6,7},{7,6},{8,9},{9,8},{10,11... | collective-permute-start | bytes 786440 | tf_op jit(solution)/shard_map/ppermute | solution.py:252
  14.3 4.8 %collective-permute-start.11 = (bf16[32,1536]{1,0:T(8,128)(2,1)S(1)}, bf16[32,1536]{1,0:T(8,128)(2,1)S(1)}, u32[]{:S(2)}, u32[]{:S(2)}) collective-permute-start(bf16[32,1536]{1,0:T(8,128)(2,1)S(1)} %get-tuple-element.35), channel_id=1, source_target_pairs={{0,2},{1,3},{2,0},{3,1},{4,6},{5,7},{6,4},{7,5},{8,10},{9,11},{10,... | collective-permute-start | bytes 294920 | tf_op jit(solution)/shard_map/ppermute | solution.py:255
  16.9 4.4 %collective-permute-start.7 = (f32[72,256]{1,0:T(8,128)S(1)}, f32[72,256]{1,0:T(8,128)S(1)}, u32[]{:S(2)}, u32[]{:S(2)}) collective-permute-start(f32[72,256]{1,0:T(8,128)S(1)} %odd.1), channel_id=1, source_target_pairs={{0,4},{4,0},{8,12},{12,8},{1,5},{5,1},{9,13},{13,9},{2,6},{6,2},{1... | collective-permute-start | bytes 221192 | tf_op jit(solution)/shard_map/ppermute | solution.py:279
  18.6 2.8 %collective-permute-start.10 = (bf16[32,2560]{1,0:T(8,128)(2,1)S(1)}, bf16[32,2560]{1,0:T(8,128)(2,1)S(1)}, u32[]{:S(2)}, u32[]{:S(2)}) collective-permute-start(bf16[32,2560]{1,0:T(8,128)(2,1)S(1)} %collective-permute-done.9.refs_2_), channel_id=1, source_target_pairs={{0,1},{1,0},{2,3},{3,2},{4,5},{5,4},{6,7},{7,6},{8,9},{9,8},{10,11... | collective-permute-start | bytes 491528 | tf_op jit(solution)/shard_map/ppermute | solution.py:252
  21.4 1.3 %collective-permute-start.12 = (bf16[32,1536]{1,0:T(8,128)(2,1)S(1)}, bf16[32,1536]{1,0:T(8,128)(2,1)S(1)}, u32[]{:S(2)}, u32[]{:S(2)}) collective-permute-start(bf16[32,1536]{1,0:T(8,128)(2,1)S(1)} %collective-permute-done.11.refs_2_), channel_id=1, source_target_pairs={{0,1},{1,0},{2,3},{3,2},{4,5},{5,4},{6,7},{7,6},{8,9},{9,8},{10,11... | collective-permute-start | bytes 294920 | tf_op jit(solution)/shard_map/ppermute | solution.py:252
  23.1 5.4 %collective-permute-start.13 = (f32[40,256]{1,0:T(8,128)S(1)}, f32[40,256]{1,0:T(8,128)S(1)}, u32[]{:S(2)}, u32[]{:S(2)}) collective-permute-start(f32[40,256]{1,0:T(8,128)S(1)} %get-tuple-element.46), channel_id=1, source_target_pairs={{0,8},{4,12},{8,0},{12,4},{1,9},{5,13},{9,1},{13,5},{2,10},{6,14},... | collective-permute-start | bytes 122888 | tf_op jit(solution)/shard_map/ppermute | solution.py:295

commit v3 on v2

--- a/solution.py
+++ b/solution.py
@@ -167,11 +167,9 @@
     )
 
 
-def dot_cores(core, ours, theirs, store, first):
-    value = 0.0
-    for layer, x in ((core, ours), (1 - core, theirs)):
-        value = value + mm(x, store[pl.ds(pl.multiple_of(layer * FLAT + first, LANES), x.shape[1]), :])
-    return value
+def scores(layer, pieces, store, first=0):
+    x = jnp.concatenate(pieces, axis=0)
+    return mm(x, store[pl.ds(pl.multiple_of(layer * FLAT + first, LANES), x.shape[1]), :])
 
 
 def store_body(store, turned, out):
@@ -185,25 +183,14 @@
     out[...] = jnp.broadcast_to(jnp.sum(squares, axis=0, keepdims=True), out.shape)
 
 
-def gathered(core, widths, first, refs, chips, store):
-    ours, theirs, pairs = refs[0], refs[1], refs[2:]
-    value, away = 0.0, chips - 1
-    for index, width in enumerate(widths):
-        sides = []
-        for k, mine in enumerate((ours, theirs)):
-            came = pairs[2 * away * index + away * k : 2 * away * index + away * (k + 1)]
-            sides.append(jnp.concatenate([mine[:, first : first + width], *[r[...] for r in came]], axis=0))
-        value = value + dot_cores(core, *sides, store, first)
-        first += width
-    return value
-
-
-def odd_body(chips, store, sq, *refs):
+def ours_body(store, *refs):
+    refs[-1][...] = scores(position()[1], [r[...] for r in refs[:-1]], store)
+
+
+def odd_body(chips, store, sq, before, *refs):
     pieces, (message, total) = refs[:-2], refs[-2:]
     x, core, _ = position()
-    half = len(pieces) // 2
-    sides = [jnp.concatenate([r[...] for r in pieces[k * half : (k + 1) * half]], axis=0) for k in range(2)]
-    total[...] = dot_cores(core, *sides, store, 0)
+    total[...] = before[...] + scores(1 - core, [r[...] for r in pieces], store)
     count = total.shape[0] // chips
     for block in range(chips):
         apart = lax.rem(x - block + chips, chips)
@@ -211,16 +198,30 @@
     message[chips * count :] = sq[...]
 
 
-def even_body(chips, widths, store, *refs):
-    _, core, _ = position()
-    refs[-1][...] = gathered(core, widths, 0, refs[:-1], chips, store)
-
-
-def send_body(chips, widths, first, partners, store, sq, got, before, *refs):
-    refs, messages, total = refs[: -1 - len(partners)], refs[-1 - len(partners) : -1], refs[-1]
+def cut_body(x, *outs):
+    first = 0
+    for out in outs:
+        out[...] = x[:, first : first + out.shape[1]]
+        first += out.shape[1]
+
+
+def cut(x, widths):
+    outs = [pltpu.VMEM((x.shape[0], width), x.dtype) for width in widths]
+    return call(cut_body, "cut", outs, [near(x)], us=0.2)
+
+
+def even_body(store, before, theirs, *refs):
+    came, out = refs[:-1], refs[-1]
+    pieces = [theirs[:, : came[0].shape[1]], *[r[...] for r in came]]
+    out[...] = before[...] + scores(1 - position()[1], pieces, store)
+
+
+def send_body(chips, first, partners, store, sq, got, before, theirs, *refs):
+    came, messages, total = refs[: chips - 1], refs[chips - 1 : -1], refs[-1]
     x, core, dim = position()
-    total[...] = before[...] + gathered(core, widths, first, refs, chips, store)
-    count = refs[0].shape[0]
+    pieces = [theirs[:, first:], *[r[...] for r in came]]
+    total[...] = before[...] + scores(1 - core, pieces, store, first)
+    count = theirs.shape[0]
     for message, partner in zip(messages, partners):
         block = partner(dim) // 2
         apart = lax.rem(x - block + chips, chips)
@@ -263,31 +264,31 @@
         odd_came.append([hop(odd[-1], step) for step in range(1, chips)])
         theirs_odd.append(swap(odd[-1]))
     widths = [FLAT * 5 // 8, FLAT * 3 // 8]
-    *even, ours = precondition(after(own, odd[-1]), other, tables, 0, 0, count, widths, True)
+    even = precondition(after(own, odd[-1]), other, tables, 0, 0, count, [FLAT])
+    ours = even[0]
     outs = [pltpu.VMEM((store.shape[1], rows), bf16), pltpu.VMEM((8, rows), f32)]
     store, sq = call(store_body, "store", outs, [near(after(store, *even))], us=1.5)
-    even_came = [[hop(p, step) for step in range(1, chips)] for p in even]
+    even_came = [hop(ours, step) for step in range(1, chips)]
     theirs = swap(ours)
 
     odd_came = [[after(x, *even, sq) for x in xs] for xs in odd_came]
     came = [x for step in zip(*odd_came) for x in step]
-    ins = [store, sq, *odd, *came, *theirs_odd, *[swap(x) for x in came]]
-    body = functools.partial(odd_body, chips)
+    scratch = [pltpu.VMEM((count * chips, rows), f32)]
+    part = call(ours_body, "odd_ours", scratch[0], [near(x) for x in (store, *odd, *came)], us=0.5)
+    ins = [store, sq, part, *theirs_odd, *[swap(x) for x in came]]
     out = pltpu.VMEM((chips * count + 8, rows), f32)
-    scratch = [pltpu.VMEM((count * chips, rows), f32)]
-    message = call(body, "odd", out, [near(x) for x in ins], scratch, us=1.4)
+    message = call(functools.partial(odd_body, chips), "odd", out, [near(x) for x in ins], scratch, us=0.5)
     got = lax.ppermute(message, "dim", [(z, z ^ 1) for z in range(dims)])
 
-    even_came = [[after(x, message) for x in xs] for xs in even_came]
-    even_came[1] = [after(x, got) for x in even_came[1]]
-    pairs = [[*xs, *[swap(x) for x in xs]] for xs in even_came]
-    body = functools.partial(even_body, chips, widths[:1])
-    ins = [store, ours, theirs, *pairs[0]]
-    total = call(body, "even", pltpu.VMEM((count * chips, rows), f32), [near(x) for x in ins], us=0.9)
+    even_came = [after(x, message) for x in even_came]
+    part = call(ours_body, "even_ours", scratch[0], [near(x) for x in (store, ours, *even_came)], us=0.5)
+    begun, last = zip(*[cut(x, widths) for x in even_came])
+    ins = [store, part, theirs, *[swap(x) for x in begun]]
+    part = call(even_body, "even", scratch[0], [near(x) for x in ins], us=0.3)
 
     partners = [lambda z, k=k: lax.bitwise_xor(z, k) for k in range(0, dims, 2)]
-    ins = [store, sq, got, total, ours, theirs, *pairs[1]]
-    body = functools.partial(send_body, chips, widths[1:], widths[0], partners)
+    ins = [store, sq, got, part, theirs, *[swap(after(x, got)) for x in last]]
+    body = functools.partial(send_body, chips, widths[0], partners)
     outs = [pltpu.VMEM((count + 8, rows), f32)] * (dims // 2)
     messages = call(body, "send", outs, [near(x) for x in ins], scratch, us=0.6)
     sums = [messages[0]]

time: 29.3 us -> 27.3 us (0.932)
  waiting for transfers between devices: 6.92 us -> 5.72 us
  starting transfers between devices: 12.8 us -> 11.7 us
    ppermute x4 -> x3, starting transfers between devices: 6.54 us -> 4.79 us  [hop(): lax.ppermute(x, 'ex', [(e, (e + 2 * step) % exs) for e in range(exs)])]
    ppermute x1, waiting for transfers between devices: 2.2 us -> 0.85 us  [local(): got = lax.ppermute(message, 'dim', [(z, z ^ 1) for z in range(dims)])]
    ppermute x4 -> x3, waiting for transfers between devices: 0.58 us -> 1.64 us  [hop(): lax.ppermute(x, 'ex', [(e, (e + 2 * step) % exs) for e in range(exs)])]
    ppermute x1, waiting for transfers between devices: 2.75 us -> 2.12 us  [local(): lax.ppermute(messages[k // 2], 'dim', [(z, z ^ k) for z in range(dims)])]
    ppermute x1, starting transfers between devices: 1.64 us -> 2 us  [local(): got = lax.ppermute(message, 'dim', [(z, z ^ 1) for z in range(dims)])]
    pallas_call x9 -> x12, Pallas kernels: 9.3 us -> 9.57 us  [call(): pl.pallas_call(body, out_shape=outs, in_specs=specs or [WHOLE] * len(ins)...]
  transfers between devices with their start and end apart: 14 -> 13, of which waited for: 6 -> 6; matrix products, arithmetic and copies ran while one was open for 0% -> 0% of each run, Pallas kernels for 24% -> 27%
where the time goes in v3:
time: 27.3 us; the launch traced here: 27.1 us
  starting transfers between devices  11.7 us (43%)
  Pallas kernels  9.57 us (35%)
  waiting for transfers between devices  5.72 us (21%)
    pallas_call x12, Pallas kernels, call(): pl.pallas_call(body, out_shape=outs, in_specs=specs or [WHOLE] * len(ins)...  9.57 us
    ppermute x3, starting transfers between devices, hop(): lax.ppermute(x, 'ex', [(e, (e + 2 * step) % exs) for e in range(exs)])  4.79 us
    ppermute x1, starting transfers between devices, local(): lax.ppermute(messages[k // 2], 'dim', [(z, z ^ k) for z in range(dims)])  2.86 us
    ppermute x1, waiting for transfers between devices, local(): lax.ppermute(messages[k // 2], 'dim', [(z, z ^ k) for z in range(dims)])  2.12 us
    ppermute x8, starting transfers between devices, swap(): return lax.ppermute(x, 'ex', across)  2.05 us
    ppermute x1, starting transfers between devices, local(): got = lax.ppermute(message, 'dim', [(z, z ^ 1) for z in range(dims)])  2 us
    ppermute x3, waiting for transfers between devices, hop(): lax.ppermute(x, 'ex', [(e, (e + 2 * step) % exs) for e in range(exs)])  1.64 us
    ppermute x8, waiting for transfers between devices, swap(): return lax.ppermute(x, 'ex', across)  1.11 us
  transfers between devices with their start and end apart: 13, of which 6 were waited for; matrix products, arithmetic and copies ran while one was open for 0% of the time, Pallas kernels for 27%

profile of v3, /device:TPU:0, one launch (start us, length us, event | category | flops | bytes accessed | tf_op | source)
XLA Modules:
  0.0 27.1 jit_solution(5150953173331230845)
XLA Ops:
  0.0 0.0 copy-start
  0.0 0.5 %collective-permute-start = (bf16[32,8192]{1,0:T(8,128)(2,1)}, bf16[32,8192]{1,0:T(8,128)(2,1)S(1)}, u32[]{:S(2)}, u32[]{:S(2)}) collective-permute-start(bf16[32,8192]{1,0:T(8,128)(2,1)} %refs_4_.1), channel_id=1, source_target_pairs={{0,1},{1,0},{2,3},{3,2},{4,5},{5,4},{6,7},{7,6},{8,9},{9,8},{10,11... | collective-permute-start | bytes 1572872 | tf_op jit(solution)/shard_map/ppermute | solution.py:253
  0.5 1.4 %factors.1 = (bf16[768,256]{1,0:T(8,128)(2,1)S(1)}, bf16[768,256]{1,0:T(8,128)(2,1)S(1)}, bf16[256,128]{1,0:T(8,128)(2,1)S(1)}, bf16[384,128]{1,0:T(8,128)(2,1)S...) custom-call(f32[2,64,64]{2,1,0:T(8,128)} %refs_0_.1, f32[2,64,64]{2,1,0:T(8,128)} %refs_1_.1, f32[2,64]{1,0:T(2,128)} %refs_2_.1, ...), custom_call_target="tpu_custom_call" | custom-call | flops 27600000 | tf_op jit(solution)/shard_map/factors/pallas_call | solution.py:37
  1.8 0.4 %collective-permute-done.other = bf16[32,8192]{1,0:T(8,128)(2,1)S(1)} collective-permute-done((bf16[32,8192]{1,0:T(8,128)(2,1)}, bf16[32,8192]{1,0:T(8,128)(2,1)S(1)}, u32[]{:S(2)}, u32[]{:S(2)}) %collective-permute-start) | collective-permute-done | bytes 524320 | tf_op jit(solution)/shard_map/ppermute | solution.py:253
  2.2 1.2 %precondition_1_0.1.refs_0_ = bf16[16,4096]{1,0:T(8,128)(2,1)S(1)} custom-call(bf16[32,8192]{1,0:T(8,128)(2,1)S(1)} %get-tuple-element.31.own, bf16[32,8192]{1,0:T(8,128)(2,1)S(1)} %collective-permute-done.other, bf16[768,256]{1,0:T(8,128)(2,1)S(1)} %get-tuple-element.25.refs_0_, bf16[768,256]{1,0:T(8,128)(2,1)S(1)} %get-tuple-element.26.refs_1_, ...), custom_call_target="tpu_custom_call" | custom-call | flops 20700000 | tf_op jit(solution)/shard_map/precondition_1_0/pallas_call | solution.py:37
  3.4 0.4 %collective-permute-start.1 = (bf16[16,4096]{1,0:T(8,128)(2,1)S(1)}, bf16[16,4096]{1,0:T(8,128)(2,1)S(1)}, u32[]{:S(2)}, u32[]{:S(2)}) collective-permute-start(bf16[16,4096]{1,0:T(8,128)(2,1)S(1)} %precondition_1_0.1.refs_0_), channel_id=1, source_target_pairs={{0,1},{1,0},{2,3},{3,2},{4,5},{5,4},{6,7},{7,6},{8,9},{9,8},{10,11... | collective-permute-start | bytes 393224 | tf_op jit(solution)/shard_map/ppermute | solution.py:253
  3.9 2.6 %collective-permute-start.2 = (bf16[16,4096]{1,0:T(8,128)(2,1)S(1)}, bf16[16,4096]{1,0:T(8,128)(2,1)S(1)}, u32[]{:S(2)}, u32[]{:S(2)}) collective-permute-start(bf16[16,4096]{1,0:T(8,128)(2,1)S(1)} %precondition_1_0.1.refs_0_), channel_id=1, source_target_pairs={{0,2},{1,3},{2,0},{3,1},{4,6},{5,7},{6,4},{7,5},{8,10},{9,11},{10,... | collective-permute-start | bytes 393224 | tf_op jit(solution)/shard_map/ppermute | solution.py:256
  6.5 0.0 collective-permute-done.1.refs_0_
  6.5 1.2 %precondition_1_16.1.refs_1_ = bf16[16,4096]{1,0:T(8,128)(2,1)S(1)} custom-call(bf16[32,8192]{1,0:T(8,128)(2,1)S(1)} %get-tuple-element.31.own, bf16[32,8192]{1,0:T(8,128)(2,1)S(1)} %collective-permute-done.other, bf16[768,256]{1,0:T(8,128)(2,1)S(1)} %get-tuple-element.25.refs_0_, bf16[768,256]{1,0:T(8,128)(2,1)S(1)} %get-tuple-element.26.refs_1_, ...), custom_call_target="tpu_custom_call" | custom-call | flops 20700000 | tf_op jit(solution)/shard_map/precondition_1_16/pallas_call | solution.py:37
  7.7 1.3 %collective-permute-start.3 = (bf16[16,4096]{1,0:T(8,128)(2,1)S(1)}, bf16[16,4096]{1,0:T(8,128)(2,1)S(1)}, u32[]{:S(2)}, u32[]{:S(2)}) collective-permute-start(bf16[16,4096]{1,0:T(8,128)(2,1)S(1)} %precondition_1_16.1.refs_1_), channel_id=1, source_target_pairs={{0,2},{1,3},{2,0},{3,1},{4,6},{5,7},{6,4},{7,5},{8,10},{9,11},{10,... | collective-permute-start | bytes 393224 | tf_op jit(solution)/shard_map/ppermute | solution.py:256
  9.0 1.7 %precondition_0_0.1.refs_0_ = bf16[32,4096]{1,0:T(8,128)(2,1)S(1)} custom-call(bf16[32,8192]{1,0:T(8,128)(2,1)S(1)} %get-tuple-element.31.own, bf16[32,8192]{1,0:T(8,128)(2,1)S(1)} %collective-permute-done.other, bf16[768,256]{1,0:T(8,128)(2,1)S(1)} %get-tuple-element.25.refs_0_, bf16[768,256]{1,0:T(8,128)(2,1)S(1)} %get-tuple-element.26.refs_1_, ...), custom_call_target="tpu_custom_call" | custom-call | flops 41400000 | tf_op jit(solution)/shard_map/precondition_0_0/pallas_call | solution.py:37
  10.8 0.9 %collective-permute-start.8 = (bf16[32,4096]{1,0:T(8,128)(2,1)S(1)}, bf16[32,4096]{1,0:T(8,128)(2,1)S(1)}, u32[]{:S(2)}, u32[]{:S(2)}) collective-permute-start(bf16[32,4096]{1,0:T(8,128)(2,1)S(1)} %precondition_0_0.1.refs_0_), channel_id=1, source_target_pairs={{0,2},{1,3},{2,0},{3,1},{4,6},{5,7},{6,4},{7,5},{8,10},{9,11},{10,... | collective-permute-start | bytes 786440 | tf_op jit(solution)/shard_map/ppermute | solution.py:256
  11.7 0.0 collective-permute-start.4
  11.7 0.0 copy-done
  11.7 1.2 %store.1 = (bf16[8192,256]{1,0:T(8,128)(2,1)S(1)}, f32[8,256]{1,0:T(8,128)S(1)}) custom-call(bf16[256,8192]{1,0:T(8,128)(2,1)S(1)} %copy-done), custom_call_target="tpu_custom_call" | custom-call | flops 34500000 | tf_op jit(solution)/shard_map/store/pallas_call | solution.py:37
  12.9 0.0 collective-permute-done.2.refs_2_
  12.9 0.6 %collective-permute-start.5 = (bf16[16,4096]{1,0:T(8,128)(2,1)S(1)}, bf16[16,4096]{1,0:T(8,128)(2,1)S(1)}, u32[]{:S(2)}, u32[]{:S(2)}) collective-permute-start(bf16[16,4096]{1,0:T(8,128)(2,1)S(1)} %collective-permute-done.2.refs_2_), channel_id=1, source_target_pairs={{0,1},{1,0},{2,3},{3,2},{4,5},{5,4},{6,7},{7,6},{8,9},{9,8},{10,11... | collective-permute-start | bytes 393224 | tf_op jit(solution)/shard_map/ppermute | solution.py:253
  13.5 0.0 collective-permute-done.3.refs_3_
  13.5 0.1 collective-permute-start.6
  13.5 0.4 %collective-permute-start.9 = (bf16[32,4096]{1,0:T(8,128)(2,1)S(1)}, bf16[32,4096]{1,0:T(8,128)(2,1)S(1)}, u32[]{:S(2)}, u32[]{:S(2)}) collective-permute-start(bf16[32,4096]{1,0:T(8,128)(2,1)S(1)} %precondition_0_0.1.refs_0_), channel_id=1, source_target_pairs={{0,1},{1,0},{2,3},{3,2},{4,5},{5,4},{6,7},{7,6},{8,9},{9,8},{10,11... | collective-permute-start | bytes 786440 | tf_op jit(solution)/shard_map/ppermute | solution.py:253
  14.0 0.5 %odd_ours.1.before = f32[64,256]{1,0:T(8,128)S(1)} custom-call(bf16[8192,256]{1,0:T(8,128)(2,1)S(1)} %get-tuple-element.33.store, bf16[16,4096]{1,0:T(8,128)(2,1)S(1)} %precondition_1_0.1.refs_0_, bf16[16,4096]{1,0:T(8,128)(2,1)S(1)} %precondition_1_16.1.refs_1_, bf16[16,4096]{1,0:T(8,128)(2,1)S(1)} %collective-permute-done.2.refs_2_, ...), custom_call_target="tpu_custom_call" | custom-call | flops 11500000 | tf_op jit(solution)/shard_map/odd_ours/pallas_call | solution.py:37
  14.5 0.0 collective-permute-done.4.refs_1_
  14.5 0.0 collective-permute-done.5.refs_2_
  14.5 0.3 %collective-permute-done.6.refs_3_ = bf16[16,4096]{1,0:T(8,128)(2,1)S(1)} collective-permute-done((bf16[16,4096]{1,0:T(8,128)(2,1)S(1)}, bf16[16,4096]{1,0:T(8,128)(2,1)S(1)}, u32[]{:S(2)}, u32[]{:S(2)}) %collective-permute-start.6) | collective-permute-done | bytes 131104 | tf_op jit(solution)/shard_map/ppermute | solution.py:253
  14.8 0.5 %odd.1 = f32[72,256]{1,0:T(8,128)S(1)} custom-call(bf16[8192,256]{1,0:T(8,128)(2,1)S(1)} %get-tuple-element.33.store, f32[8,256]{1,0:T(8,128)S(1)} %get-tuple-element.34.sq, f32[64,256]{1,0:T(8,128)S(1)} %odd_ours.1.before, bf16[16,4096]{1,0:T(8,128)(2,1)S(1)} %collective-permute-done.1.refs_0_, bf16[16,4096]{1,0:T(8,128)(2,1)S(1)} %collective-permute-done.4.refs_1_, ...), custom_call_target="tpu_custom_call" | custom-call | flops 11500000 | tf_op jit(solution)/shard_map/odd/pallas_call | solution.py:37
  15.3 2.0 %collective-permute-start.7 = (f32[72,256]{1,0:T(8,128)S(1)}, f32[72,256]{1,0:T(8,128)S(1)}, u32[]{:S(2)}, u32[]{:S(2)}) collective-permute-start(f32[72,256]{1,0:T(8,128)S(1)} %odd.1), channel_id=1, source_target_pairs={{0,4},{4,0},{8,12},{12,8},{1,5},{5,1},{9,13},{13,9},{2,6},{6,2},{1... | collective-permute-start | bytes 221192 | tf_op jit(solution)/shard_map/ppermute | solution.py:281
  17.3 1.6 %collective-permute-done.8.refs_1_.x = bf16[32,4096]{1,0:T(8,128)(2,1)S(1)} collective-permute-done((bf16[32,4096]{1,0:T(8,128)(2,1)S(1)}, bf16[32,4096]{1,0:T(8,128)(2,1)S(1)}, u32[]{:S(2)}, u32[]{:S(2)}) %collective-permute-start.8) | collective-permute-done | bytes 262176 | tf_op jit(solution)/shard_map/ppermute | solution.py:256
  19.0 0.1 collective-permute-start.10
  19.1 0.8 %collective-permute-done.7.got = f32[72,256]{1,0:T(8,128)S(1)} collective-permute-done((f32[72,256]{1,0:T(8,128)S(1)}, f32[72,256]{1,0:T(8,128)S(1)}, u32[]{:S(2)}, u32[]{:S(2)}) %collective-permute-start.7) | collective-permute-done | bytes 73760 | tf_op jit(solution)/shard_map/ppermute | solution.py:281
  19.9 0.0 collective-permute-start.11
  19.9 0.5 %even_ours.1.before = f32[64,256]{1,0:T(8,128)S(1)} custom-call(bf16[8192,256]{1,0:T(8,128)(2,1)S(1)} %get-tuple-element.33.store, bf16[32,4096]{1,0:T(8,128)(2,1)S(1)} %precondition_0_0.1.refs_0_, bf16[32,4096]{1,0:T(8,128)(2,1)S(1)} %collective-permute-done.8.refs_1_.x), custom_call_target="tpu_custom_call" | custom-call | flops 11500000 | tf_op jit(solution)/shard_map/even_ours/pallas_call | solution.py:37
  20.4 0.0 collective-permute-done.9.theirs
  20.4 0.0 collective-permute-done.10.refs_0_
  20.4 0.4 %even.1.before = f32[64,256]{1,0:T(8,128)S(1)} custom-call(bf16[8192,256]{1,0:T(8,128)(2,1)S(1)} %get-tuple-element.33.store, f32[64,256]{1,0:T(8,128)S(1)} %even_ours.1.before, bf16[32,4096]{1,0:T(8,128)(2,1)S(1)} %collective-permute-done.9.theirs, bf16[32,2560]{1,0:T(8,128)(2,1)S(1)} %collective-permute-done.10.refs_0_), custom_call_target="tpu_custom_call" | custom-call | flops 6900000 | tf_op jit(solution)/shard_map/even/pallas_call | solution.py:37
  20.8 0.4 %collective-permute-done.11.refs_0_ = bf16[32,1536]{1,0:T(8,128)(2,1)S(1)} collective-permute-done((bf16[32,1536]{1,0:T(8,128)(2,1)S(1)}, bf16[32,1536]{1,0:T(8,128)(2,1)S(1)}, u32[]{:S(2)}, u32[]{:S(2)}) %collective-permute-start.11) | collective-permute-done | bytes 98336 | tf_op jit(solution)/shard_map/ppermute | solution.py:253
  21.2 0.3 %send.1 = (f32[40,256]{1,0:T(8,128)S(1)}, f32[40,256]{1,0:T(8,128)S(1)}) custom-call(bf16[8192,256]{1,0:T(8,128)(2,1)S(1)} %get-tuple-element.33.store, f32[8,256]{1,0:T(8,128)S(1)} %get-tuple-element.34.sq, f32[72,256]{1,0:T(8,128)S(1)} %collective-permute-done.7.got, f32[64,256]{1,0:T(8,128)S(1)} %even.1.before, ...), custom_call_target="tpu_custom_call" | custom-call | flops 13800000 | tf_op jit(solution)/shard_map/send/pallas_call | solution.py:37
  21.5 2.9 %collective-permute-start.12 = (f32[40,256]{1,0:T(8,128)S(1)}, f32[40,256]{1,0:T(8,128)S(1)}, u32[]{:S(2)}, u32[]{:S(2)}) collective-permute-start(f32[40,256]{1,0:T(8,128)S(1)} %get-tuple-element.42), channel_id=1, source_target_pairs={{0,8},{4,12},{8,0},{12,4},{1,9},{5,13},{9,1},{13,5},{2,10},{6,14},... | collective-permute-start | bytes 122888 | tf_op jit(solution)/shard_map/ppermute | solution.py:296
  24.3 2.1 %collective-permute-done.12.refs_1_ = f32[40,256]{1,0:T(8,128)S(1)} collective-permute-done((f32[40,256]{1,0:T(8,128)S(1)}, f32[40,256]{1,0:T(8,128)S(1)}, u32[]{:S(2)}, u32[]{:S(2)}) %collective-permute-start.12) | collective-permute-done | bytes 40992 | tf_op jit(solution)/shard_map/ppermute | solution.py:296
  26.5 0.6 %finish.1 = f32[32,256]{1,0:T(8,128)} custom-call(f32[40,256]{1,0:T(8,128)S(1)} %get-tuple-element.41.refs_0_, f32[40,256]{1,0:T(8,128)S(1)} %collective-permute-done.12.refs_1_), custom_call_target="tpu_custom_call" | custom-call | flops 13800000 | tf_op jit(solution)/shard_map/finish/pallas_call | solution.py:37
  (1 shorter events, 0.0 us)
Async XLA Ops:
  0.0 11.7 %copy-start = (bf16[256,8192]{1,0:T(8,128)(2,1)S(1)}, bf16[256,8192]{1,0:T(8,128)(2,1)}, u32[]{:S(2)}) copy-start(bf16[256,8192]{1,0:T(8,128)(2,1)} %store.2) | copy-start | bytes 12582916
  0.0 2.2 %collective-permute-start = (bf16[32,8192]{1,0:T(8,128)(2,1)}, bf16[32,8192]{1,0:T(8,128)(2,1)S(1)}, u32[]{:S(2)}, u32[]{:S(2)}) collective-permute-start(bf16[32,8192]{1,0:T(8,128)(2,1)} %refs_4_.1), channel_id=1, source_target_pairs={{0,1},{1,0},{2,3},{3,2},{4,5},{5,4},{6,7},{7,6},{8,9},{9,8},{10,11... | collective-permute-start | bytes 1572872 | tf_op jit(solution)/shard_map/ppermute | solution.py:253
  3.4 3.1 %collective-permute-start.1 = (bf16[16,4096]{1,0:T(8,128)(2,1)S(1)}, bf16[16,4096]{1,0:T(8,128)(2,1)S(1)}, u32[]{:S(2)}, u32[]{:S(2)}) collective-permute-start(bf16[16,4096]{1,0:T(8,128)(2,1)S(1)} %precondition_1_0.1.refs_0_), channel_id=1, source_target_pairs={{0,1},{1,0},{2,3},{3,2},{4,5},{5,4},{6,7},{7,6},{8,9},{9,8},{10,11... | collective-permute-start | bytes 393224 | tf_op jit(solution)/shard_map/ppermute | solution.py:253
  3.9 9.0 %collective-permute-start.2 = (bf16[16,4096]{1,0:T(8,128)(2,1)S(1)}, bf16[16,4096]{1,0:T(8,128)(2,1)S(1)}, u32[]{:S(2)}, u32[]{:S(2)}) collective-permute-start(bf16[16,4096]{1,0:T(8,128)(2,1)S(1)} %precondition_1_0.1.refs_0_), channel_id=1, source_target_pairs={{0,2},{1,3},{2,0},{3,1},{4,6},{5,7},{6,4},{7,5},{8,10},{9,11},{10,... | collective-permute-start | bytes 393224 | tf_op jit(solution)/shard_map/ppermute | solution.py:256
  7.7 5.7 %collective-permute-start.3 = (bf16[16,4096]{1,0:T(8,128)(2,1)S(1)}, bf16[16,4096]{1,0:T(8,128)(2,1)S(1)}, u32[]{:S(2)}, u32[]{:S(2)}) collective-permute-start(bf16[16,4096]{1,0:T(8,128)(2,1)S(1)} %precondition_1_16.1.refs_1_), channel_id=1, source_target_pairs={{0,2},{1,3},{2,0},{3,1},{4,6},{5,7},{6,4},{7,5},{8,10},{9,11},{10,... | collective-permute-start | bytes 393224 | tf_op jit(solution)/shard_map/ppermute | solution.py:256
  10.8 8.2 %collective-permute-start.8 = (bf16[32,4096]{1,0:T(8,128)(2,1)S(1)}, bf16[32,4096]{1,0:T(8,128)(2,1)S(1)}, u32[]{:S(2)}, u32[]{:S(2)}) collective-permute-start(bf16[32,4096]{1,0:T(8,128)(2,1)S(1)} %precondition_0_0.1.refs_0_), channel_id=1, source_target_pairs={{0,2},{1,3},{2,0},{3,1},{4,6},{5,7},{6,4},{7,5},{8,10},{9,11},{10,... | collective-permute-start | bytes 786440 | tf_op jit(solution)/shard_map/ppermute | solution.py:256
  11.7 2.8 %collective-permute-start.4 = (bf16[16,4096]{1,0:T(8,128)(2,1)S(1)}, bf16[16,4096]{1,0:T(8,128)(2,1)S(1)}, u32[]{:S(2)}, u32[]{:S(2)}) collective-permute-start(bf16[16,4096]{1,0:T(8,128)(2,1)S(1)} %precondition_1_16.1.refs_1_), channel_id=1, source_target_pairs={{0,1},{1,0},{2,3},{3,2},{4,5},{5,4},{6,7},{7,6},{8,9},{9,8},{10,11... | collective-permute-start | bytes 393224 | tf_op jit(solution)/shard_map/ppermute | solution.py:253
  12.9 1.6 %collective-permute-start.5 = (bf16[16,4096]{1,0:T(8,128)(2,1)S(1)}, bf16[16,4096]{1,0:T(8,128)(2,1)S(1)}, u32[]{:S(2)}, u32[]{:S(2)}) collective-permute-start(bf16[16,4096]{1,0:T(8,128)(2,1)S(1)} %collective-permute-done.2.refs_2_), channel_id=1, source_target_pairs={{0,1},{1,0},{2,3},{3,2},{4,5},{5,4},{6,7},{7,6},{8,9},{9,8},{10,11... | collective-permute-start | bytes 393224 | tf_op jit(solution)/shard_map/ppermute | solution.py:253
  13.5 1.3 %collective-permute-start.6 = (bf16[16,4096]{1,0:T(8,128)(2,1)S(1)}, bf16[16,4096]{1,0:T(8,128)(2,1)S(1)}, u32[]{:S(2)}, u32[]{:S(2)}) collective-permute-start(bf16[16,4096]{1,0:T(8,128)(2,1)S(1)} %collective-permute-done.3.refs_3_), channel_id=1, source_target_pairs={{0,1},{1,0},{2,3},{3,2},{4,5},{5,4},{6,7},{7,6},{8,9},{9,8},{10,11... | collective-permute-start | bytes 393224 | tf_op jit(solution)/shard_map/ppermute | solution.py:253
  13.5 6.9 %collective-permute-start.9 = (bf16[32,4096]{1,0:T(8,128)(2,1)S(1)}, bf16[32,4096]{1,0:T(8,128)(2,1)S(1)}, u32[]{:S(2)}, u32[]{:S(2)}) collective-permute-start(bf16[32,4096]{1,0:T(8,128)(2,1)S(1)} %precondition_0_0.1.refs_0_), channel_id=1, source_target_pairs={{0,1},{1,0},{2,3},{3,2},{4,5},{5,4},{6,7},{7,6},{8,9},{9,8},{10,11... | collective-permute-start | bytes 786440 | tf_op jit(solution)/shard_map/ppermute | solution.py:253
  15.3 4.6 %collective-permute-start.7 = (f32[72,256]{1,0:T(8,128)S(1)}, f32[72,256]{1,0:T(8,128)S(1)}, u32[]{:S(2)}, u32[]{:S(2)}) collective-permute-start(f32[72,256]{1,0:T(8,128)S(1)} %odd.1), channel_id=1, source_target_pairs={{0,4},{4,0},{8,12},{12,8},{1,5},{5,1},{9,13},{13,9},{2,6},{6,2},{1... | collective-permute-start | bytes 221192 | tf_op jit(solution)/shard_map/ppermute | solution.py:281
  19.0 1.5 %collective-permute-start.10 = (bf16[32,2560]{1,0:T(8,128)(2,1)S(1)}, bf16[32,2560]{1,0:T(8,128)(2,1)S(1)}, u32[]{:S(2)}, u32[]{:S(2)}) collective-permute-start(bf16[32,2560]{1,0:T(8,128)(2,1)S(1)} %get-tuple-element.38), channel_id=1, source_target_pairs={{0,1},{1,0},{2,3},{3,2},{4,5},{5,4},{6,7},{7,6},{8,9},{9,8},{10,11... | collective-permute-start | bytes 491528 | tf_op jit(solution)/shard_map/ppermute | solution.py:253
  19.9 1.3 %collective-permute-start.11 = (bf16[32,1536]{1,0:T(8,128)(2,1)S(1)}, bf16[32,1536]{1,0:T(8,128)(2,1)S(1)}, u32[]{:S(2)}, u32[]{:S(2)}) collective-permute-start(bf16[32,1536]{1,0:T(8,128)(2,1)S(1)} %get-tuple-element.40), channel_id=1, source_target_pairs={{0,1},{1,0},{2,3},{3,2},{4,5},{5,4},{6,7},{7,6},{8,9},{9,8},{10,11... | collective-permute-start | bytes 294920 | tf_op jit(solution)/shard_map/ppermute | solution.py:253
  21.5 5.0 %collective-permute-start.12 = (f32[40,256]{1,0:T(8,128)S(1)}, f32[40,256]{1,0:T(8,128)S(1)}, u32[]{:S(2)}, u32[]{:S(2)}) collective-permute-start(f32[40,256]{1,0:T(8,128)S(1)} %get-tuple-element.42), channel_id=1, source_target_pairs={{0,8},{4,12},{8,0},{12,4},{1,9},{5,13},{9,1},{13,5},{2,10},{6,14},... | collective-permute-start | bytes 122888 | tf_op jit(solution)/shard_map/ppermute | solution.py:296

commit v4 on v3

v4 whole, which is shorter than its diff:
```python
import functools

import jax
import jax.numpy as jnp
from jax import lax
from jax.experimental import pallas as pl
from jax.experimental.pallas import tpu as pltpu
from jax.sharding import PartitionSpec as P

damping = 0.1
f32, bf16 = jnp.float32, jnp.bfloat16
WHOLE = pl.BlockSpec(memory_space=pltpu.VMEM)
HBM = pl.BlockSpec(memory_space=pltpu.HBM)
SIDE = 64
SCALE = 0.02
LANES = 128
PAIRS = SIDE // 2
FLAT = SIDE * SIDE
PAD = 8
ROWS = 16


def near(x):
    return pltpu.with_memory_space_constraint(x, pltpu.VMEM)


def far(x):
    return pltpu.with_memory_space_constraint(x, pltpu.HBM)


def after(x, *others):
    return lax.optimization_barrier((x, *others))[0]


def call(body, name, outs, ins, scratch=(), us=1.0, specs=None, to=WHOLE):
    return pl.pallas_call(
        body,
        out_shape=outs,
        in_specs=specs or [WHOLE] * len(ins),
        out_specs=jax.tree.map(lambda _: to, outs, is_leaf=lambda o: hasattr(o, "shape")),
        scratch_shapes=scratch,
        cost_estimate=pl.CostEstimate(flops=int(us * 1.15e9 * SCALE), bytes_accessed=0, transcendentals=0),
        compiler_params=pltpu.CompilerParams(vmem_limit_bytes=40 * 2**20),
        name=name,
    )(*ins)


def split(x):
    high = x.astype(bf16)
    return high, (x - high.astype(f32)).astype(bf16)


def mm(a, b):
    return jnp.dot(a, b, preferred_element_type=f32)


def position():
    ex, dim = lax.axis_index("ex"), lax.axis_index("dim")
    return ex // 2, ex % 2, dim


def sides(table):
    high, low = split(table)
    return jnp.concatenate([high, high, low, low], axis=1)


def four(x):
    high, low = split(x)
    return jnp.concatenate([high, low, high, low], axis=0)


def paired(x, y):
    first = lax.broadcasted_iota(jnp.int32, x.shape, 1) < SIDE
    return jnp.where(first, x, pltpu.roll(y, SIDE, 1)), jnp.where(first, pltpu.roll(x, SIDE, 1), y)


def turn_store(store, turned, first):
    columns, rows = turned.shape
    squares = jnp.zeros((8, rows), f32)
    for column in range(0, columns, rows):
        part = store[:, pl.ds(pl.multiple_of(first + column, LANES), rows)].T
        turned[column : column + rows] = part
        part = part.astype(f32)
        squares += jnp.sum((part * part).reshape(-1, 8, rows), axis=0)
    return squares


def factors_body(*refs):
    given, refs = refs[:5], refs[5:]
    forth, back, turn, unturn, inverse, own = refs[:6]
    left, right, val_left, val_right, sems = refs[6:]
    layer = position()[1]
    copies = []
    for k, (g, h) in enumerate(zip(given, [left, right, val_left, val_right, own])):
        copies.append(pltpu.make_async_copy(g.at[layer] if k < 2 else g, h, sems.at[k]))
    for copy in copies:
        copy.start()
    for copy in copies[:4]:
        copy.wait()
    table = jnp.concatenate([left[pl.ds(low, PAIRS, stride=2), :] for low in range(2)], axis=0)
    back[...] = sides(table)
    forth[...] = sides(table.T)
    twice = jnp.concatenate([right[...]] * 2, axis=1)
    half = lax.broadcasted_iota(jnp.int32, (SIDE, LANES), 1) // SIDE
    table = jnp.concatenate([jnp.where(half == low, twice, 0.0) for low in range(2)], axis=0)
    turn[...] = jnp.concatenate(split(table), axis=0)
    both = jnp.concatenate(split(table.T), axis=1)
    unturn[...] = jnp.concatenate([both, both], axis=0)
    along = jnp.concatenate([val_right[pl.ds(layer, 1), :]] * 2, axis=1)
    down = jnp.broadcast_to(val_left[pl.ds(layer, 1), :], (SIDE, SIDE)).T
    inverse[...] = 1.0 / (jnp.concatenate([down] * 2, axis=1) * along + damping)
    copies[4].wait()


def factors(queries, left, right, val_left, val_right):
    shapes = [((64, 256), bf16)] * 2 + [((256, 128), bf16), ((256, 256), bf16), ((64, 128), f32), (queries.shape, bf16)]
    given = (left, right, val_left, val_right, queries)
    scratch = [pltpu.VMEM(x.shape[1:] if x.ndim == 3 else x.shape, f32) for x in given[:4]]
    scratch.append(pltpu.SemaphoreType.DMA((5,)))
    *tables, own = call(
        factors_body,
        "factors",
        [pltpu.VMEM(shape, kind) for shape, kind in shapes],
        [far(x) for x in given],
        scratch,
        us=1.2,
        specs=[HBM] * 5,
    )
    return tables, own


def pick_body(own, other, out):
    _, core, dim = position()
    part = pl.ds(pl.multiple_of(core * FLAT, FLAT), FLAT)
    out[...] = jnp.where((core + dim) % 2 == 1, own[:ROWS, part], other[:ROWS, part])


def pick(own, other):
    return call(pick_body, "pick", pltpu.VMEM((ROWS, FLAT), bf16), [near(x) for x in (own, other)], us=0.1)


def precondition_body(parity, first, pieces, *refs):
    pieces, refs = refs[:pieces], refs[pieces:]
    forth, back, turn, unturn, inverse = refs[:5]
    outs, buffer = refs[5:-1], refs[-1]
    _, core, dim = position()
    size = outs[0].shape[0]
    count = size * len(outs)
    pitch, pitch_back = count + PAD, PAIRS + PAD
    x = []
    for a in range(PAIRS):
        if parity is None:
            x += [piece[:, a * LANES : (a + 1) * LANES] for piece in pieces]
        else:
            part = pl.ds(pl.multiple_of(core * FLAT + a * LANES, LANES), LANES)
            own, other = [piece[first : first + count, part] for piece in pieces]
            x.append(jnp.where((core + dim) % 2 == parity, own, other))
    x = jnp.concatenate(x, axis=0)
    t = mm(x, turn[:LANES]) + mm(x, turn[LANES:])
    for a in range(PAIRS):
        buffer[a * pitch : a * pitch + count] = t[a * count : (a + 1) * count]
    turned = []
    for n in range(0, count, 2):
        two = [buffer[pl.ds(n + k, PAIRS, stride=pitch), :] for k in range(2)]
        turned.append(jnp.concatenate(paired(*two), axis=0))
    t = mm(forth[...], four(jnp.concatenate(turned, axis=1)))
    t = mm(back[...], four(t * jnp.concatenate([inverse[...]] * (count // 2), axis=1)))
    rows = []
    for n in range(0, count * SIDE, LANES):
        rows += paired(t[:PAIRS, n : n + LANES], t[PAIRS:, n : n + LANES])
    t = mm(jnp.concatenate(split(jnp.concatenate(rows, axis=0)), axis=1), unturn[...])
    t = t[:, :LANES] + t[:, LANES:]
    for n in range(count):
        buffer[n * pitch_back : n * pitch_back + PAIRS] = t[n * PAIRS : (n + 1) * PAIRS]
    for a in range(PAIRS):
        part = buffer[pl.ds(a, count, stride=pitch_back), :].astype(bf16)
        for k, out in enumerate(outs):
            out[:, a * LANES : (a + 1) * LANES] = part[k * size : (k + 1) * size]


def precondition(name, pieces, tables, outs, rows, parity=None, first=0):
    count = outs * rows
    return call(
        functools.partial(precondition_body, parity, first, len(pieces)),
        name,
        [pltpu.VMEM((rows, FLAT), bf16)] * outs,
        [near(x) for x in (*pieces, *tables)],
        [pltpu.VMEM((max(PAIRS * (count + PAD), count * (PAIRS + PAD)), LANES), f32)],
        us=1.8 * count / 32,
    )


def scores(pieces, turned, first=0):
    x = jnp.concatenate(pieces, axis=0)
    return mm(x, turned[first : first + x.shape[1], :])


def store_body(store, ours, theirs, out):
    core = position()[1]
    total = turn_store(store, ours, core * FLAT) + turn_store(store, theirs, (1 - core) * FLAT)
    out[...] = jnp.broadcast_to(jnp.sum(total, axis=0, keepdims=True), out.shape)


def ours_body(turned, *refs):
    refs[-1][...] = scores([r[...] for r in refs[:-1]], turned)


def odd_body(chips, turned, sq, before, *refs):
    pieces, (message, total) = refs[:-2], refs[-2:]
    x = position()[0]
    total[...] = before[...] + scores([r[...] for r in pieces], turned)
    count = total.shape[0] // chips
    for block in range(chips):
        apart = lax.rem(x - block + chips, chips)
        message[block * count : (block + 1) * count] = total[pl.ds(pl.multiple_of(apart * count, count), count), :]
    message[chips * count :] = sq[...]


def even_body(turned, before, theirs, *refs):
    out = refs[-1]
    out[...] = before[...] + scores([theirs[...], *[r[...] for r in refs[:-1]]], turned)


def relay_body(count, partners, sq, got, *outs):
    dim = position()[2]
    for out, partner in zip(outs, partners):
        block = partner(dim) // 2
        out[:count] = got[pl.ds(pl.multiple_of(block * count, count), count), :]
        out[count:] = sq[...] + got[got.shape[0] - sq.shape[0] :]


def send_body(chips, partners, total, *refs):
    x, _, dim = position()
    count = total.shape[0] // chips
    for relayed, message, partner in zip(refs[: len(partners)], refs[len(partners) :], partners):
        apart = lax.rem(x - partner(dim) // 2 + chips, chips)
        message[:count] = relayed[:count] + total[pl.ds(pl.multiple_of(apart * count, count), count), :]
        message[count:] = relayed[count:]


def finish_body(*refs):
    out, here, sem = refs[-3:]
    total = refs[0][...]
    for r in refs[1:-3]:
        total = total + r[...]
    count = out.shape[0]
    here[...] = total[:count] / jnp.sqrt(total[count : count + 1] + 1e-06)
    copy = pltpu.make_async_copy(here, out, sem)
    copy.start()
    copy.wait()


def local(dims, exs, store, queries, eig_left, eig_right, val_left, val_right):
    count, rows = queries.shape[0], store.shape[0]
    chips = exs // 2
    across = [(e, e ^ 1) for e in range(exs)]

    def swap(x):
        return lax.ppermute(x, "ex", across)

    def hop(x, step):
        return lax.ppermute(x, "ex", [(e, (e + 2 * step) % exs) for e in range(exs)])

    other = swap(queries)
    tables, own = factors(queries, eig_left, eig_right, val_left, val_right)
    raw = pick(own, other)
    raw_came = [hop(raw, step) for step in range(1, chips)]
    later = count - ROWS
    odd_b = precondition("odd_b", (own, other), tables, 1, later, 1, ROWS)[0]
    odd_b_came = [hop(odd_b, step) for step in range(1, chips)]
    odd_b_swapped = swap(odd_b)
    ours = precondition("even", (after(own, odd_b), other), tables, 1, count, 0)[0]
    outs = [pltpu.VMEM((FLAT, rows), bf16)] * 2 + [pltpu.VMEM((8, rows), f32)]
    turned_ours, turned_theirs, sq = call(store_body, "store", outs, [near(after(store, ours))], us=1.2)
    even_came = [hop(after(ours, sq), step) for step in range(1, chips)]
    theirs = swap(ours)
    odd_a, *odd_a_came = precondition("odd_a", (after(raw, sq), *raw_came), tables, chips, ROWS)

    odd_b_came = [after(x, odd_a) for x in odd_b_came]
    odd = [x for pair in zip((odd_a, *odd_a_came), (odd_b, *odd_b_came)) for x in pair]
    scratch = [pltpu.VMEM((count * chips, rows), f32)]
    part = call(ours_body, "odd_ours", scratch[0], [near(x) for x in (turned_ours, *odd)], us=0.5)
    swapped = [x for pair in zip(map(swap, (odd_a, *odd_a_came)), (odd_b_swapped, *map(swap, odd_b_came))) for x in pair]
    out = pltpu.VMEM((chips * count + 8, rows), f32)
    ins = [near(x) for x in (turned_theirs, sq, part, *swapped)]
    message = call(functools.partial(odd_body, chips), "odd", out, ins, scratch, us=0.5)
    got = lax.ppermute(message, "dim", [(z, z ^ 1) for z in range(dims)])

    even_came = [after(x, message) for x in even_came]
    part = call(ours_body, "even_ours", scratch[0], [near(x) for x in (turned_ours, ours, *even_came)], us=0.5)
    ins = [turned_theirs, part, theirs, *[swap(x) for x in even_came]]
    total = call(even_body, "even", scratch[0], [near(x) for x in ins], us=0.0)

    partners = [lambda z, k=k: lax.bitwise_xor(z, k) for k in range(0, dims, 2)]
    outs = [pltpu.VMEM((count + 8, rows), f32)] * (dims // 2)
    body = functools.partial(relay_body, count, partners)
    relayed = call(body, "relay", outs, [near(x) for x in (sq, got)], us=100.0)
    body = functools.partial(send_body, chips, partners)
    messages = call(body, "send", outs, [near(x) for x in (total, *relayed)], us=0.2)
    sums = [messages[0]]
    for k in range(2, dims, 2):
        sums.append(lax.ppermute(messages[k // 2], "dim", [(z, z ^ k) for z in range(dims)]))
    turned = call(
        finish_body,
        "finish",
        jax.ShapeDtypeStruct((count, rows), f32),
        [near(x) for x in sums],
        [pltpu.VMEM((count, rows), f32), pltpu.SemaphoreType.DMA],
        us=0.6,
        to=HBM,
    )
    return turned.T


def solution(mesh):
    in_specs = (
        P(("grp", "ex"), "dim"),
        P(("grp", "ex"), "dim"),
        P(("grp", "dim"), None, None),
        P(("grp", "dim"), None, None),
        P(("grp", "dim"), None),
        P(("grp", "dim"), None),
    )
    out_specs = P(("grp", "ex"), "dim")
    body = functools.partial(local, mesh.shape["dim"], mesh.shape["ex"])
    return jax.shard_map(body, mesh=mesh, in_specs=in_specs, out_specs=out_specs, check_vma=False)
```

time: 27.3 us -> 26.1 us (0.956)
  Pallas kernels: 9.57 us -> 8.62 us
  starting transfers between devices: 11.7 us -> 11 us
  waiting for transfers between devices: 5.72 us -> 6.2 us
    pallas_call x12 -> x13, Pallas kernels: 9.57 us -> 8.62 us  [call(): pl.pallas_call(body, out_shape=outs, in_specs=specs or [WHOLE] * len(ins)...]
    ppermute x3, waiting for transfers between devices: 1.64 us -> 0.9 us  [hop(): lax.ppermute(x, 'ex', [(e, (e + 2 * step) % exs) for e in range(exs)])]
    ppermute x1, waiting for transfers between devices: 0.85 us -> 1.5 us  [local(): got = lax.ppermute(message, 'dim', [(z, z ^ 1) for z in range(dims)])]
    ppermute x1, waiting for transfers between devices: 2.12 us -> 2.69 us  [local(): lax.ppermute(messages[k // 2], 'dim', [(z, z ^ k) for z in range(dims)])]
    ppermute x8 -> x7, starting transfers between devices: 2.05 us -> 1.59 us  [swap(): return lax.ppermute(x, 'ex', across)]
    ppermute x1, starting transfers between devices: 2 us -> 1.64 us  [local(): got = lax.ppermute(message, 'dim', [(z, z ^ 1) for z in range(dims)])]
    ppermute x3, starting transfers between devices: 4.79 us -> 5.08 us  [hop(): lax.ppermute(x, 'ex', [(e, (e + 2 * step) % exs) for e in range(exs)])]
    ppermute x8 -> x7, waiting for transfers between devices: 1.11 us -> 1.11 us  [swap(): return lax.ppermute(x, 'ex', across)]
  transfers between devices with their start and end apart: 13 -> 12, of which waited for: 6 -> 6; matrix products, arithmetic and copies ran while one was open for 0% -> 0% of each run, Pallas kernels for 27% -> 29%
where the time goes in v4:
time: 26.1 us; the launch traced here: 25.9 us
  starting transfers between devices  11 us (42%)
  Pallas kernels  8.62 us (33%)
  waiting for transfers between devices  6.2 us (24%)
    pallas_call x13, Pallas kernels, call(): pl.pallas_call(body, out_shape=outs, in_specs=specs or [WHOLE] * len(ins)...  8.62 us
    ppermute x3, starting transfers between devices, hop(): lax.ppermute(x, 'ex', [(e, (e + 2 * step) % exs) for e in range(exs)])  5.08 us
    ppermute x1, waiting for transfers between devices, local(): lax.ppermute(messages[k // 2], 'dim', [(z, z ^ k) for z in range(dims)])  2.69 us
    ppermute x1, starting transfers between devices, local(): lax.ppermute(messages[k // 2], 'dim', [(z, z ^ k) for z in range(dims)])  2.66 us
    ppermute x1, starting transfers between devices, local(): got = lax.ppermute(message, 'dim', [(z, z ^ 1) for z in range(dims)])  1.64 us
    ppermute x7, starting transfers between devices, swap(): return lax.ppermute(x, 'ex', across)  1.59 us
    ppermute x1, waiting for transfers between devices, local(): got = lax.ppermute(message, 'dim', [(z, z ^ 1) for z in range(dims)])  1.5 us
    ppermute x7, waiting for transfers between devices, swap(): return lax.ppermute(x, 'ex', across)  1.11 us
  transfers between devices with their start and end apart: 12, of which 6 were waited for; matrix products, arithmetic and copies ran while one was open for 0% of the time, Pallas kernels for 29%

profile of v4, /device:TPU:0, one launch (start us, length us, event | category | flops | bytes accessed | tf_op | source)
XLA Modules:
  0.0 25.9 jit_solution(843018266705470274)
XLA Ops:
  0.0 0.5 %collective-permute-start = (bf16[32,8192]{1,0:T(8,128)(2,1)}, bf16[32,8192]{1,0:T(8,128)(2,1)S(1)}, u32[]{:S(2)}, u32[]{:S(2)}) collective-permute-start(bf16[32,8192]{1,0:T(8,128)(2,1)} %refs_4_.1), channel_id=1, source_target_pairs={{0,1},{1,0},{2,3},{3,2},{4,5},{5,4},{6,7},{7,6},{8,9},{9,8},{10,11... | collective-permute-start | bytes 1572872 | tf_op jit(solution)/shard_map/ppermute | solution.py:259
  0.5 1.2 %factors.1 = (bf16[64,256]{1,0:T(8,128)(2,1)S(1)}, bf16[64,256]{1,0:T(8,128)(2,1)S(1)}, bf16[256,128]{1,0:T(8,128)(2,1)S(1)}, bf16[256,256]{1,0:T(8,128)(2,1)S(1...) custom-call(f32[2,64,64]{2,1,0:T(8,128)} %refs_0_.1, f32[2,64,64]{2,1,0:T(8,128)} %refs_1_.1, f32[2,64]{1,0:T(2,128)} %refs_2_.1, ...), custom_call_target="tpu_custom_call" | custom-call | flops 27600000 | tf_op jit(solution)/shard_map/factors/pallas_call | solution.py:36
  1.6 0.6 %collective-permute-done.refs_1_.other = bf16[32,8192]{1,0:T(8,128)(2,1)S(1)} collective-permute-done((bf16[32,8192]{1,0:T(8,128)(2,1)}, bf16[32,8192]{1,0:T(8,128)(2,1)S(1)}, u32[]{:S(2)}, u32[]{:S(2)}) %collective-permute-start) | collective-permute-done | bytes 524320 | tf_op jit(solution)/shard_map/ppermute | solution.py:259
  2.2 0.0 copy-start
  2.2 2.9 %collective-permute-start.2 = (bf16[16,4096]{1,0:T(8,128)(2,1)S(1)}, bf16[16,4096]{1,0:T(8,128)(2,1)S(1)}, u32[]{:S(2)}, u32[]{:S(2)}) collective-permute-start(bf16[16,4096]{1,0:T(8,128)(2,1)S(1)} %pick.1.refs_0_), channel_id=1, source_target_pairs={{0,2},{1,3},{2,0},{3,1},{4,6},{5,7},{6,4},{7,5},{8,10},{9,11},{10,... | collective-permute-start | bytes 393224 | tf_op jit(solution)/shard_map/ppermute | solution.py:262
  5.1 1.0 %odd_b.1.refs_1_ = bf16[16,4096]{1,0:T(8,128)(2,1)S(1)} custom-call(bf16[32,8192]{1,0:T(8,128)(2,1)S(1)} %get-tuple-element.32.refs_0_.own, bf16[32,8192]{1,0:T(8,128)(2,1)S(1)} %collective-permute-done.refs_1_.other, bf16[64,256]{1,0:T(8,128)(2,1)S(1)} %get-tuple-element.27.refs_2_, bf16[64,256]{1,0:T(8,128)(2,1)S(1)} %get-tuple-element.28.refs_3_, ...), custom_call_target="tpu_custom_call" | custom-call | flops 20700000 | tf_op jit(solution)/shard_map/odd_b/pallas_call | solution.py:36
  6.1 0.1 collective-permute-start.3
  6.2 1.3 %even.2.refs_0_ = bf16[32,4096]{1,0:T(8,128)(2,1)S(1)} custom-call(bf16[32,8192]{1,0:T(8,128)(2,1)S(1)} %get-tuple-element.32.refs_0_.own, bf16[32,8192]{1,0:T(8,128)(2,1)S(1)} %collective-permute-done.refs_1_.other, bf16[64,256]{1,0:T(8,128)(2,1)S(1)} %get-tuple-element.27.refs_2_, bf16[64,256]{1,0:T(8,128)(2,1)S(1)} %get-tuple-element.28.refs_3_, ...), custom_call_target="tpu_custom_call" | custom-call | flops 41400000 | tf_op jit(solution)/shard_map/even/pallas_call | solution.py:36
  7.5 0.0 copy-done
  7.5 1.2 %store.1 = (bf16[4096,256]{1,0:T(8,128)(2,1)S(1)}, bf16[4096,256]{1,0:T(8,128)(2,1)S(1)}, f32[8,256]{1,0:T(8,128)S(1)}) custom-call(bf16[256,8192]{1,0:T(8,128)(2,1)S(1)} %copy-done), custom_call_target="tpu_custom_call" | custom-call | flops 27600000 | tf_op jit(solution)/shard_map/store/pallas_call | solution.py:36
  8.8 2.1 %collective-permute-start.1 = (bf16[32,4096]{1,0:T(8,128)(2,1)S(1)}, bf16[32,4096]{1,0:T(8,128)(2,1)S(1)}, u32[]{:S(2)}, u32[]{:S(2)}) collective-permute-start(bf16[32,4096]{1,0:T(8,128)(2,1)S(1)} %even.2.refs_0_), channel_id=1, source_target_pairs={{0,2},{1,3},{2,0},{3,1},{4,6},{5,7},{6,4},{7,5},{8,10},{9,11},{10,... | collective-permute-start | bytes 786440 | tf_op jit(solution)/shard_map/ppermute | solution.py:262
  10.9 0.0 collective-permute-start.5
  10.9 0.0 collective-permute-done.2.refs_1_
  10.9 1.3 %odd_a.1 = (bf16[16,4096]{1,0:T(8,128)(2,1)S(1)}, bf16[16,4096]{1,0:T(8,128)(2,1)S(1)}) custom-call(bf16[16,4096]{1,0:T(8,128)(2,1)S(1)} %pick.1.refs_0_, bf16[16,4096]{1,0:T(8,128)(2,1)S(1)} %collective-permute-done.2.refs_1_, bf16[64,256]{1,0:T(8,128)(2,1)S(1)} %get-tuple-element.27.refs_2_, bf16[64,256]{1,0:T(8,128)(2,1)S(1)} %get-tuple-element.28.refs_3_, ...), custom_call_target="tpu_custom_call" | custom-call | flops 41400000 | tf_op jit(solution)/shard_map/odd_a/pallas_call | solution.py:36
  12.2 0.0 collective-permute-done.3.refs_3_
  12.2 0.6 %collective-permute-start.7 = (bf16[16,4096]{1,0:T(8,128)(2,1)S(1)}, bf16[16,4096]{1,0:T(8,128)(2,1)S(1)}, u32[]{:S(2)}, u32[]{:S(2)}) collective-permute-start(bf16[16,4096]{1,0:T(8,128)(2,1)S(1)} %collective-permute-done.3.refs_3_), channel_id=1, source_target_pairs={{0,1},{1,0},{2,3},{3,2},{4,5},{5,4},{6,7},{7,6},{8,9},{9,8},{10,11... | collective-permute-start | bytes 393224 | tf_op jit(solution)/shard_map/ppermute | solution.py:259
  12.8 0.1 collective-permute-start.6
  12.8 0.4 %collective-permute-start.4 = (bf16[16,4096]{1,0:T(8,128)(2,1)S(1)}, bf16[16,4096]{1,0:T(8,128)(2,1)S(1)}, u32[]{:S(2)}, u32[]{:S(2)}) collective-permute-start(bf16[16,4096]{1,0:T(8,128)(2,1)S(1)} %get-tuple-element.39.refs_0_), channel_id=1, source_target_pairs={{0,1},{1,0},{2,3},{3,2},{4,5},{5,4},{6,7},{7,6},{8,9},{9,8},{10,11... | collective-permute-start | bytes 393224 | tf_op jit(solution)/shard_map/ppermute | solution.py:259
  13.3 0.5 %odd_ours.1.before = f32[64,256]{1,0:T(8,128)S(1)} custom-call(bf16[4096,256]{1,0:T(8,128)(2,1)S(1)} %get-tuple-element.35.turned, bf16[16,4096]{1,0:T(8,128)(2,1)S(1)} %get-tuple-element.39.refs_0_, bf16[16,4096]{1,0:T(8,128)(2,1)S(1)} %odd_b.1.refs_1_, bf16[16,4096]{1,0:T(8,128)(2,1)S(1)} %get-tuple-element.40.refs_2_, ...), custom_call_target="tpu_custom_call" | custom-call | flops 11500000 | tf_op jit(solution)/shard_map/odd_ours/pallas_call | solution.py:36
  13.7 0.0 collective-permute-done.5.refs_1_
  13.8 0.0 collective-permute-done.7.refs_3_
  13.8 0.3 %collective-permute-done.6.refs_2_ = bf16[16,4096]{1,0:T(8,128)(2,1)S(1)} collective-permute-done((bf16[16,4096]{1,0:T(8,128)(2,1)S(1)}, bf16[16,4096]{1,0:T(8,128)(2,1)S(1)}, u32[]{:S(2)}, u32[]{:S(2)}) %collective-permute-start.6) | collective-permute-done | bytes 131104 | tf_op jit(solution)/shard_map/ppermute | solution.py:259
  14.1 0.2 collective-permute-done.4.refs_0_
  14.3 0.5 %odd.1 = f32[72,256]{1,0:T(8,128)S(1)} custom-call(bf16[4096,256]{1,0:T(8,128)(2,1)S(1)} %get-tuple-element.34.turned, f32[8,256]{1,0:T(8,128)S(1)} %get-tuple-element.36.sq, f32[64,256]{1,0:T(8,128)S(1)} %odd_ours.1.before, bf16[16,4096]{1,0:T(8,128)(2,1)S(1)} %collective-permute-done.4.refs_0_, bf16[16,4096]{1,0:T(8,128)(2,1)S(1)} %collective-permute-done.5.refs_1_, ...), custom_call_target="tpu_custom_call" | custom-call | flops 11500000 | tf_op jit(solution)/shard_map/odd/pallas_call | solution.py:36
  14.8 1.6 %collective-permute-start.10 = (f32[72,256]{1,0:T(8,128)S(1)}, f32[72,256]{1,0:T(8,128)S(1)}, u32[]{:S(2)}, u32[]{:S(2)}) collective-permute-start(f32[72,256]{1,0:T(8,128)S(1)} %odd.1), channel_id=1, source_target_pairs={{0,4},{4,0},{8,12},{12,8},{1,5},{5,1},{9,13},{13,9},{2,6},{6,2},{1... | collective-permute-start | bytes 221192 | tf_op jit(solution)/shard_map/ppermute | solution.py:287
  16.4 0.0 collective-permute-start.8
  16.5 0.9 %collective-permute-done.1.refs_1_ = bf16[32,4096]{1,0:T(8,128)(2,1)S(1)} collective-permute-done((bf16[32,4096]{1,0:T(8,128)(2,1)S(1)}, bf16[32,4096]{1,0:T(8,128)(2,1)S(1)}, u32[]{:S(2)}, u32[]{:S(2)}) %collective-permute-start.1) | collective-permute-done | bytes 262176 | tf_op jit(solution)/shard_map/ppermute | solution.py:262
  17.4 0.0 collective-permute-start.9
  17.4 0.5 %even_ours.1.before = f32[64,256]{1,0:T(8,128)S(1)} custom-call(bf16[4096,256]{1,0:T(8,128)(2,1)S(1)} %get-tuple-element.35.turned, bf16[32,4096]{1,0:T(8,128)(2,1)S(1)} %even.2.refs_0_, bf16[32,4096]{1,0:T(8,128)(2,1)S(1)} %collective-permute-done.1.refs_1_), custom_call_target="tpu_custom_call" | custom-call | flops 11500000 | tf_op jit(solution)/shard_map/even_ours/pallas_call | solution.py:36
  17.9 1.5 %collective-permute-done.10.got = f32[72,256]{1,0:T(8,128)S(1)} collective-permute-done((f32[72,256]{1,0:T(8,128)S(1)}, f32[72,256]{1,0:T(8,128)S(1)}, u32[]{:S(2)}, u32[]{:S(2)}) %collective-permute-start.10) | collective-permute-done | bytes 73760 | tf_op jit(solution)/shard_map/ppermute | solution.py:287
  19.4 0.0 collective-permute-done.8.theirs
  19.4 0.0 collective-permute-done.9.refs_0_
  19.4 0.5 %even.3.total = f32[64,256]{1,0:T(8,128)S(1)} custom-call(bf16[4096,256]{1,0:T(8,128)(2,1)S(1)} %get-tuple-element.34.turned, f32[64,256]{1,0:T(8,128)S(1)} %even_ours.1.before, bf16[32,4096]{1,0:T(8,128)(2,1)S(1)} %collective-permute-done.8.theirs, bf16[32,4096]{1,0:T(8,128)(2,1)S(1)} %collective-permute-done.9.refs_0_), custom_call_target="tpu_custom_call" | custom-call | tf_op jit(solution)/shard_map/even/pallas_call | solution.py:36
  19.9 2.7 %collective-permute-start.11 = (f32[40,256]{1,0:T(8,128)S(1)}, f32[40,256]{1,0:T(8,128)S(1)}, u32[]{:S(2)}, u32[]{:S(2)}) collective-permute-start(f32[40,256]{1,0:T(8,128)S(1)} %get-tuple-element.46), channel_id=1, source_target_pairs={{0,8},{4,12},{8,0},{12,4},{1,9},{5,13},{9,1},{13,5},{2,10},{6,14},... | collective-permute-start | bytes 122888 | tf_op jit(solution)/shard_map/ppermute | solution.py:302
  22.6 2.7 %collective-permute-done.11.refs_1_ = f32[40,256]{1,0:T(8,128)S(1)} collective-permute-done((f32[40,256]{1,0:T(8,128)S(1)}, f32[40,256]{1,0:T(8,128)S(1)}, u32[]{:S(2)}, u32[]{:S(2)}) %collective-permute-start.11) | collective-permute-done | bytes 40992 | tf_op jit(solution)/shard_map/ppermute | solution.py:302
  25.3 0.6 %finish.1 = f32[32,256]{1,0:T(8,128)} custom-call(f32[40,256]{1,0:T(8,128)S(1)} %get-tuple-element.45.refs_0_, f32[40,256]{1,0:T(8,128)S(1)} %collective-permute-done.11.refs_1_), custom_call_target="tpu_custom_call" | custom-call | flops 13800000 | tf_op jit(solution)/shard_map/finish/pallas_call | solution.py:36
  (3 shorter events, 0.1 us)
Async XLA Ops:
  0.0 2.2 %collective-permute-start = (bf16[32,8192]{1,0:T(8,128)(2,1)}, bf16[32,8192]{1,0:T(8,128)(2,1)S(1)}, u32[]{:S(2)}, u32[]{:S(2)}) collective-permute-start(bf16[32,8192]{1,0:T(8,128)(2,1)} %refs_4_.1), channel_id=1, source_target_pairs={{0,1},{1,0},{2,3},{3,2},{4,5},{5,4},{6,7},{7,6},{8,9},{9,8},{10,11... | collective-permute-start | bytes 1572872 | tf_op jit(solution)/shard_map/ppermute | solution.py:259
  2.2 5.3 %copy-start = (bf16[256,8192]{1,0:T(8,128)(2,1)S(1)}, bf16[256,8192]{1,0:T(8,128)(2,1)}, u32[]{:S(2)}) copy-start(bf16[256,8192]{1,0:T(8,128)(2,1)} %store.2) | copy-start | bytes 12582916
  2.2 8.7 %collective-permute-start.2 = (bf16[16,4096]{1,0:T(8,128)(2,1)S(1)}, bf16[16,4096]{1,0:T(8,128)(2,1)S(1)}, u32[]{:S(2)}, u32[]{:S(2)}) collective-permute-start(bf16[16,4096]{1,0:T(8,128)(2,1)S(1)} %pick.1.refs_0_), channel_id=1, source_target_pairs={{0,2},{1,3},{2,0},{3,1},{4,6},{5,7},{6,4},{7,5},{8,10},{9,11},{10,... | collective-permute-start | bytes 393224 | tf_op jit(solution)/shard_map/ppermute | solution.py:262
  6.1 6.0 %collective-permute-start.3 = (bf16[16,4096]{1,0:T(8,128)(2,1)S(1)}, bf16[16,4096]{1,0:T(8,128)(2,1)S(1)}, u32[]{:S(2)}, u32[]{:S(2)}) collective-permute-start(bf16[16,4096]{1,0:T(8,128)(2,1)S(1)} %odd_b.1.refs_1_), channel_id=1, source_target_pairs={{0,2},{1,3},{2,0},{3,1},{4,6},{5,7},{6,4},{7,5},{8,10},{9,11},{10,... | collective-permute-start | bytes 393224 | tf_op jit(solution)/shard_map/ppermute | solution.py:262
  8.8 8.6 %collective-permute-start.1 = (bf16[32,4096]{1,0:T(8,128)(2,1)S(1)}, bf16[32,4096]{1,0:T(8,128)(2,1)S(1)}, u32[]{:S(2)}, u32[]{:S(2)}) collective-permute-start(bf16[32,4096]{1,0:T(8,128)(2,1)S(1)} %even.2.refs_0_), channel_id=1, source_target_pairs={{0,2},{1,3},{2,0},{3,1},{4,6},{5,7},{6,4},{7,5},{8,10},{9,11},{10,... | collective-permute-start | bytes 786440 | tf_op jit(solution)/shard_map/ppermute | solution.py:262
  10.9 2.9 %collective-permute-start.5 = (bf16[16,4096]{1,0:T(8,128)(2,1)S(1)}, bf16[16,4096]{1,0:T(8,128)(2,1)S(1)}, u32[]{:S(2)}, u32[]{:S(2)}) collective-permute-start(bf16[16,4096]{1,0:T(8,128)(2,1)S(1)} %odd_b.1.refs_1_), channel_id=1, source_target_pairs={{0,1},{1,0},{2,3},{3,2},{4,5},{5,4},{6,7},{7,6},{8,9},{9,8},{10,11... | collective-permute-start | bytes 393224 | tf_op jit(solution)/shard_map/ppermute | solution.py:259
  12.2 1.6 %collective-permute-start.7 = (bf16[16,4096]{1,0:T(8,128)(2,1)S(1)}, bf16[16,4096]{1,0:T(8,128)(2,1)S(1)}, u32[]{:S(2)}, u32[]{:S(2)}) collective-permute-start(bf16[16,4096]{1,0:T(8,128)(2,1)S(1)} %collective-permute-done.3.refs_3_), channel_id=1, source_target_pairs={{0,1},{1,0},{2,3},{3,2},{4,5},{5,4},{6,7},{7,6},{8,9},{9,8},{10,11... | collective-permute-start | bytes 393224 | tf_op jit(solution)/shard_map/ppermute | solution.py:259
  12.8 1.3 %collective-permute-start.6 = (bf16[16,4096]{1,0:T(8,128)(2,1)S(1)}, bf16[16,4096]{1,0:T(8,128)(2,1)S(1)}, u32[]{:S(2)}, u32[]{:S(2)}) collective-permute-start(bf16[16,4096]{1,0:T(8,128)(2,1)S(1)} %get-tuple-element.40.refs_2_), channel_id=1, source_target_pairs={{0,1},{1,0},{2,3},{3,2},{4,5},{5,4},{6,7},{7,6},{8,9},{9,8},{10,11... | collective-permute-start | bytes 393224 | tf_op jit(solution)/shard_map/ppermute | solution.py:259
  12.8 1.5 %collective-permute-start.4 = (bf16[16,4096]{1,0:T(8,128)(2,1)S(1)}, bf16[16,4096]{1,0:T(8,128)(2,1)S(1)}, u32[]{:S(2)}, u32[]{:S(2)}) collective-permute-start(bf16[16,4096]{1,0:T(8,128)(2,1)S(1)} %get-tuple-element.39.refs_0_), channel_id=1, source_target_pairs={{0,1},{1,0},{2,3},{3,2},{4,5},{5,4},{6,7},{7,6},{8,9},{9,8},{10,11... | collective-permute-start | bytes 393224 | tf_op jit(solution)/shard_map/ppermute | solution.py:259
  14.8 4.6 %collective-permute-start.10 = (f32[72,256]{1,0:T(8,128)S(1)}, f32[72,256]{1,0:T(8,128)S(1)}, u32[]{:S(2)}, u32[]{:S(2)}) collective-permute-start(f32[72,256]{1,0:T(8,128)S(1)} %odd.1), channel_id=1, source_target_pairs={{0,4},{4,0},{8,12},{12,8},{1,5},{5,1},{9,13},{13,9},{2,6},{6,2},{1... | collective-permute-start | bytes 221192 | tf_op jit(solution)/shard_map/ppermute | solution.py:287
  16.4 2.9 %collective-permute-start.8 = (bf16[32,4096]{1,0:T(8,128)(2,1)S(1)}, bf16[32,4096]{1,0:T(8,128)(2,1)S(1)}, u32[]{:S(2)}, u32[]{:S(2)}) collective-permute-start(bf16[32,4096]{1,0:T(8,128)(2,1)S(1)} %even.2.refs_0_), channel_id=1, source_target_pairs={{0,1},{1,0},{2,3},{3,2},{4,5},{5,4},{6,7},{7,6},{8,9},{9,8},{10,11... | collective-permute-start | bytes 786440 | tf_op jit(solution)/shard_map/ppermute | solution.py:259
  17.4 2.0 %collective-permute-start.9 = (bf16[32,4096]{1,0:T(8,128)(2,1)S(1)}, bf16[32,4096]{1,0:T(8,128)(2,1)S(1)}, u32[]{:S(2)}, u32[]{:S(2)}) collective-permute-start(bf16[32,4096]{1,0:T(8,128)(2,1)S(1)} %collective-permute-done.1.refs_1_), channel_id=1, source_target_pairs={{0,1},{1,0},{2,3},{3,2},{4,5},{5,4},{6,7},{7,6},{8,9},{9,8},{10,11... | collective-permute-start | bytes 786440 | tf_op jit(solution)/shard_map/ppermute | solution.py:259
  19.9 5.3 %collective-permute-start.11 = (f32[40,256]{1,0:T(8,128)S(1)}, f32[40,256]{1,0:T(8,128)S(1)}, u32[]{:S(2)}, u32[]{:S(2)}) collective-permute-start(f32[40,256]{1,0:T(8,128)S(1)} %get-tuple-element.46), channel_id=1, source_target_pairs={{0,8},{4,12},{8,0},{12,4},{1,9},{5,13},{9,1},{13,5},{2,10},{6,14},... | collective-permute-start | bytes 122888 | tf_op jit(solution)/shard_map/ppermute | solution.py:302

commit v5 on v4

--- a/solution.py
+++ b/solution.py
@@ -17,6 +17,10 @@
 PAIRS = SIDE // 2
 FLAT = SIDE * SIDE
 PAD = 8
+EVEN = 1000.0
+FACTORS = 1.2
+ODDB = 1.0
+PICK = 200.0
 ROWS = 16
 
 
@@ -123,7 +127,7 @@
         [pltpu.VMEM(shape, kind) for shape, kind in shapes],
         [far(x) for x in given],
         scratch,
-        us=1.2,
+        us=FACTORS,
         specs=[HBM] * 5,
     )
     return tables, own
@@ -136,16 +140,15 @@
 
 
 def pick(own, other):
-    return call(pick_body, "pick", pltpu.VMEM((ROWS, FLAT), bf16), [near(x) for x in (own, other)], us=0.1)
+    return call(pick_body, "pick", pltpu.VMEM((ROWS, FLAT), bf16), [near(x) for x in (own, other)], us=PICK)
 
 
 def precondition_body(parity, first, pieces, *refs):
     pieces, refs = refs[:pieces], refs[pieces:]
     forth, back, turn, unturn, inverse = refs[:5]
-    outs, buffer = refs[5:-1], refs[-1]
+    out, buffer = refs[5:]
     _, core, dim = position()
-    size = outs[0].shape[0]
-    count = size * len(outs)
+    count = out.shape[0]
     pitch, pitch_back = count + PAD, PAIRS + PAD
     x = []
     for a in range(PAIRS):
@@ -173,20 +176,17 @@
     for n in range(count):
         buffer[n * pitch_back : n * pitch_back + PAIRS] = t[n * PAIRS : (n + 1) * PAIRS]
     for a in range(PAIRS):
-        part = buffer[pl.ds(a, count, stride=pitch_back), :].astype(bf16)
-        for k, out in enumerate(outs):
-            out[:, a * LANES : (a + 1) * LANES] = part[k * size : (k + 1) * size]
-
-
-def precondition(name, pieces, tables, outs, rows, parity=None, first=0):
-    count = outs * rows
+        out[:, a * LANES : (a + 1) * LANES] = buffer[pl.ds(a, count, stride=pitch_back), :].astype(bf16)
+
+
+def precondition(name, pieces, tables, count, parity=None, first=0, us=1.0):
     return call(
         functools.partial(precondition_body, parity, first, len(pieces)),
         name,
-        [pltpu.VMEM((rows, FLAT), bf16)] * outs,
+        pltpu.VMEM((count, FLAT), bf16),
         [near(x) for x in (*pieces, *tables)],
         [pltpu.VMEM((max(PAIRS * (count + PAD), count * (PAIRS + PAD)), LANES), f32)],
-        us=1.8 * count / 32,
+        us=us,
     )
 
 
@@ -195,46 +195,64 @@
     return mm(x, turned[first : first + x.shape[1], :])
 
 
-def store_body(store, ours, theirs, out):
+def theirs_body(store, _, turned, rest, out):
     core = position()[1]
-    total = turn_store(store, ours, core * FLAT) + turn_store(store, theirs, (1 - core) * FLAT)
-    out[...] = jnp.broadcast_to(jnp.sum(total, axis=0, keepdims=True), out.shape)
-
-
-def ours_body(turned, *refs):
-    refs[-1][...] = scores([r[...] for r in refs[:-1]], turned)
-
-
-def odd_body(chips, turned, sq, before, *refs):
-    pieces, (message, total) = refs[:-2], refs[-2:]
+    out[...] = turn_store(store, turned, (1 - core) * FLAT)
+    rest[...] = store[:, pl.ds(pl.multiple_of(core * FLAT, FLAT), FLAT)]
+
+
+def ours_body(rest, before, turned, out):
+    out[...] = before[...] + turn_store(rest, turned, 0)
+
+
+def woven(pieces, rows):
+    first, others = pieces[0], pieces[1:]
+    parts = []
+    for k, other in enumerate(others):
+        parts += [first[k * rows : (k + 1) * rows], other[...]]
+    return parts
+
+
+def scores_body(weave, turned, *refs):
+    pieces = woven(refs[:-1], ROWS) if weave else [r[...] for r in refs[:-1]]
+    refs[-1][...] = scores(pieces, turned)
+
+
+def both_scores(name, weave, ours, far_rows, pieces, swap):
+    count = sum(p.shape[0] for p in pieces)
+    out = pltpu.VMEM((count, ours.shape[1]), f32)
+    parts = []
+    for side, turned in (("far", far_rows), ("near", ours)):
+        ins = [near(x) for x in (turned, *pieces)]
+        parts.append(call(functools.partial(scores_body, weave), f"{name}_{side}", out, ins, us=0.5))
+    return swap(parts[0]), parts[1]
+
+
+def odd_body(chips, squares, one, two, message, total):
     x = position()[0]
-    total[...] = before[...] + scores([r[...] for r in pieces], turned)
+    total[...] = one[...] + two[...]
     count = total.shape[0] // chips
     for block in range(chips):
         apart = lax.rem(x - block + chips, chips)
         message[block * count : (block + 1) * count] = total[pl.ds(pl.multiple_of(apart * count, count), count), :]
-    message[chips * count :] = sq[...]
-
-
-def even_body(turned, before, theirs, *refs):
-    out = refs[-1]
-    out[...] = before[...] + scores([theirs[...], *[r[...] for r in refs[:-1]]], turned)
-
-
-def relay_body(count, partners, sq, got, *outs):
+    message[chips * count :] = squares[...]
+
+
+def relay_body(count, partners, squares, got, *outs):
     dim = position()[2]
     for out, partner in zip(outs, partners):
         block = partner(dim) // 2
         out[:count] = got[pl.ds(pl.multiple_of(block * count, count), count), :]
-        out[count:] = sq[...] + got[got.shape[0] - sq.shape[0] :]
-
-
-def send_body(chips, partners, total, *refs):
+        out[count:] = squares[...] + got[got.shape[0] - squares.shape[0] :]
+
+
+def send_body(chips, partners, one, two, *refs):
     x, _, dim = position()
-    count = total.shape[0] // chips
+    count = one.shape[0] // chips
     for relayed, message, partner in zip(refs[: len(partners)], refs[len(partners) :], partners):
         apart = lax.rem(x - partner(dim) // 2 + chips, chips)
-        message[:count] = relayed[:count] + total[pl.ds(pl.multiple_of(apart * count, count), count), :]
+        here = pl.ds(pl.multiple_of(apart * count, count), count)
+        message[:count] = relayed[:count] + (one[here, :] + two[here, :])
         message[count:] = relayed[count:]
 
 
@@ -244,7 +262,7 @@
     for r in refs[1:-3]:
         total = total + r[...]
     count = out.shape[0]
-    here[...] = total[:count] / jnp.sqrt(total[count : count + 1] + 1e-06)
+    here[...] = total[:count] / jnp.sqrt(jnp.sum(total[count:], axis=0, keepdims=True) + 1e-06)
     copy = pltpu.make_async_copy(here, out, sem)
     copy.start()
     copy.wait()
@@ -265,38 +283,35 @@
     tables, own = factors(queries, eig_left, eig_right, val_left, val_right)
     raw = pick(own, other)
     raw_came = [hop(raw, step) for step in range(1, chips)]
-    later = count - ROWS
-    odd_b = precondition("odd_b", (own, other), tables, 1, later, 1, ROWS)[0]
+    odd_b = precondition("odd_b", (after(own, raw), other), tables, count - ROWS, 1, ROWS, us=ODDB)
     odd_b_came = [hop(odd_b, step) for step in range(1, chips)]
-    odd_b_swapped = swap(odd_b)
-    ours = precondition("even", (after(own, odd_b), other), tables, 1, count, 0)[0]
-    outs = [pltpu.VMEM((FLAT, rows), bf16)] * 2 + [pltpu.VMEM((8, rows), f32)]
-    turned_ours, turned_theirs, sq = call(store_body, "store", outs, [near(after(store, ours))], us=1.2)
-    even_came = [hop(after(ours, sq), step) for step in range(1, chips)]
-    theirs = swap(ours)
-    odd_a, *odd_a_came = precondition("odd_a", (after(raw, sq), *raw_came), tables, chips, ROWS)
+    turned, squares = pltpu.VMEM((FLAT, rows), bf16), pltpu.VMEM((8, rows), f32)
+    outs = [turned, pltpu.VMEM((rows, FLAT), bf16), squares]
+    turned_theirs, rest, part = call(theirs_body, "theirs", outs, [near(store), near(odd_b)], us=0.7)
+    far_rows = swap(turned_theirs)
+    ours = precondition("even", (after(own, part), other), tables, count, 0, us=EVEN)
+    even_came = [hop(ours, step) for step in range(1, chips)]
+    ins = [near(x) for x in (after(rest, ours), part)]
+    turned_ours, squares = call(ours_body, "ours", [turned, squares], ins, us=0.6)
+    odd_a = precondition("odd_a", (after(raw, squares), *raw_came), tables, chips * ROWS)
 
     odd_b_came = [after(x, odd_a) for x in odd_b_came]
-    odd = [x for pair in zip((odd_a, *odd_a_came), (odd_b, *odd_b_came)) for x in pair]
+    parts = both_scores("odd", True, turned_ours, far_rows, (odd_a, odd_b, *odd_b_came), swap)
+    out = pltpu.VMEM((chips * count + 8, rows), f32)
     scratch = [pltpu.VMEM((count * chips, rows), f32)]
-    part = call(ours_body, "odd_ours", scratch[0], [near(x) for x in (turned_ours, *odd)], us=0.5)
-    swapped = [x for pair in zip(map(swap, (odd_a, *odd_a_came)), (odd_b_swapped, *map(swap, odd_b_came))) for x in pair]
-    out = pltpu.VMEM((chips * count + 8, rows), f32)
-    ins = [near(x) for x in (turned_theirs, sq, part, *swapped)]
-    message = call(functools.partial(odd_body, chips), "odd", out, ins, scratch, us=0.5)
+    ins = [near(x) for x in (squares, *parts)]
+    message = call(functools.partial(odd_body, chips), "odd", out, ins, scratch, us=0.1)
     got = lax.ppermute(message, "dim", [(z, z ^ 1) for z in range(dims)])
 
     even_came = [after(x, message) for x in even_came]
-    part = call(ours_body, "even_ours", scratch[0], [near(x) for x in (turned_ours, ours, *even_came)], us=0.5)
-    ins = [turned_theirs, part, theirs, *[swap(x) for x in even_came]]
-    total = call(even_body, "even", scratch[0], [near(x) for x in ins], us=0.0)
+    parts = both_scores("even", False, turned_ours, far_rows, (ours, *even_came), swap)
 
     partners = [lambda z, k=k: lax.bitwise_xor(z, k) for k in range(0, dims, 2)]
     outs = [pltpu.VMEM((count + 8, rows), f32)] * (dims // 2)
     body = functools.partial(relay_body, count, partners)
-    relayed = call(body, "relay", outs, [near(x) for x in (sq, got)], us=100.0)
+    relayed = call(body, "relay", outs, [near(x) for x in (squares, got)], us=100.0)
     body = functools.partial(send_body, chips, partners)
-    messages = call(body, "send", outs, [near(x) for x in (total, *relayed)], us=0.2)
+    messages = call(body, "send", outs, [near(x) for x in (*parts, *relayed)], us=0.2)
     sums = [messages[0]]
     for k in range(2, dims, 2):
         sums.append(lax.ppermute(messages[k // 2], "dim", [(z, z ^ k) for z in range(dims)]))

time: 26.1 us -> 25 us (0.958)
  waiting for transfers between devices: 6.2 us -> 5.48 us
  starting transfers between devices: 11 us -> 10.5 us
    ppermute x1, waiting for transfers between devices: 1.5 us -> 0.24 us  [local(): got = lax.ppermute(message, 'dim', [(z, z ^ 1) for z in range(dims)])]
    ppermute x7 -> x4, starting transfers between devices: 1.59 us -> 0.87 us  [swap(): return lax.ppermute(x, 'ex', across)]
    ppermute x3, waiting for transfers between devices: 0.9 us -> 1.53 us  [hop(): lax.ppermute(x, 'ex', [(e, (e + 2 * step) % exs) for e in range(exs)])]
    ppermute x1, waiting for transfers between devices: 2.69 us -> 2.06 us  [local(): lax.ppermute(messages[k // 2], 'dim', [(z, z ^ k) for z in range(dims)])]
    ppermute x7 -> x4, waiting for transfers between devices: 1.11 us -> 1.65 us  [swap(): return lax.ppermute(x, 'ex', across)]
    pallas_call x13 -> x15, Pallas kernels: 8.62 us -> 8.76 us  [call(): pl.pallas_call(body, out_shape=outs, in_specs=specs or [WHOLE] * len(ins)...]
  transfers between devices with their start and end apart: 12 -> 9, of which waited for: 6 -> 6; matrix products, arithmetic and copies ran while one was open for 0% -> 0% of each run, Pallas kernels for 29% -> 32%
where the time goes in v5:
time: 25 us; the launch traced here: 24.9 us
  starting transfers between devices  10.5 us (42%)
  Pallas kernels  8.76 us (35%)
  waiting for transfers between devices  5.48 us (22%)
    pallas_call x15, Pallas kernels, call(): pl.pallas_call(body, out_shape=outs, in_specs=specs or [WHOLE] * len(ins)...  8.76 us
    ppermute x3, starting transfers between devices, hop(): lax.ppermute(x, 'ex', [(e, (e + 2 * step) % exs) for e in range(exs)])  5.07 us
    ppermute x1, starting transfers between devices, local(): lax.ppermute(messages[k // 2], 'dim', [(z, z ^ k) for z in range(dims)])  2.9 us
    ppermute x1, waiting for transfers between devices, local(): lax.ppermute(messages[k // 2], 'dim', [(z, z ^ k) for z in range(dims)])  2.06 us
    ppermute x4, waiting for transfers between devices, swap(): return lax.ppermute(x, 'ex', across)  1.65 us
    ppermute x1, starting transfers between devices, local(): got = lax.ppermute(message, 'dim', [(z, z ^ 1) for z in range(dims)])  1.64 us
    ppermute x3, waiting for transfers between devices, hop(): lax.ppermute(x, 'ex', [(e, (e + 2 * step) % exs) for e in range(exs)])  1.53 us
    ppermute x4, starting transfers between devices, swap(): return lax.ppermute(x, 'ex', across)  0.87 us
  transfers between devices with their start and end apart: 9, of which 6 were waited for; matrix products, arithmetic and copies ran while one was open for 0% of the time, Pallas kernels for 32%

profile of v5, /device:TPU:0, one launch (start us, length us, event | category | flops | bytes accessed | tf_op | source)
XLA Modules:
  0.0 24.9 jit_solution(11675657139894015299)
XLA Ops:
  0.0 0.5 %collective-permute-start = (bf16[32,8192]{1,0:T(8,128)(2,1)}, bf16[32,8192]{1,0:T(8,128)(2,1)S(1)}, u32[]{:S(2)}, u32[]{:S(2)}) collective-permute-start(bf16[32,8192]{1,0:T(8,128)(2,1)} %refs_4_.1), channel_id=1, source_target_pairs={{0,1},{1,0},{2,3},{3,2},{4,5},{5,4},{6,7},{7,6},{8,9},{9,8},{10,11... | collective-permute-start | bytes 1572872 | tf_op jit(solution)/shard_map/ppermute | solution.py:277
  0.5 1.2 %factors.1 = (bf16[64,256]{1,0:T(8,128)(2,1)S(1)}, bf16[64,256]{1,0:T(8,128)(2,1)S(1)}, bf16[256,128]{1,0:T(8,128)(2,1)S(1)}, bf16[256,256]{1,0:T(8,128)(2,1)S(1...) custom-call(f32[2,64,64]{2,1,0:T(8,128)} %refs_0_.1, f32[2,64,64]{2,1,0:T(8,128)} %refs_1_.1, f32[2,64]{1,0:T(2,128)} %refs_2_.1, ...), custom_call_target="tpu_custom_call" | custom-call | flops 27600000 | tf_op jit(solution)/shard_map/factors/pallas_call | solution.py:40
  1.6 0.6 %collective-permute-done.other.refs_1_ = bf16[32,8192]{1,0:T(8,128)(2,1)S(1)} collective-permute-done((bf16[32,8192]{1,0:T(8,128)(2,1)}, bf16[32,8192]{1,0:T(8,128)(2,1)S(1)}, u32[]{:S(2)}, u32[]{:S(2)}) %collective-permute-start) | collective-permute-done | bytes 524320 | tf_op jit(solution)/shard_map/ppermute | solution.py:277
  2.2 0.0 copy-start
  2.2 2.9 %collective-permute-start.3 = (bf16[16,4096]{1,0:T(8,128)(2,1)S(1)}, bf16[16,4096]{1,0:T(8,128)(2,1)S(1)}, u32[]{:S(2)}, u32[]{:S(2)}) collective-permute-start(bf16[16,4096]{1,0:T(8,128)(2,1)S(1)} %pick.1.refs_0_), channel_id=1, source_target_pairs={{0,2},{1,3},{2,0},{3,1},{4,6},{5,7},{6,4},{7,5},{8,10},{9,11},{10,... | collective-permute-start | bytes 393224 | tf_op jit(solution)/shard_map/ppermute | solution.py:280
  5.1 1.0 %odd_b.1._.refs_1_ = bf16[16,4096]{1,0:T(8,128)(2,1)S(1)} custom-call(bf16[32,8192]{1,0:T(8,128)(2,1)S(1)} %get-tuple-element.35.own.refs_0_, bf16[32,8192]{1,0:T(8,128)(2,1)S(1)} %collective-permute-done.other.refs_1_, bf16[64,256]{1,0:T(8,128)(2,1)S(1)} %get-tuple-element.28.refs_2_, bf16[64,256]{1,0:T(8,128)(2,1)S(1)} %get-tuple-element.29.refs_3_, ...), custom_call_target="tpu_custom_call" | custom-call | flops 23000000 | tf_op jit(solution)/shard_map/odd_b/pallas_call | solution.py:40
  6.1 0.1 collective-permute-start.4
  6.2 0.0 copy-done
  6.2 0.8 %theirs.1 = (bf16[4096,256]{1,0:T(8,128)(2,1)S(1)}, bf16[256,4096]{1,0:T(8,128)(2,1)S(1)}, f32[8,256]{1,0:T(8,128)S(1)}) custom-call(bf16[256,8192]{1,0:T(8,128)(2,1)S(1)} %copy-done, bf16[16,4096]{1,0:T(8,128)(2,1)S(1)} %odd_b.1._.refs_1_), custom_call_target="tpu_custom_call" | custom-call | flops 16100000 | tf_op jit(solution)/shard_map/theirs/pallas_call | solution.py:40
  7.0 0.1 collective-permute-start.1
  7.1 1.3 %even.1.refs_0_ = bf16[32,4096]{1,0:T(8,128)(2,1)S(1)} custom-call(bf16[32,8192]{1,0:T(8,128)(2,1)S(1)} %get-tuple-element.35.own.refs_0_, bf16[32,8192]{1,0:T(8,128)(2,1)S(1)} %collective-permute-done.other.refs_1_, bf16[64,256]{1,0:T(8,128)(2,1)S(1)} %get-tuple-element.28.refs_2_, bf16[64,256]{1,0:T(8,128)(2,1)S(1)} %get-tuple-element.29.refs_3_, ...), custom_call_target="tpu_custom_call" | custom-call | flops 23000000512 | tf_op jit(solution)/shard_map/even/pallas_call | solution.py:40
  8.4 2.1 %collective-permute-start.2 = (bf16[32,4096]{1,0:T(8,128)(2,1)S(1)}, bf16[32,4096]{1,0:T(8,128)(2,1)S(1)}, u32[]{:S(2)}, u32[]{:S(2)}) collective-permute-start(bf16[32,4096]{1,0:T(8,128)(2,1)S(1)} %even.1.refs_0_), channel_id=1, source_target_pairs={{0,2},{1,3},{2,0},{3,1},{4,6},{5,7},{6,4},{7,5},{8,10},{9,11},{10,... | collective-permute-start | bytes 786440 | tf_op jit(solution)/shard_map/ppermute | solution.py:280
  10.5 0.6 %ours.1 = (bf16[4096,256]{1,0:T(8,128)(2,1)S(1)}, f32[8,256]{1,0:T(8,128)S(1)}) custom-call(bf16[256,4096]{1,0:T(8,128)(2,1)S(1)} %get-tuple-element.37.rest, f32[8,256]{1,0:T(8,128)S(1)} %get-tuple-element.34.before), custom_call_target="tpu_custom_call" | custom-call | flops 13800000 | tf_op jit(solution)/shard_map/ours/pallas_call | solution.py:40
  11.1 0.0 collective-permute-done.3.refs_1_
  11.1 1.3 %odd_a.1.refs_0_ = bf16[32,4096]{1,0:T(8,128)(2,1)S(1)} custom-call(bf16[16,4096]{1,0:T(8,128)(2,1)S(1)} %pick.1.refs_0_, bf16[16,4096]{1,0:T(8,128)(2,1)S(1)} %collective-permute-done.3.refs_1_, bf16[64,256]{1,0:T(8,128)(2,1)S(1)} %get-tuple-element.28.refs_2_, bf16[64,256]{1,0:T(8,128)(2,1)S(1)} %get-tuple-element.29.refs_3_, ...), custom_call_target="tpu_custom_call" | custom-call | flops 23000000 | tf_op jit(solution)/shard_map/odd_a/pallas_call | solution.py:40
  12.4 0.0 collective-permute-done.4.refs_2_
  12.4 0.0 collective-permute-done.1.turned
  12.4 0.5 %odd_far.1 = f32[64,256]{1,0:T(8,128)S(1)} custom-call(bf16[4096,256]{1,0:T(8,128)(2,1)S(1)} %collective-permute-done.1.turned, bf16[32,4096]{1,0:T(8,128)(2,1)S(1)} %odd_a.1.refs_0_, bf16[16,4096]{1,0:T(8,128)(2,1)S(1)} %odd_b.1._.refs_1_, bf16[16,4096]{1,0:T(8,128)(2,1)S(1)} %collective-permute-done.4.refs_2_), custom_call_target="tpu_custom_call" | custom-call | flops 11500000 | tf_op jit(solution)/shard_map/odd_far/pallas_call | solution.py:40
  12.9 0.3 %collective-permute-start.5 = (f32[64,256]{1,0:T(8,128)S(1)}, f32[64,256]{1,0:T(8,128)S(1)}, u32[]{:S(2)}, u32[]{:S(2)}) collective-permute-start(f32[64,256]{1,0:T(8,128)S(1)} %odd_far.1), channel_id=1, source_target_pairs={{0,1},{1,0},{2,3},{3,2},{4,5},{5,4},{6,7},{7,6},{8,9},{9,8},{10,11... | collective-permute-start | bytes 196616 | tf_op jit(solution)/shard_map/ppermute | solution.py:277
  13.2 0.5 %odd_near.1.two = f32[64,256]{1,0:T(8,128)S(1)} custom-call(bf16[4096,256]{1,0:T(8,128)(2,1)S(1)} %get-tuple-element.41.turned, bf16[32,4096]{1,0:T(8,128)(2,1)S(1)} %odd_a.1.refs_0_, bf16[16,4096]{1,0:T(8,128)(2,1)S(1)} %odd_b.1._.refs_1_, bf16[16,4096]{1,0:T(8,128)(2,1)S(1)} %collective-permute-done.4.refs_2_), custom_call_target="tpu_custom_call" | custom-call | flops 11500000 | tf_op jit(solution)/shard_map/odd_near/pallas_call | solution.py:40
  13.7 0.6 %collective-permute-done.5.one = f32[64,256]{1,0:T(8,128)S(1)} collective-permute-done((f32[64,256]{1,0:T(8,128)S(1)}, f32[64,256]{1,0:T(8,128)S(1)}, u32[]{:S(2)}, u32[]{:S(2)}) %collective-permute-start.5) | collective-permute-done | bytes 65568 | tf_op jit(solution)/shard_map/ppermute | solution.py:277
  14.3 1.6 %collective-permute-start.7 = (f32[72,256]{1,0:T(8,128)S(1)}, f32[72,256]{1,0:T(8,128)S(1)}, u32[]{:S(2)}, u32[]{:S(2)}) collective-permute-start(f32[72,256]{1,0:T(8,128)S(1)} %odd.1), channel_id=1, source_target_pairs={{0,4},{4,0},{8,12},{12,8},{1,5},{5,1},{9,13},{13,9},{2,6},{6,2},{1... | collective-permute-start | bytes 221192 | tf_op jit(solution)/shard_map/ppermute | solution.py:304
  15.9 1.5 %collective-permute-done.2.refs_1_ = bf16[32,4096]{1,0:T(8,128)(2,1)S(1)} collective-permute-done((bf16[32,4096]{1,0:T(8,128)(2,1)S(1)}, bf16[32,4096]{1,0:T(8,128)(2,1)S(1)}, u32[]{:S(2)}, u32[]{:S(2)}) %collective-permute-start.2) | collective-permute-done | bytes 262176 | tf_op jit(solution)/shard_map/ppermute | solution.py:280
  17.4 0.5 %even_far.1 = f32[64,256]{1,0:T(8,128)S(1)} custom-call(bf16[4096,256]{1,0:T(8,128)(2,1)S(1)} %collective-permute-done.1.turned, bf16[32,4096]{1,0:T(8,128)(2,1)S(1)} %even.1.refs_0_, bf16[32,4096]{1,0:T(8,128)(2,1)S(1)} %collective-permute-done.2.refs_1_), custom_call_target="tpu_custom_call" | custom-call | flops 11500000 | tf_op jit(solution)/shard_map/even_far/pallas_call | solution.py:40
  17.9 0.1 collective-permute-start.6
  18.0 0.5 %even_near.1.two = f32[64,256]{1,0:T(8,128)S(1)} custom-call(bf16[4096,256]{1,0:T(8,128)(2,1)S(1)} %get-tuple-element.41.turned, bf16[32,4096]{1,0:T(8,128)(2,1)S(1)} %even.1.refs_0_, bf16[32,4096]{1,0:T(8,128)(2,1)S(1)} %collective-permute-done.2.refs_1_), custom_call_target="tpu_custom_call" | custom-call | flops 11500000 | tf_op jit(solution)/shard_map/even_near/pallas_call | solution.py:40
  18.5 0.2 collective-permute-done.7.got
  18.7 0.5 %collective-permute-done.6.one = f32[64,256]{1,0:T(8,128)S(1)} collective-permute-done((f32[64,256]{1,0:T(8,128)S(1)}, f32[64,256]{1,0:T(8,128)S(1)}, u32[]{:S(2)}, u32[]{:S(2)}) %collective-permute-start.6) | collective-permute-done | bytes 65568 | tf_op jit(solution)/shard_map/ppermute | solution.py:277
  19.2 2.9 %collective-permute-start.8 = (f32[40,256]{1,0:T(8,128)S(1)}, f32[40,256]{1,0:T(8,128)S(1)}, u32[]{:S(2)}, u32[]{:S(2)}) collective-permute-start(f32[40,256]{1,0:T(8,128)S(1)} %get-tuple-element.46), channel_id=1, source_target_pairs={{0,8},{4,12},{8,0},{12,4},{1,9},{5,13},{9,1},{13,5},{2,10},{6,14},... | collective-permute-start | bytes 122888 | tf_op jit(solution)/shard_map/ppermute | solution.py:317
  22.1 2.1 %collective-permute-done.8.refs_1_ = f32[40,256]{1,0:T(8,128)S(1)} collective-permute-done((f32[40,256]{1,0:T(8,128)S(1)}, f32[40,256]{1,0:T(8,128)S(1)}, u32[]{:S(2)}, u32[]{:S(2)}) %collective-permute-start.8) | collective-permute-done | bytes 40992 | tf_op jit(solution)/shard_map/ppermute | solution.py:317
  24.2 0.6 %finish.1 = f32[32,256]{1,0:T(8,128)} custom-call(f32[40,256]{1,0:T(8,128)S(1)} %get-tuple-element.45.refs_0_, f32[40,256]{1,0:T(8,128)S(1)} %collective-permute-done.8.refs_1_), custom_call_target="tpu_custom_call" | custom-call | flops 13800000 | tf_op jit(solution)/shard_map/finish/pallas_call | solution.py:40
  (4 shorter events, 0.1 us)
Async XLA Ops:
  0.0 2.2 %collective-permute-start = (bf16[32,8192]{1,0:T(8,128)(2,1)}, bf16[32,8192]{1,0:T(8,128)(2,1)S(1)}, u32[]{:S(2)}, u32[]{:S(2)}) collective-permute-start(bf16[32,8192]{1,0:T(8,128)(2,1)} %refs_4_.1), channel_id=1, source_target_pairs={{0,1},{1,0},{2,3},{3,2},{4,5},{5,4},{6,7},{7,6},{8,9},{9,8},{10,11... | collective-permute-start | bytes 1572872 | tf_op jit(solution)/shard_map/ppermute | solution.py:277
  2.2 4.0 %copy-start = (bf16[256,8192]{1,0:T(8,128)(2,1)S(1)}, bf16[256,8192]{1,0:T(8,128)(2,1)}, u32[]{:S(2)}) copy-start(bf16[256,8192]{1,0:T(8,128)(2,1)} %store.1) | copy-start | bytes 12582916
  2.2 8.9 %collective-permute-start.3 = (bf16[16,4096]{1,0:T(8,128)(2,1)S(1)}, bf16[16,4096]{1,0:T(8,128)(2,1)S(1)}, u32[]{:S(2)}, u32[]{:S(2)}) collective-permute-start(bf16[16,4096]{1,0:T(8,128)(2,1)S(1)} %pick.1.refs_0_), channel_id=1, source_target_pairs={{0,2},{1,3},{2,0},{3,1},{4,6},{5,7},{6,4},{7,5},{8,10},{9,11},{10,... | collective-permute-start | bytes 393224 | tf_op jit(solution)/shard_map/ppermute | solution.py:280
  6.1 6.3 %collective-permute-start.4 = (bf16[16,4096]{1,0:T(8,128)(2,1)S(1)}, bf16[16,4096]{1,0:T(8,128)(2,1)S(1)}, u32[]{:S(2)}, u32[]{:S(2)}) collective-permute-start(bf16[16,4096]{1,0:T(8,128)(2,1)S(1)} %odd_b.1._.refs_1_), channel_id=1, source_target_pairs={{0,2},{1,3},{2,0},{3,1},{4,6},{5,7},{6,4},{7,5},{8,10},{9,11},{10,... | collective-permute-start | bytes 393224 | tf_op jit(solution)/shard_map/ppermute | solution.py:280
  7.0 5.4 %collective-permute-start.1 = (bf16[4096,256]{1,0:T(8,128)(2,1)S(1)}, bf16[4096,256]{1,0:T(8,128)(2,1)S(1)}, u32[]{:S(2)}, u32[]{:S(2)}) collective-permute-start(bf16[4096,256]{1,0:T(8,128)(2,1)S(1)} %get-tuple-element.33), channel_id=1, source_target_pairs={{0,1},{1,0},{2,3},{3,2},{4,5},{5,4},{6,7},{7,6},{8,9},{9,8},{10,11... | collective-permute-start | bytes 6291464 | tf_op jit(solution)/shard_map/ppermute | solution.py:277
  8.4 9.0 %collective-permute-start.2 = (bf16[32,4096]{1,0:T(8,128)(2,1)S(1)}, bf16[32,4096]{1,0:T(8,128)(2,1)S(1)}, u32[]{:S(2)}, u32[]{:S(2)}) collective-permute-start(bf16[32,4096]{1,0:T(8,128)(2,1)S(1)} %even.1.refs_0_), channel_id=1, source_target_pairs={{0,2},{1,3},{2,0},{3,1},{4,6},{5,7},{6,4},{7,5},{8,10},{9,11},{10,... | collective-permute-start | bytes 786440 | tf_op jit(solution)/shard_map/ppermute | solution.py:280
  12.9 1.3 %collective-permute-start.5 = (f32[64,256]{1,0:T(8,128)S(1)}, f32[64,256]{1,0:T(8,128)S(1)}, u32[]{:S(2)}, u32[]{:S(2)}) collective-permute-start(f32[64,256]{1,0:T(8,128)S(1)} %odd_far.1), channel_id=1, source_target_pairs={{0,1},{1,0},{2,3},{3,2},{4,5},{5,4},{6,7},{7,6},{8,9},{9,8},{10,11... | collective-permute-start | bytes 196616 | tf_op jit(solution)/shard_map/ppermute | solution.py:277
  14.3 4.5 %collective-permute-start.7 = (f32[72,256]{1,0:T(8,128)S(1)}, f32[72,256]{1,0:T(8,128)S(1)}, u32[]{:S(2)}, u32[]{:S(2)}) collective-permute-start(f32[72,256]{1,0:T(8,128)S(1)} %odd.1), channel_id=1, source_target_pairs={{0,4},{4,0},{8,12},{12,8},{1,5},{5,1},{9,13},{13,9},{2,6},{6,2},{1... | collective-permute-start | bytes 221192 | tf_op jit(solution)/shard_map/ppermute | solution.py:304
  17.9 1.3 %collective-permute-start.6 = (f32[64,256]{1,0:T(8,128)S(1)}, f32[64,256]{1,0:T(8,128)S(1)}, u32[]{:S(2)}, u32[]{:S(2)}) collective-permute-start(f32[64,256]{1,0:T(8,128)S(1)} %even_far.1), channel_id=1, source_target_pairs={{0,1},{1,0},{2,3},{3,2},{4,5},{5,4},{6,7},{7,6},{8,9},{9,8},{10,11... | collective-permute-start | bytes 196616 | tf_op jit(solution)/shard_map/ppermute | solution.py:277
  19.2 5.0 %collective-permute-start.8 = (f32[40,256]{1,0:T(8,128)S(1)}, f32[40,256]{1,0:T(8,128)S(1)}, u32[]{:S(2)}, u32[]{:S(2)}) collective-permute-start(f32[40,256]{1,0:T(8,128)S(1)} %get-tuple-element.46), channel_id=1, source_target_pairs={{0,8},{4,12},{8,0},{12,4},{1,9},{5,13},{9,1},{13,5},{2,10},{6,14},... | collective-permute-start | bytes 122888 | tf_op jit(solution)/shard_map/ppermute | solution.py:317

commit v6 on v5

--- a/solution.py
+++ b/solution.py
@@ -206,8 +206,8 @@
 
 
 def woven(pieces, rows):
-    first, others = pieces[0], pieces[1:]
-    parts = []
+    first, others = pieces[0], pieces[1:-1]
+    parts = [pieces[-1][...]]
     for k, other in enumerate(others):
         parts += [first[k * rows : (k + 1) * rows], other[...]]
     return parts
@@ -231,10 +231,10 @@
 def odd_body(chips, squares, one, two, message, total):
     x = position()[0]
     total[...] = one[...] + two[...]
-    count = total.shape[0] // chips
+    count = total.shape[0] // (chips + 1)
     for block in range(chips):
-        apart = lax.rem(x - block + chips, chips)
-        message[block * count : (block + 1) * count] = total[pl.ds(pl.multiple_of(apart * count, count), count), :]
+        place = 1 + lax.rem(x - block + chips, chips)
+        message[block * count : (block + 1) * count] = total[pl.ds(pl.multiple_of(place * count, count), count), :]
     message[chips * count :] = squares[...]
 
 
@@ -246,13 +246,13 @@
         out[count:] = squares[...] + got[got.shape[0] - squares.shape[0] :]
 
 
-def send_body(chips, partners, one, two, *refs):
+def send_body(chips, partners, own, one, two, *refs):
     x, _, dim = position()
-    count = one.shape[0] // chips
+    count = one.shape[0] // (chips - 1)
     for relayed, message, partner in zip(refs[: len(partners)], refs[len(partners) :], partners):
         apart = lax.rem(x - partner(dim) // 2 + chips, chips)
-        here = pl.ds(pl.multiple_of(apart * count, count), count)
-        message[:count] = relayed[:count] + (one[here, :] + two[here, :])
+        there = pl.ds(pl.multiple_of(jnp.maximum(apart - 1, 0) * count, count), count)
+        message[:count] = relayed[:count] + jnp.where(apart == 0, own[:count], one[there, :] + two[there, :])
         message[count:] = relayed[count:]
 
 
@@ -296,22 +296,21 @@
     odd_a = precondition("odd_a", (after(raw, squares), *raw_came), tables, chips * ROWS)
 
     odd_b_came = [after(x, odd_a) for x in odd_b_came]
-    parts = both_scores("odd", True, turned_ours, far_rows, (odd_a, odd_b, *odd_b_came), swap)
+    parts = both_scores("odd", True, turned_ours, far_rows, (odd_a, odd_b, *odd_b_came, ours), swap)
     out = pltpu.VMEM((chips * count + 8, rows), f32)
-    scratch = [pltpu.VMEM((count * chips, rows), f32)]
-    ins = [near(x) for x in (squares, *parts)]
-    message = call(functools.partial(odd_body, chips), "odd", out, ins, scratch, us=0.1)
+    outs = [out, pltpu.VMEM((count * (chips + 1), rows), f32)]
+    message, begun = call(functools.partial(odd_body, chips), "odd", outs, [near(x) for x in (squares, *parts)], us=0.1)
     got = lax.ppermute(message, "dim", [(z, z ^ 1) for z in range(dims)])
 
     even_came = [after(x, message) for x in even_came]
-    parts = both_scores("even", False, turned_ours, far_rows, (ours, *even_came), swap)
+    parts = both_scores("even", False, turned_ours, far_rows, even_came, swap)
 
     partners = [lambda z, k=k: lax.bitwise_xor(z, k) for k in range(0, dims, 2)]
     outs = [pltpu.VMEM((count + 8, rows), f32)] * (dims // 2)
     body = functools.partial(relay_body, count, partners)
     relayed = call(body, "relay", outs, [near(x) for x in (squares, got)], us=100.0)
     body = functools.partial(send_body, chips, partners)
-    messages = call(body, "send", outs, [near(x) for x in (*parts, *relayed)], us=0.2)
+    messages = call(body, "send", outs, [near(x) for x in (begun, *parts, *relayed)], us=0.2)
     sums = [messages[0]]
     for k in range(2, dims, 2):
         sums.append(lax.ppermute(messages[k // 2], "dim", [(z, z ^ k) for z in range(dims)]))

time: 25 us -> 24.9 us (level)
  no operation moved by 1% of the time
where the time goes in v6:
time: 24.9 us; the launch traced here: 24.8 us
  starting transfers between devices  10.4 us (42%)
  Pallas kernels  8.73 us (35%)
  waiting for transfers between devices  5.47 us (22%)
    pallas_call x15, Pallas kernels, call(): pl.pallas_call(body, out_shape=outs, in_specs=specs or [WHOLE] * len(ins)...  8.73 us
    ppermute x3, starting transfers between devices, hop(): lax.ppermute(x, 'ex', [(e, (e + 2 * step) % exs) for e in range(exs)])  5.07 us
    ppermute x1, starting transfers between devices, local(): lax.ppermute(messages[k // 2], 'dim', [(z, z ^ k) for z in range(dims)])  2.9 us
    ppermute x1, waiting for transfers between devices, local(): lax.ppermute(messages[k // 2], 'dim', [(z, z ^ k) for z in range(dims)])  2.06 us
    ppermute x1, starting transfers between devices, local(): got = lax.ppermute(message, 'dim', [(z, z ^ 1) for z in range(dims)])  1.64 us
    ppermute x4, waiting for transfers between devices, swap(): return lax.ppermute(x, 'ex', across)  1.54 us
    ppermute x3, waiting for transfers between devices, hop(): lax.ppermute(x, 'ex', [(e, (e + 2 * step) % exs) for e in range(exs)])  1.49 us
    ppermute x4, starting transfers between devices, swap(): return lax.ppermute(x, 'ex', across)  0.83 us
  transfers between devices with their start and end apart: 9, of which 6 were waited for; matrix products, arithmetic and copies ran while one was open for 0% of the time, Pallas kernels for 32%

profile of v6, /device:TPU:0, one launch (start us, length us, event | category | flops | bytes accessed | tf_op | source)
XLA Modules:
  0.0 24.8 jit_solution(5431619454768354998)
XLA Ops:
  0.0 0.5 %collective-permute-start = (bf16[32,8192]{1,0:T(8,128)(2,1)}, bf16[32,8192]{1,0:T(8,128)(2,1)S(1)}, u32[]{:S(2)}, u32[]{:S(2)}) collective-permute-start(bf16[32,8192]{1,0:T(8,128)(2,1)} %refs_4_.1), channel_id=1, source_target_pairs={{0,1},{1,0},{2,3},{3,2},{4,5},{5,4},{6,7},{7,6},{8,9},{9,8},{10,11... | collective-permute-start | bytes 1572872 | tf_op jit(solution)/shard_map/ppermute | solution.py:277
  0.5 1.2 %factors.1 = (bf16[64,256]{1,0:T(8,128)(2,1)S(1)}, bf16[64,256]{1,0:T(8,128)(2,1)S(1)}, bf16[256,128]{1,0:T(8,128)(2,1)S(1)}, bf16[256,256]{1,0:T(8,128)(2,1)S(1...) custom-call(f32[2,64,64]{2,1,0:T(8,128)} %refs_0_.1, f32[2,64,64]{2,1,0:T(8,128)} %refs_1_.1, f32[2,64]{1,0:T(2,128)} %refs_2_.1, ...), custom_call_target="tpu_custom_call" | custom-call | flops 27600000 | tf_op jit(solution)/shard_map/factors/pallas_call | solution.py:40
  1.6 0.6 %collective-permute-done.other.refs_1_ = bf16[32,8192]{1,0:T(8,128)(2,1)S(1)} collective-permute-done((bf16[32,8192]{1,0:T(8,128)(2,1)}, bf16[32,8192]{1,0:T(8,128)(2,1)S(1)}, u32[]{:S(2)}, u32[]{:S(2)}) %collective-permute-start) | collective-permute-done | bytes 524320 | tf_op jit(solution)/shard_map/ppermute | solution.py:277
  2.2 0.0 copy-start
  2.2 2.9 %collective-permute-start.2 = (bf16[16,4096]{1,0:T(8,128)(2,1)S(1)}, bf16[16,4096]{1,0:T(8,128)(2,1)S(1)}, u32[]{:S(2)}, u32[]{:S(2)}) collective-permute-start(bf16[16,4096]{1,0:T(8,128)(2,1)S(1)} %pick.1.refs_0_), channel_id=1, source_target_pairs={{0,2},{1,3},{2,0},{3,1},{4,6},{5,7},{6,4},{7,5},{8,10},{9,11},{10,... | collective-permute-start | bytes 393224 | tf_op jit(solution)/shard_map/ppermute | solution.py:280
  5.1 1.0 %odd_b.1._.refs_1_ = bf16[16,4096]{1,0:T(8,128)(2,1)S(1)} custom-call(bf16[32,8192]{1,0:T(8,128)(2,1)S(1)} %get-tuple-element.37.own.refs_0_, bf16[32,8192]{1,0:T(8,128)(2,1)S(1)} %collective-permute-done.other.refs_1_, bf16[64,256]{1,0:T(8,128)(2,1)S(1)} %get-tuple-element.30.refs_2_, bf16[64,256]{1,0:T(8,128)(2,1)S(1)} %get-tuple-element.31.refs_3_, ...), custom_call_target="tpu_custom_call" | custom-call | flops 23000000 | tf_op jit(solution)/shard_map/odd_b/pallas_call | solution.py:40
  6.1 0.1 collective-permute-start.3
  6.2 0.0 copy-done
  6.2 0.8 %theirs.1 = (bf16[4096,256]{1,0:T(8,128)(2,1)S(1)}, bf16[256,4096]{1,0:T(8,128)(2,1)S(1)}, f32[8,256]{1,0:T(8,128)S(1)}) custom-call(bf16[256,8192]{1,0:T(8,128)(2,1)S(1)} %copy-done, bf16[16,4096]{1,0:T(8,128)(2,1)S(1)} %odd_b.1._.refs_1_), custom_call_target="tpu_custom_call" | custom-call | flops 16100000 | tf_op jit(solution)/shard_map/theirs/pallas_call | solution.py:40
  7.0 0.1 collective-permute-start.1
  7.1 1.3 %even.1.refs_3_ = bf16[32,4096]{1,0:T(8,128)(2,1)S(1)} custom-call(bf16[32,8192]{1,0:T(8,128)(2,1)S(1)} %get-tuple-element.37.own.refs_0_, bf16[32,8192]{1,0:T(8,128)(2,1)S(1)} %collective-permute-done.other.refs_1_, bf16[64,256]{1,0:T(8,128)(2,1)S(1)} %get-tuple-element.30.refs_2_, bf16[64,256]{1,0:T(8,128)(2,1)S(1)} %get-tuple-element.31.refs_3_, ...), custom_call_target="tpu_custom_call" | custom-call | flops 23000000512 | tf_op jit(solution)/shard_map/even/pallas_call | solution.py:40
  8.4 2.1 %collective-permute-start.5 = (bf16[32,4096]{1,0:T(8,128)(2,1)S(1)}, bf16[32,4096]{1,0:T(8,128)(2,1)S(1)}, u32[]{:S(2)}, u32[]{:S(2)}) collective-permute-start(bf16[32,4096]{1,0:T(8,128)(2,1)S(1)} %even.1.refs_3_), channel_id=1, source_target_pairs={{0,2},{1,3},{2,0},{3,1},{4,6},{5,7},{6,4},{7,5},{8,10},{9,11},{10,... | collective-permute-start | bytes 786440 | tf_op jit(solution)/shard_map/ppermute | solution.py:280
  10.5 0.6 %ours.1 = (bf16[4096,256]{1,0:T(8,128)(2,1)S(1)}, f32[8,256]{1,0:T(8,128)S(1)}) custom-call(bf16[256,4096]{1,0:T(8,128)(2,1)S(1)} %get-tuple-element.38.rest, f32[8,256]{1,0:T(8,128)S(1)} %get-tuple-element.36.before), custom_call_target="tpu_custom_call" | custom-call | flops 13800000 | tf_op jit(solution)/shard_map/ours/pallas_call | solution.py:40
  11.1 0.0 collective-permute-done.2.refs_1_
  11.1 1.3 %odd_a.1.refs_0_ = bf16[32,4096]{1,0:T(8,128)(2,1)S(1)} custom-call(bf16[16,4096]{1,0:T(8,128)(2,1)S(1)} %pick.1.refs_0_, bf16[16,4096]{1,0:T(8,128)(2,1)S(1)} %collective-permute-done.2.refs_1_, bf16[64,256]{1,0:T(8,128)(2,1)S(1)} %get-tuple-element.30.refs_2_, bf16[64,256]{1,0:T(8,128)(2,1)S(1)} %get-tuple-element.31.refs_3_, ...), custom_call_target="tpu_custom_call" | custom-call | flops 23000000 | tf_op jit(solution)/shard_map/odd_a/pallas_call | solution.py:40
  12.4 0.0 collective-permute-done.3.refs_2_
  12.4 0.0 collective-permute-done.1.turned
  12.4 0.5 %odd_far.1 = f32[96,256]{1,0:T(8,128)S(1)} custom-call(bf16[4096,256]{1,0:T(8,128)(2,1)S(1)} %collective-permute-done.1.turned, bf16[32,4096]{1,0:T(8,128)(2,1)S(1)} %odd_a.1.refs_0_, bf16[16,4096]{1,0:T(8,128)(2,1)S(1)} %odd_b.1._.refs_1_, bf16[16,4096]{1,0:T(8,128)(2,1)S(1)} %collective-permute-done.3.refs_2_, bf16[32,4096]{1,0:T(8,128)(2,1)S(1)} %even.1.refs_3_), custom_call_target="tpu_custom_call" | custom-call | flops 11500000 | tf_op jit(solution)/shard_map/odd_far/pallas_call | solution.py:40
  12.9 0.3 %collective-permute-start.4 = (f32[96,256]{1,0:T(8,128)S(1)}, f32[96,256]{1,0:T(8,128)S(1)}, u32[]{:S(2)}, u32[]{:S(2)}) collective-permute-start(f32[96,256]{1,0:T(8,128)S(1)} %odd_far.1), channel_id=1, source_target_pairs={{0,1},{1,0},{2,3},{3,2},{4,5},{5,4},{6,7},{7,6},{8,9},{9,8},{10,11... | collective-permute-start | bytes 294920 | tf_op jit(solution)/shard_map/ppermute | solution.py:277
  13.2 0.5 %odd_near.1.two = f32[96,256]{1,0:T(8,128)S(1)} custom-call(bf16[4096,256]{1,0:T(8,128)(2,1)S(1)} %get-tuple-element.43.turned, bf16[32,4096]{1,0:T(8,128)(2,1)S(1)} %odd_a.1.refs_0_, bf16[16,4096]{1,0:T(8,128)(2,1)S(1)} %odd_b.1._.refs_1_, bf16[16,4096]{1,0:T(8,128)(2,1)S(1)} %collective-permute-done.3.refs_2_, bf16[32,4096]{1,0:T(8,128)(2,1)S(1)} %even.1.refs_3_), custom_call_target="tpu_custom_call" | custom-call | flops 11500000 | tf_op jit(solution)/shard_map/odd_near/pallas_call | solution.py:40
  13.7 0.6 %collective-permute-done.4.one = f32[96,256]{1,0:T(8,128)S(1)} collective-permute-done((f32[96,256]{1,0:T(8,128)S(1)}, f32[96,256]{1,0:T(8,128)S(1)}, u32[]{:S(2)}, u32[]{:S(2)}) %collective-permute-start.4) | collective-permute-done | bytes 98336 | tf_op jit(solution)/shard_map/ppermute | solution.py:277
  14.3 1.6 %collective-permute-start.7 = (f32[72,256]{1,0:T(8,128)S(1)}, f32[72,256]{1,0:T(8,128)S(1)}, u32[]{:S(2)}, u32[]{:S(2)}) collective-permute-start(f32[72,256]{1,0:T(8,128)S(1)} %get-tuple-element.45), channel_id=1, source_target_pairs={{0,4},{4,0},{8,12},{12,8},{1,5},{5,1},{9,13},{13,9},{2,6},{6,2},{1... | collective-permute-start | bytes 221192 | tf_op jit(solution)/shard_map/ppermute | solution.py:303
  15.9 1.5 %collective-permute-done.5.refs_0_ = bf16[32,4096]{1,0:T(8,128)(2,1)S(1)} collective-permute-done((bf16[32,4096]{1,0:T(8,128)(2,1)S(1)}, bf16[32,4096]{1,0:T(8,128)(2,1)S(1)}, u32[]{:S(2)}, u32[]{:S(2)}) %collective-permute-start.5) | collective-permute-done | bytes 262176 | tf_op jit(solution)/shard_map/ppermute | solution.py:280
  17.4 0.5 %even_far.1 = f32[32,256]{1,0:T(8,128)S(1)} custom-call(bf16[4096,256]{1,0:T(8,128)(2,1)S(1)} %collective-permute-done.1.turned, bf16[32,4096]{1,0:T(8,128)(2,1)S(1)} %collective-permute-done.5.refs_0_), custom_call_target="tpu_custom_call" | custom-call | flops 11500000 | tf_op jit(solution)/shard_map/even_far/pallas_call | solution.py:40
  17.9 0.0 collective-permute-start.6
  17.9 0.5 %even_near.1.two = f32[32,256]{1,0:T(8,128)S(1)} custom-call(bf16[4096,256]{1,0:T(8,128)(2,1)S(1)} %get-tuple-element.43.turned, bf16[32,4096]{1,0:T(8,128)(2,1)S(1)} %collective-permute-done.5.refs_0_), custom_call_target="tpu_custom_call" | custom-call | flops 11500000 | tf_op jit(solution)/shard_map/even_near/pallas_call | solution.py:40
  18.4 0.4 %collective-permute-done.7.got = f32[72,256]{1,0:T(8,128)S(1)} collective-permute-done((f32[72,256]{1,0:T(8,128)S(1)}, f32[72,256]{1,0:T(8,128)S(1)}, u32[]{:S(2)}, u32[]{:S(2)}) %collective-permute-start.7) | collective-permute-done | bytes 73760 | tf_op jit(solution)/shard_map/ppermute | solution.py:303
  18.8 0.3 %collective-permute-done.6.one = f32[32,256]{1,0:T(8,128)S(1)} collective-permute-done((f32[32,256]{1,0:T(8,128)S(1)}, f32[32,256]{1,0:T(8,128)S(1)}, u32[]{:S(2)}, u32[]{:S(2)}) %collective-permute-start.6) | collective-permute-done | bytes 32800 | tf_op jit(solution)/shard_map/ppermute | solution.py:277
  19.1 2.9 %collective-permute-start.8 = (f32[40,256]{1,0:T(8,128)S(1)}, f32[40,256]{1,0:T(8,128)S(1)}, u32[]{:S(2)}, u32[]{:S(2)}) collective-permute-start(f32[40,256]{1,0:T(8,128)S(1)} %get-tuple-element.50), channel_id=1, source_target_pairs={{0,8},{4,12},{8,0},{12,4},{1,9},{5,13},{9,1},{13,5},{2,10},{6,14},... | collective-permute-start | bytes 122888 | tf_op jit(solution)/shard_map/ppermute | solution.py:316
  22.0 2.1 %collective-permute-done.8.refs_1_ = f32[40,256]{1,0:T(8,128)S(1)} collective-permute-done((f32[40,256]{1,0:T(8,128)S(1)}, f32[40,256]{1,0:T(8,128)S(1)}, u32[]{:S(2)}, u32[]{:S(2)}) %collective-permute-start.8) | collective-permute-done | bytes 40992 | tf_op jit(solution)/shard_map/ppermute | solution.py:316
  24.1 0.6 %finish.1 = f32[32,256]{1,0:T(8,128)} custom-call(f32[40,256]{1,0:T(8,128)S(1)} %get-tuple-element.49.refs_0_, f32[40,256]{1,0:T(8,128)S(1)} %collective-permute-done.8.refs_1_), custom_call_target="tpu_custom_call" | custom-call | flops 13800000 | tf_op jit(solution)/shard_map/finish/pallas_call | solution.py:40
  (4 shorter events, 0.1 us)
Async XLA Ops:
  0.0 2.2 %collective-permute-start = (bf16[32,8192]{1,0:T(8,128)(2,1)}, bf16[32,8192]{1,0:T(8,128)(2,1)S(1)}, u32[]{:S(2)}, u32[]{:S(2)}) collective-permute-start(bf16[32,8192]{1,0:T(8,128)(2,1)} %refs_4_.1), channel_id=1, source_target_pairs={{0,1},{1,0},{2,3},{3,2},{4,5},{5,4},{6,7},{7,6},{8,9},{9,8},{10,11... | collective-permute-start | bytes 1572872 | tf_op jit(solution)/shard_map/ppermute | solution.py:277
  2.2 4.0 %copy-start = (bf16[256,8192]{1,0:T(8,128)(2,1)S(1)}, bf16[256,8192]{1,0:T(8,128)(2,1)}, u32[]{:S(2)}) copy-start(bf16[256,8192]{1,0:T(8,128)(2,1)} %store.1) | copy-start | bytes 12582916
  2.2 8.9 %collective-permute-start.2 = (bf16[16,4096]{1,0:T(8,128)(2,1)S(1)}, bf16[16,4096]{1,0:T(8,128)(2,1)S(1)}, u32[]{:S(2)}, u32[]{:S(2)}) collective-permute-start(bf16[16,4096]{1,0:T(8,128)(2,1)S(1)} %pick.1.refs_0_), channel_id=1, source_target_pairs={{0,2},{1,3},{2,0},{3,1},{4,6},{5,7},{6,4},{7,5},{8,10},{9,11},{10,... | collective-permute-start | bytes 393224 | tf_op jit(solution)/shard_map/ppermute | solution.py:280
  6.1 6.3 %collective-permute-start.3 = (bf16[16,4096]{1,0:T(8,128)(2,1)S(1)}, bf16[16,4096]{1,0:T(8,128)(2,1)S(1)}, u32[]{:S(2)}, u32[]{:S(2)}) collective-permute-start(bf16[16,4096]{1,0:T(8,128)(2,1)S(1)} %odd_b.1._.refs_1_), channel_id=1, source_target_pairs={{0,2},{1,3},{2,0},{3,1},{4,6},{5,7},{6,4},{7,5},{8,10},{9,11},{10,... | collective-permute-start | bytes 393224 | tf_op jit(solution)/shard_map/ppermute | solution.py:280
  7.0 5.4 %collective-permute-start.1 = (bf16[4096,256]{1,0:T(8,128)(2,1)S(1)}, bf16[4096,256]{1,0:T(8,128)(2,1)S(1)}, u32[]{:S(2)}, u32[]{:S(2)}) collective-permute-start(bf16[4096,256]{1,0:T(8,128)(2,1)S(1)} %get-tuple-element.40), channel_id=1, source_target_pairs={{0,1},{1,0},{2,3},{3,2},{4,5},{5,4},{6,7},{7,6},{8,9},{9,8},{10,11... | collective-permute-start | bytes 6291464 | tf_op jit(solution)/shard_map/ppermute | solution.py:277
  8.4 9.0 %collective-permute-start.5 = (bf16[32,4096]{1,0:T(8,128)(2,1)S(1)}, bf16[32,4096]{1,0:T(8,128)(2,1)S(1)}, u32[]{:S(2)}, u32[]{:S(2)}) collective-permute-start(bf16[32,4096]{1,0:T(8,128)(2,1)S(1)} %even.1.refs_3_), channel_id=1, source_target_pairs={{0,2},{1,3},{2,0},{3,1},{4,6},{5,7},{6,4},{7,5},{8,10},{9,11},{10,... | collective-permute-start | bytes 786440 | tf_op jit(solution)/shard_map/ppermute | solution.py:280
  12.9 1.4 %collective-permute-start.4 = (f32[96,256]{1,0:T(8,128)S(1)}, f32[96,256]{1,0:T(8,128)S(1)}, u32[]{:S(2)}, u32[]{:S(2)}) collective-permute-start(f32[96,256]{1,0:T(8,128)S(1)} %odd_far.1), channel_id=1, source_target_pairs={{0,1},{1,0},{2,3},{3,2},{4,5},{5,4},{6,7},{7,6},{8,9},{9,8},{10,11... | collective-permute-start | bytes 294920 | tf_op jit(solution)/shard_map/ppermute | solution.py:277
  14.3 4.5 %collective-permute-start.7 = (f32[72,256]{1,0:T(8,128)S(1)}, f32[72,256]{1,0:T(8,128)S(1)}, u32[]{:S(2)}, u32[]{:S(2)}) collective-permute-start(f32[72,256]{1,0:T(8,128)S(1)} %get-tuple-element.45), channel_id=1, source_target_pairs={{0,4},{4,0},{8,12},{12,8},{1,5},{5,1},{9,13},{13,9},{2,6},{6,2},{1... | collective-permute-start | bytes 221192 | tf_op jit(solution)/shard_map/ppermute | solution.py:303
  17.9 1.2 %collective-permute-start.6 = (f32[32,256]{1,0:T(8,128)S(1)}, f32[32,256]{1,0:T(8,128)S(1)}, u32[]{:S(2)}, u32[]{:S(2)}) collective-permute-start(f32[32,256]{1,0:T(8,128)S(1)} %even_far.1), channel_id=1, source_target_pairs={{0,1},{1,0},{2,3},{3,2},{4,5},{5,4},{6,7},{7,6},{8,9},{9,8},{10,11... | collective-permute-start | bytes 98312 | tf_op jit(solution)/shard_map/ppermute | solution.py:277
  19.1 5.0 %collective-permute-start.8 = (f32[40,256]{1,0:T(8,128)S(1)}, f32[40,256]{1,0:T(8,128)S(1)}, u32[]{:S(2)}, u32[]{:S(2)}) collective-permute-start(f32[40,256]{1,0:T(8,128)S(1)} %get-tuple-element.50), channel_id=1, source_target_pairs={{0,8},{4,12},{8,0},{12,4},{1,9},{5,13},{9,1},{13,5},{2,10},{6,14},... | collective-permute-start | bytes 122888 | tf_op jit(solution)/shard_map/ppermute | solution.py:316

commit v7 on v6

--- a/solution.py
+++ b/solution.py
@@ -252,8 +252,15 @@
     for relayed, message, partner in zip(refs[: len(partners)], refs[len(partners) :], partners):
         apart = lax.rem(x - partner(dim) // 2 + chips, chips)
         there = pl.ds(pl.multiple_of(jnp.maximum(apart - 1, 0) * count, count), count)
-        message[:count] = relayed[:count] + jnp.where(apart == 0, own[:count], one[there, :] + two[there, :])
-        message[count:] = relayed[count:]
+        value = relayed[:count] + jnp.where(apart == 0, own[:count], one[there, :] + two[there, :])
+        squares = jnp.sum(relayed[count:], axis=0, keepdims=True)
+        row = lax.broadcasted_iota(jnp.int32, (8, LANES), 0)
+        last = jnp.zeros((8, LANES), f32)
+        for k in range(value.shape[1] // LANES):
+            part = slice(k * LANES, (k + 1) * LANES)
+            message[k * count : (k + 1) * count] = value[:, part]
+            last = jnp.where(row == k, squares[:, part], last)
+        message[message.shape[0] - 8 :] = last
 
 
 def finish_body(*refs):
@@ -261,8 +268,11 @@
     total = refs[0][...]
     for r in refs[1:-3]:
         total = total + r[...]
-    count = out.shape[0]
-    here[...] = total[:count] / jnp.sqrt(jnp.sum(total[count:], axis=0, keepdims=True) + 1e-06)
+    count, rows = out.shape
+    squares = total[rows // LANES * count :]
+    for k in range(rows // LANES):
+        part = total[k * count : (k + 1) * count] / jnp.sqrt(squares[k : k + 1] + 1e-06)
+        here[:, k * LANES : (k + 1) * LANES] = part
     copy = pltpu.make_async_copy(here, out, sem)
     copy.start()
     copy.wait()
@@ -310,6 +320,7 @@
     body = functools.partial(relay_body, count, partners)
     relayed = call(body, "relay", outs, [near(x) for x in (squares, got)], us=100.0)
     body = functools.partial(send_body, chips, partners)
+    outs = [pltpu.VMEM((rows // LANES * count + 8, LANES), f32)] * (dims // 2)
     messages = call(body, "send", outs, [near(x) for x in (begun, *parts, *relayed)], us=0.2)
     sums = [messages[0]]
     for k in range(2, dims, 2):

time: 24.9 us -> 24.9 us (level)
  transfers between devices with their start and end apart: 9 -> 9, of which waited for: 6 -> 6; matrix products, arithmetic and copies ran while one was open for 0% -> 0% of each run, Pallas kernels for 32% -> 33%
where the time goes in v7:
time: 24.9 us; the launch traced here: 24.7 us
  starting transfers between devices  10.4 us (42%)
  Pallas kernels  8.73 us (35%)
  waiting for transfers between devices  5.43 us (22%)
    pallas_call x15, Pallas kernels, call(): pl.pallas_call(body, out_shape=outs, in_specs=specs or [WHOLE] * len(ins)...  8.73 us
    ppermute x3, starting transfers between devices, hop(): lax.ppermute(x, 'ex', [(e, (e + 2 * step) % exs) for e in range(exs)])  5.07 us
    ppermute x1, starting transfers between devices, local(): lax.ppermute(messages[k // 2], 'dim', [(z, z ^ k) for z in range(dims)])  2.9 us
    ppermute x1, waiting for transfers between devices, local(): lax.ppermute(messages[k // 2], 'dim', [(z, z ^ k) for z in range(dims)])  2.02 us
    ppermute x1, starting transfers between devices, local(): got = lax.ppermute(message, 'dim', [(z, z ^ 1) for z in range(dims)])  1.64 us
    ppermute x4, waiting for transfers between devices, swap(): return lax.ppermute(x, 'ex', across)  1.54 us
    ppermute x3, waiting for transfers between devices, hop(): lax.ppermute(x, 'ex', [(e, (e + 2 * step) % exs) for e in range(exs)])  1.49 us
    ppermute x4, starting transfers between devices, swap(): return lax.ppermute(x, 'ex', across)  0.83 us
  transfers between devices with their start and end apart: 9, of which 6 were waited for; matrix products, arithmetic and copies ran while one was open for 0% of the time, Pallas kernels for 33%

profile of v7, /device:TPU:0, one launch (start us, length us, event | category | flops | bytes accessed | tf_op | source)
XLA Modules:
  0.0 24.7 jit_solution(1784599274756849564)
XLA Ops:
  0.0 0.5 %collective-permute-start = (bf16[32,8192]{1,0:T(8,128)(2,1)}, bf16[32,8192]{1,0:T(8,128)(2,1)S(1)}, u32[]{:S(2)}, u32[]{:S(2)}) collective-permute-start(bf16[32,8192]{1,0:T(8,128)(2,1)} %refs_4_.1), channel_id=1, source_target_pairs={{0,1},{1,0},{2,3},{3,2},{4,5},{5,4},{6,7},{7,6},{8,9},{9,8},{10,11... | collective-permute-start | bytes 1572872 | tf_op jit(solution)/shard_map/ppermute | solution.py:287
  0.5 1.2 %factors.1 = (bf16[64,256]{1,0:T(8,128)(2,1)S(1)}, bf16[64,256]{1,0:T(8,128)(2,1)S(1)}, bf16[256,128]{1,0:T(8,128)(2,1)S(1)}, bf16[256,256]{1,0:T(8,128)(2,1)S(1...) custom-call(f32[2,64,64]{2,1,0:T(8,128)} %refs_0_.1, f32[2,64,64]{2,1,0:T(8,128)} %refs_1_.1, f32[2,64]{1,0:T(2,128)} %refs_2_.1, ...), custom_call_target="tpu_custom_call" | custom-call | flops 27600000 | tf_op jit(solution)/shard_map/factors/pallas_call | solution.py:40
  1.6 0.6 %collective-permute-done.other.refs_1_ = bf16[32,8192]{1,0:T(8,128)(2,1)S(1)} collective-permute-done((bf16[32,8192]{1,0:T(8,128)(2,1)}, bf16[32,8192]{1,0:T(8,128)(2,1)S(1)}, u32[]{:S(2)}, u32[]{:S(2)}) %collective-permute-start) | collective-permute-done | bytes 524320 | tf_op jit(solution)/shard_map/ppermute | solution.py:287
  2.2 0.0 copy-start
  2.2 2.9 %collective-permute-start.2 = (bf16[16,4096]{1,0:T(8,128)(2,1)S(1)}, bf16[16,4096]{1,0:T(8,128)(2,1)S(1)}, u32[]{:S(2)}, u32[]{:S(2)}) collective-permute-start(bf16[16,4096]{1,0:T(8,128)(2,1)S(1)} %pick.1.refs_0_), channel_id=1, source_target_pairs={{0,2},{1,3},{2,0},{3,1},{4,6},{5,7},{6,4},{7,5},{8,10},{9,11},{10,... | collective-permute-start | bytes 393224 | tf_op jit(solution)/shard_map/ppermute | solution.py:290
  5.1 1.0 %odd_b.1._.refs_1_ = bf16[16,4096]{1,0:T(8,128)(2,1)S(1)} custom-call(bf16[32,8192]{1,0:T(8,128)(2,1)S(1)} %get-tuple-element.37.own.refs_0_, bf16[32,8192]{1,0:T(8,128)(2,1)S(1)} %collective-permute-done.other.refs_1_, bf16[64,256]{1,0:T(8,128)(2,1)S(1)} %get-tuple-element.30.refs_2_, bf16[64,256]{1,0:T(8,128)(2,1)S(1)} %get-tuple-element.31.refs_3_, ...), custom_call_target="tpu_custom_call" | custom-call | flops 23000000 | tf_op jit(solution)/shard_map/odd_b/pallas_call | solution.py:40
  6.1 0.1 collective-permute-start.3
  6.2 0.0 copy-done
  6.2 0.8 %theirs.1 = (bf16[4096,256]{1,0:T(8,128)(2,1)S(1)}, bf16[256,4096]{1,0:T(8,128)(2,1)S(1)}, f32[8,256]{1,0:T(8,128)S(1)}) custom-call(bf16[256,8192]{1,0:T(8,128)(2,1)S(1)} %copy-done, bf16[16,4096]{1,0:T(8,128)(2,1)S(1)} %odd_b.1._.refs_1_), custom_call_target="tpu_custom_call" | custom-call | flops 16100000 | tf_op jit(solution)/shard_map/theirs/pallas_call | solution.py:40
  7.0 0.1 collective-permute-start.1
  7.1 1.3 %even.1.refs_3_ = bf16[32,4096]{1,0:T(8,128)(2,1)S(1)} custom-call(bf16[32,8192]{1,0:T(8,128)(2,1)S(1)} %get-tuple-element.37.own.refs_0_, bf16[32,8192]{1,0:T(8,128)(2,1)S(1)} %collective-permute-done.other.refs_1_, bf16[64,256]{1,0:T(8,128)(2,1)S(1)} %get-tuple-element.30.refs_2_, bf16[64,256]{1,0:T(8,128)(2,1)S(1)} %get-tuple-element.31.refs_3_, ...), custom_call_target="tpu_custom_call" | custom-call | flops 23000000512 | tf_op jit(solution)/shard_map/even/pallas_call | solution.py:40
  8.4 2.1 %collective-permute-start.5 = (bf16[32,4096]{1,0:T(8,128)(2,1)S(1)}, bf16[32,4096]{1,0:T(8,128)(2,1)S(1)}, u32[]{:S(2)}, u32[]{:S(2)}) collective-permute-start(bf16[32,4096]{1,0:T(8,128)(2,1)S(1)} %even.1.refs_3_), channel_id=1, source_target_pairs={{0,2},{1,3},{2,0},{3,1},{4,6},{5,7},{6,4},{7,5},{8,10},{9,11},{10,... | collective-permute-start | bytes 786440 | tf_op jit(solution)/shard_map/ppermute | solution.py:290
  10.5 0.6 %ours.1 = (bf16[4096,256]{1,0:T(8,128)(2,1)S(1)}, f32[8,256]{1,0:T(8,128)S(1)}) custom-call(bf16[256,4096]{1,0:T(8,128)(2,1)S(1)} %get-tuple-element.38.rest, f32[8,256]{1,0:T(8,128)S(1)} %get-tuple-element.36.before), custom_call_target="tpu_custom_call" | custom-call | flops 13800000 | tf_op jit(solution)/shard_map/ours/pallas_call | solution.py:40
  11.1 0.0 collective-permute-done.2.refs_1_
  11.1 1.3 %odd_a.1.refs_0_ = bf16[32,4096]{1,0:T(8,128)(2,1)S(1)} custom-call(bf16[16,4096]{1,0:T(8,128)(2,1)S(1)} %pick.1.refs_0_, bf16[16,4096]{1,0:T(8,128)(2,1)S(1)} %collective-permute-done.2.refs_1_, bf16[64,256]{1,0:T(8,128)(2,1)S(1)} %get-tuple-element.30.refs_2_, bf16[64,256]{1,0:T(8,128)(2,1)S(1)} %get-tuple-element.31.refs_3_, ...), custom_call_target="tpu_custom_call" | custom-call | flops 23000000 | tf_op jit(solution)/shard_map/odd_a/pallas_call | solution.py:40
  12.4 0.0 collective-permute-done.3.refs_2_
  12.4 0.0 collective-permute-done.1.turned
  12.4 0.5 %odd_far.1 = f32[96,256]{1,0:T(8,128)S(1)} custom-call(bf16[4096,256]{1,0:T(8,128)(2,1)S(1)} %collective-permute-done.1.turned, bf16[32,4096]{1,0:T(8,128)(2,1)S(1)} %odd_a.1.refs_0_, bf16[16,4096]{1,0:T(8,128)(2,1)S(1)} %odd_b.1._.refs_1_, bf16[16,4096]{1,0:T(8,128)(2,1)S(1)} %collective-permute-done.3.refs_2_, bf16[32,4096]{1,0:T(8,128)(2,1)S(1)} %even.1.refs_3_), custom_call_target="tpu_custom_call" | custom-call | flops 11500000 | tf_op jit(solution)/shard_map/odd_far/pallas_call | solution.py:40
  12.9 0.3 %collective-permute-start.4 = (f32[96,256]{1,0:T(8,128)S(1)}, f32[96,256]{1,0:T(8,128)S(1)}, u32[]{:S(2)}, u32[]{:S(2)}) collective-permute-start(f32[96,256]{1,0:T(8,128)S(1)} %odd_far.1), channel_id=1, source_target_pairs={{0,1},{1,0},{2,3},{3,2},{4,5},{5,4},{6,7},{7,6},{8,9},{9,8},{10,11... | collective-permute-start | bytes 294920 | tf_op jit(solution)/shard_map/ppermute | solution.py:287
  13.2 0.5 %odd_near.1.two = f32[96,256]{1,0:T(8,128)S(1)} custom-call(bf16[4096,256]{1,0:T(8,128)(2,1)S(1)} %get-tuple-element.43.turned, bf16[32,4096]{1,0:T(8,128)(2,1)S(1)} %odd_a.1.refs_0_, bf16[16,4096]{1,0:T(8,128)(2,1)S(1)} %odd_b.1._.refs_1_, bf16[16,4096]{1,0:T(8,128)(2,1)S(1)} %collective-permute-done.3.refs_2_, bf16[32,4096]{1,0:T(8,128)(2,1)S(1)} %even.1.refs_3_), custom_call_target="tpu_custom_call" | custom-call | flops 11500000 | tf_op jit(solution)/shard_map/odd_near/pallas_call | solution.py:40
  13.7 0.6 %collective-permute-done.4.one = f32[96,256]{1,0:T(8,128)S(1)} collective-permute-done((f32[96,256]{1,0:T(8,128)S(1)}, f32[96,256]{1,0:T(8,128)S(1)}, u32[]{:S(2)}, u32[]{:S(2)}) %collective-permute-start.4) | collective-permute-done | bytes 98336 | tf_op jit(solution)/shard_map/ppermute | solution.py:287
  14.3 1.6 %collective-permute-start.7 = (f32[72,256]{1,0:T(8,128)S(1)}, f32[72,256]{1,0:T(8,128)S(1)}, u32[]{:S(2)}, u32[]{:S(2)}) collective-permute-start(f32[72,256]{1,0:T(8,128)S(1)} %get-tuple-element.45), channel_id=1, source_target_pairs={{0,4},{4,0},{8,12},{12,8},{1,5},{5,1},{9,13},{13,9},{2,6},{6,2},{1... | collective-permute-start | bytes 221192 | tf_op jit(solution)/shard_map/ppermute | solution.py:313
  15.9 1.5 %collective-permute-done.5.refs_0_ = bf16[32,4096]{1,0:T(8,128)(2,1)S(1)} collective-permute-done((bf16[32,4096]{1,0:T(8,128)(2,1)S(1)}, bf16[32,4096]{1,0:T(8,128)(2,1)S(1)}, u32[]{:S(2)}, u32[]{:S(2)}) %collective-permute-start.5) | collective-permute-done | bytes 262176 | tf_op jit(solution)/shard_map/ppermute | solution.py:290
  17.4 0.5 %even_far.1 = f32[32,256]{1,0:T(8,128)S(1)} custom-call(bf16[4096,256]{1,0:T(8,128)(2,1)S(1)} %collective-permute-done.1.turned, bf16[32,4096]{1,0:T(8,128)(2,1)S(1)} %collective-permute-done.5.refs_0_), custom_call_target="tpu_custom_call" | custom-call | flops 11500000 | tf_op jit(solution)/shard_map/even_far/pallas_call | solution.py:40
  17.9 0.0 collective-permute-start.6
  17.9 0.5 %even_near.1.two = f32[32,256]{1,0:T(8,128)S(1)} custom-call(bf16[4096,256]{1,0:T(8,128)(2,1)S(1)} %get-tuple-element.43.turned, bf16[32,4096]{1,0:T(8,128)(2,1)S(1)} %collective-permute-done.5.refs_0_), custom_call_target="tpu_custom_call" | custom-call | flops 11500000 | tf_op jit(solution)/shard_map/even_near/pallas_call | solution.py:40
  18.4 0.4 %collective-permute-done.7.got = f32[72,256]{1,0:T(8,128)S(1)} collective-permute-done((f32[72,256]{1,0:T(8,128)S(1)}, f32[72,256]{1,0:T(8,128)S(1)}, u32[]{:S(2)}, u32[]{:S(2)}) %collective-permute-start.7) | collective-permute-done | bytes 73760 | tf_op jit(solution)/shard_map/ppermute | solution.py:313
  18.8 0.3 %collective-permute-done.6.one = f32[32,256]{1,0:T(8,128)S(1)} collective-permute-done((f32[32,256]{1,0:T(8,128)S(1)}, f32[32,256]{1,0:T(8,128)S(1)}, u32[]{:S(2)}, u32[]{:S(2)}) %collective-permute-start.6) | collective-permute-done | bytes 32800 | tf_op jit(solution)/shard_map/ppermute | solution.py:287
  19.1 2.9 %collective-permute-start.8 = (f32[72,128]{1,0:T(8,128)S(1)}, f32[72,128]{1,0:T(8,128)S(1)}, u32[]{:S(2)}, u32[]{:S(2)}) collective-permute-start(f32[72,128]{1,0:T(8,128)S(1)} %get-tuple-element.50), channel_id=1, source_target_pairs={{0,8},{4,12},{8,0},{12,4},{1,9},{5,13},{9,1},{13,5},{2,10},{6,14},... | collective-permute-start | bytes 110600 | tf_op jit(solution)/shard_map/ppermute | solution.py:327
  22.1 2.0 %collective-permute-done.8.refs_1_ = f32[72,128]{1,0:T(8,128)S(1)} collective-permute-done((f32[72,128]{1,0:T(8,128)S(1)}, f32[72,128]{1,0:T(8,128)S(1)}, u32[]{:S(2)}, u32[]{:S(2)}) %collective-permute-start.8) | collective-permute-done | bytes 36896 | tf_op jit(solution)/shard_map/ppermute | solution.py:327
  24.1 0.6 %finish.1 = f32[32,256]{1,0:T(8,128)} custom-call(f32[72,128]{1,0:T(8,128)S(1)} %get-tuple-element.49.refs_0_, f32[72,128]{1,0:T(8,128)S(1)} %collective-permute-done.8.refs_1_), custom_call_target="tpu_custom_call" | custom-call | flops 13800000 | tf_op jit(solution)/shard_map/finish/pallas_call | solution.py:40
  (4 shorter events, 0.1 us)
Async XLA Ops:
  0.0 2.2 %collective-permute-start = (bf16[32,8192]{1,0:T(8,128)(2,1)}, bf16[32,8192]{1,0:T(8,128)(2,1)S(1)}, u32[]{:S(2)}, u32[]{:S(2)}) collective-permute-start(bf16[32,8192]{1,0:T(8,128)(2,1)} %refs_4_.1), channel_id=1, source_target_pairs={{0,1},{1,0},{2,3},{3,2},{4,5},{5,4},{6,7},{7,6},{8,9},{9,8},{10,11... | collective-permute-start | bytes 1572872 | tf_op jit(solution)/shard_map/ppermute | solution.py:287
  2.2 4.0 %copy-start = (bf16[256,8192]{1,0:T(8,128)(2,1)S(1)}, bf16[256,8192]{1,0:T(8,128)(2,1)}, u32[]{:S(2)}) copy-start(bf16[256,8192]{1,0:T(8,128)(2,1)} %store.1) | copy-start | bytes 12582916
  2.2 8.9 %collective-permute-start.2 = (bf16[16,4096]{1,0:T(8,128)(2,1)S(1)}, bf16[16,4096]{1,0:T(8,128)(2,1)S(1)}, u32[]{:S(2)}, u32[]{:S(2)}) collective-permute-start(bf16[16,4096]{1,0:T(8,128)(2,1)S(1)} %pick.1.refs_0_), channel_id=1, source_target_pairs={{0,2},{1,3},{2,0},{3,1},{4,6},{5,7},{6,4},{7,5},{8,10},{9,11},{10,... | collective-permute-start | bytes 393224 | tf_op jit(solution)/shard_map/ppermute | solution.py:290
  6.1 6.3 %collective-permute-start.3 = (bf16[16,4096]{1,0:T(8,128)(2,1)S(1)}, bf16[16,4096]{1,0:T(8,128)(2,1)S(1)}, u32[]{:S(2)}, u32[]{:S(2)}) collective-permute-start(bf16[16,4096]{1,0:T(8,128)(2,1)S(1)} %odd_b.1._.refs_1_), channel_id=1, source_target_pairs={{0,2},{1,3},{2,0},{3,1},{4,6},{5,7},{6,4},{7,5},{8,10},{9,11},{10,... | collective-permute-start | bytes 393224 | tf_op jit(solution)/shard_map/ppermute | solution.py:290
  7.0 5.4 %collective-permute-start.1 = (bf16[4096,256]{1,0:T(8,128)(2,1)S(1)}, bf16[4096,256]{1,0:T(8,128)(2,1)S(1)}, u32[]{:S(2)}, u32[]{:S(2)}) collective-permute-start(bf16[4096,256]{1,0:T(8,128)(2,1)S(1)} %get-tuple-element.40), channel_id=1, source_target_pairs={{0,1},{1,0},{2,3},{3,2},{4,5},{5,4},{6,7},{7,6},{8,9},{9,8},{10,11... | collective-permute-start | bytes 6291464 | tf_op jit(solution)/shard_map/ppermute | solution.py:287
  8.4 9.0 %collective-permute-start.5 = (bf16[32,4096]{1,0:T(8,128)(2,1)S(1)}, bf16[32,4096]{1,0:T(8,128)(2,1)S(1)}, u32[]{:S(2)}, u32[]{:S(2)}) collective-permute-start(bf16[32,4096]{1,0:T(8,128)(2,1)S(1)} %even.1.refs_3_), channel_id=1, source_target_pairs={{0,2},{1,3},{2,0},{3,1},{4,6},{5,7},{6,4},{7,5},{8,10},{9,11},{10,... | collective-permute-start | bytes 786440 | tf_op jit(solution)/shard_map/ppermute | solution.py:290
  12.9 1.4 %collective-permute-start.4 = (f32[96,256]{1,0:T(8,128)S(1)}, f32[96,256]{1,0:T(8,128)S(1)}, u32[]{:S(2)}, u32[]{:S(2)}) collective-permute-start(f32[96,256]{1,0:T(8,128)S(1)} %odd_far.1), channel_id=1, source_target_pairs={{0,1},{1,0},{2,3},{3,2},{4,5},{5,4},{6,7},{7,6},{8,9},{9,8},{10,11... | collective-permute-start | bytes 294920 | tf_op jit(solution)/shard_map/ppermute | solution.py:287
  14.3 4.5 %collective-permute-start.7 = (f32[72,256]{1,0:T(8,128)S(1)}, f32[72,256]{1,0:T(8,128)S(1)}, u32[]{:S(2)}, u32[]{:S(2)}) collective-permute-start(f32[72,256]{1,0:T(8,128)S(1)} %get-tuple-element.45), channel_id=1, source_target_pairs={{0,4},{4,0},{8,12},{12,8},{1,5},{5,1},{9,13},{13,9},{2,6},{6,2},{1... | collective-permute-start | bytes 221192 | tf_op jit(solution)/shard_map/ppermute | solution.py:313
  17.9 1.2 %collective-permute-start.6 = (f32[32,256]{1,0:T(8,128)S(1)}, f32[32,256]{1,0:T(8,128)S(1)}, u32[]{:S(2)}, u32[]{:S(2)}) collective-permute-start(f32[32,256]{1,0:T(8,128)S(1)} %even_far.1), channel_id=1, source_target_pairs={{0,1},{1,0},{2,3},{3,2},{4,5},{5,4},{6,7},{7,6},{8,9},{9,8},{10,11... | collective-permute-start | bytes 98312 | tf_op jit(solution)/shard_map/ppermute | solution.py:287
  19.1 4.9 %collective-permute-start.8 = (f32[72,128]{1,0:T(8,128)S(1)}, f32[72,128]{1,0:T(8,128)S(1)}, u32[]{:S(2)}, u32[]{:S(2)}) collective-permute-start(f32[72,128]{1,0:T(8,128)S(1)} %get-tuple-element.50), channel_id=1, source_target_pairs={{0,8},{4,12},{8,0},{12,4},{1,9},{5,13},{9,1},{13,5},{2,10},{6,14},... | collective-permute-start | bytes 110600 | tf_op jit(solution)/shard_map/ppermute | solution.py:327

commit v8 on v7

--- a/solution.py
+++ b/solution.py
@@ -95,7 +95,7 @@
     left, right, val_left, val_right, sems = refs[6:]
     layer = position()[1]
     copies = []
-    for k, (g, h) in enumerate(zip(given, [left, right, val_left, val_right, own])):
+    for k, (g, h) in enumerate(zip(given, [left.at[:SIDE], right, val_left, val_right, own])):
         copies.append(pltpu.make_async_copy(g.at[layer] if k < 2 else g, h, sems.at[k]))
     for copy in copies:
         copy.start()
@@ -119,7 +119,8 @@
 def factors(queries, left, right, val_left, val_right):
     shapes = [((64, 256), bf16)] * 2 + [((256, 128), bf16), ((256, 256), bf16), ((64, 128), f32), (queries.shape, bf16)]
     given = (left, right, val_left, val_right, queries)
-    scratch = [pltpu.VMEM(x.shape[1:] if x.ndim == 3 else x.shape, f32) for x in given[:4]]
+    shapes_in = [(SIDE + PAD, SIDE), (SIDE, SIDE), val_left.shape, val_right.shape]
+    scratch = [pltpu.VMEM(shape, f32) for shape in shapes_in]
     scratch.append(pltpu.SemaphoreType.DMA((5,)))
     *tables, own = call(
         factors_body,
@@ -185,7 +186,7 @@
         name,
         pltpu.VMEM((count, FLAT), bf16),
         [near(x) for x in (*pieces, *tables)],
-        [pltpu.VMEM((max(PAIRS * (count + PAD), count * (PAIRS + PAD)), LANES), f32)],
+        [pltpu.VMEM((max((PAIRS + 1) * (count + PAD), (count + 1) * (PAIRS + PAD)), LANES), f32)],
         us=us,
     )
 

time: 24.9 us -> 24.9 us (level)
  no operation moved by 1% of the time
where the time goes in v8:
time: 24.9 us; the launch traced here: 24.7 us
  starting transfers between devices  10.4 us (42%)
  Pallas kernels  8.73 us (35%)
  waiting for transfers between devices  5.43 us (22%)
    pallas_call x15, Pallas kernels, call(): pl.pallas_call(body, out_shape=outs, in_specs=specs or [WHOLE] * len(ins)...  8.73 us
    ppermute x3, starting transfers between devices, hop(): lax.ppermute(x, 'ex', [(e, (e + 2 * step) % exs) for e in range(exs)])  5.07 us
    ppermute x1, starting transfers between devices, local(): lax.ppermute(messages[k // 2], 'dim', [(z, z ^ k) for z in range(dims)])  2.9 us
    ppermute x1, waiting for transfers between devices, local(): lax.ppermute(messages[k // 2], 'dim', [(z, z ^ k) for z in range(dims)])  2.02 us
    ppermute x1, starting transfers between devices, local(): got = lax.ppermute(message, 'dim', [(z, z ^ 1) for z in range(dims)])  1.64 us
    ppermute x4, waiting for transfers between devices, swap(): return lax.ppermute(x, 'ex', across)  1.55 us
    ppermute x3, waiting for transfers between devices, hop(): lax.ppermute(x, 'ex', [(e, (e + 2 * step) % exs) for e in range(exs)])  1.48 us
    ppermute x4, starting transfers between devices, swap(): return lax.ppermute(x, 'ex', across)  0.82 us
  transfers between devices with their start and end apart: 9, of which 6 were waited for; matrix products, arithmetic and copies ran while one was open for 0% of the time, Pallas kernels for 33%

profile of v8, /device:TPU:0, one launch (start us, length us, event | category | flops | bytes accessed | tf_op | source)
XLA Modules:
  0.0 24.7 jit_solution(6747119490896347321)
XLA Ops:
  0.0 0.5 %collective-permute-start = (bf16[32,8192]{1,0:T(8,128)(2,1)}, bf16[32,8192]{1,0:T(8,128)(2,1)S(1)}, u32[]{:S(2)}, u32[]{:S(2)}) collective-permute-start(bf16[32,8192]{1,0:T(8,128)(2,1)} %refs_4_.1), channel_id=1, source_target_pairs={{0,1},{1,0},{2,3},{3,2},{4,5},{5,4},{6,7},{7,6},{8,9},{9,8},{10,11... | collective-permute-start | bytes 1572872 | tf_op jit(solution)/shard_map/ppermute | solution.py:288
  0.5 1.2 %factors.1 = (bf16[64,256]{1,0:T(8,128)(2,1)S(1)}, bf16[64,256]{1,0:T(8,128)(2,1)S(1)}, bf16[256,128]{1,0:T(8,128)(2,1)S(1)}, bf16[256,256]{1,0:T(8,128)(2,1)S(1...) custom-call(f32[2,64,64]{2,1,0:T(8,128)} %refs_0_.1, f32[2,64,64]{2,1,0:T(8,128)} %refs_1_.1, f32[2,64]{1,0:T(2,128)} %refs_2_.1, ...), custom_call_target="tpu_custom_call" | custom-call | flops 27600000 | tf_op jit(solution)/shard_map/factors/pallas_call | solution.py:40
  1.6 0.6 %collective-permute-done.other.refs_1_ = bf16[32,8192]{1,0:T(8,128)(2,1)S(1)} collective-permute-done((bf16[32,8192]{1,0:T(8,128)(2,1)}, bf16[32,8192]{1,0:T(8,128)(2,1)S(1)}, u32[]{:S(2)}, u32[]{:S(2)}) %collective-permute-start) | collective-permute-done | bytes 524320 | tf_op jit(solution)/shard_map/ppermute | solution.py:288
  2.2 0.0 copy-start
  2.2 2.9 %collective-permute-start.2 = (bf16[16,4096]{1,0:T(8,128)(2,1)S(1)}, bf16[16,4096]{1,0:T(8,128)(2,1)S(1)}, u32[]{:S(2)}, u32[]{:S(2)}) collective-permute-start(bf16[16,4096]{1,0:T(8,128)(2,1)S(1)} %pick.1.refs_0_), channel_id=1, source_target_pairs={{0,2},{1,3},{2,0},{3,1},{4,6},{5,7},{6,4},{7,5},{8,10},{9,11},{10,... | collective-permute-start | bytes 393224 | tf_op jit(solution)/shard_map/ppermute | solution.py:291
  5.1 1.0 %odd_b.1._.refs_1_ = bf16[16,4096]{1,0:T(8,128)(2,1)S(1)} custom-call(bf16[32,8192]{1,0:T(8,128)(2,1)S(1)} %get-tuple-element.37.own.refs_0_, bf16[32,8192]{1,0:T(8,128)(2,1)S(1)} %collective-permute-done.other.refs_1_, bf16[64,256]{1,0:T(8,128)(2,1)S(1)} %get-tuple-element.30.refs_2_, bf16[64,256]{1,0:T(8,128)(2,1)S(1)} %get-tuple-element.31.refs_3_, ...), custom_call_target="tpu_custom_call" | custom-call | flops 23000000 | tf_op jit(solution)/shard_map/odd_b/pallas_call | solution.py:40
  6.1 0.1 collective-permute-start.3
  6.2 0.0 copy-done
  6.2 0.8 %theirs.1 = (bf16[4096,256]{1,0:T(8,128)(2,1)S(1)}, bf16[256,4096]{1,0:T(8,128)(2,1)S(1)}, f32[8,256]{1,0:T(8,128)S(1)}) custom-call(bf16[256,8192]{1,0:T(8,128)(2,1)S(1)} %copy-done, bf16[16,4096]{1,0:T(8,128)(2,1)S(1)} %odd_b.1._.refs_1_), custom_call_target="tpu_custom_call" | custom-call | flops 16100000 | tf_op jit(solution)/shard_map/theirs/pallas_call | solution.py:40
  7.0 0.1 collective-permute-start.1
  7.1 1.3 %even.1.refs_3_ = bf16[32,4096]{1,0:T(8,128)(2,1)S(1)} custom-call(bf16[32,8192]{1,0:T(8,128)(2,1)S(1)} %get-tuple-element.37.own.refs_0_, bf16[32,8192]{1,0:T(8,128)(2,1)S(1)} %collective-permute-done.other.refs_1_, bf16[64,256]{1,0:T(8,128)(2,1)S(1)} %get-tuple-element.30.refs_2_, bf16[64,256]{1,0:T(8,128)(2,1)S(1)} %get-tuple-element.31.refs_3_, ...), custom_call_target="tpu_custom_call" | custom-call | flops 23000000512 | tf_op jit(solution)/shard_map/even/pallas_call | solution.py:40
  8.4 2.1 %collective-permute-start.5 = (bf16[32,4096]{1,0:T(8,128)(2,1)S(1)}, bf16[32,4096]{1,0:T(8,128)(2,1)S(1)}, u32[]{:S(2)}, u32[]{:S(2)}) collective-permute-start(bf16[32,4096]{1,0:T(8,128)(2,1)S(1)} %even.1.refs_3_), channel_id=1, source_target_pairs={{0,2},{1,3},{2,0},{3,1},{4,6},{5,7},{6,4},{7,5},{8,10},{9,11},{10,... | collective-permute-start | bytes 786440 | tf_op jit(solution)/shard_map/ppermute | solution.py:291
  10.5 0.6 %ours.1 = (bf16[4096,256]{1,0:T(8,128)(2,1)S(1)}, f32[8,256]{1,0:T(8,128)S(1)}) custom-call(bf16[256,4096]{1,0:T(8,128)(2,1)S(1)} %get-tuple-element.38.rest, f32[8,256]{1,0:T(8,128)S(1)} %get-tuple-element.36.before), custom_call_target="tpu_custom_call" | custom-call | flops 13800000 | tf_op jit(solution)/shard_map/ours/pallas_call | solution.py:40
  11.1 0.0 collective-permute-done.2.refs_1_
  11.1 1.3 %odd_a.1.refs_0_ = bf16[32,4096]{1,0:T(8,128)(2,1)S(1)} custom-call(bf16[16,4096]{1,0:T(8,128)(2,1)S(1)} %pick.1.refs_0_, bf16[16,4096]{1,0:T(8,128)(2,1)S(1)} %collective-permute-done.2.refs_1_, bf16[64,256]{1,0:T(8,128)(2,1)S(1)} %get-tuple-element.30.refs_2_, bf16[64,256]{1,0:T(8,128)(2,1)S(1)} %get-tuple-element.31.refs_3_, ...), custom_call_target="tpu_custom_call" | custom-call | flops 23000000 | tf_op jit(solution)/shard_map/odd_a/pallas_call | solution.py:40
  12.4 0.0 collective-permute-done.3.refs_2_
  12.4 0.0 collective-permute-done.1.turned
  12.4 0.5 %odd_far.1 = f32[96,256]{1,0:T(8,128)S(1)} custom-call(bf16[4096,256]{1,0:T(8,128)(2,1)S(1)} %collective-permute-done.1.turned, bf16[32,4096]{1,0:T(8,128)(2,1)S(1)} %odd_a.1.refs_0_, bf16[16,4096]{1,0:T(8,128)(2,1)S(1)} %odd_b.1._.refs_1_, bf16[16,4096]{1,0:T(8,128)(2,1)S(1)} %collective-permute-done.3.refs_2_, bf16[32,4096]{1,0:T(8,128)(2,1)S(1)} %even.1.refs_3_), custom_call_target="tpu_custom_call" | custom-call | flops 11500000 | tf_op jit(solution)/shard_map/odd_far/pallas_call | solution.py:40
  12.9 0.3 %collective-permute-start.4 = (f32[96,256]{1,0:T(8,128)S(1)}, f32[96,256]{1,0:T(8,128)S(1)}, u32[]{:S(2)}, u32[]{:S(2)}) collective-permute-start(f32[96,256]{1,0:T(8,128)S(1)} %odd_far.1), channel_id=1, source_target_pairs={{0,1},{1,0},{2,3},{3,2},{4,5},{5,4},{6,7},{7,6},{8,9},{9,8},{10,11... | collective-permute-start | bytes 294920 | tf_op jit(solution)/shard_map/ppermute | solution.py:288
  13.2 0.5 %odd_near.1.two = f32[96,256]{1,0:T(8,128)S(1)} custom-call(bf16[4096,256]{1,0:T(8,128)(2,1)S(1)} %get-tuple-element.43.turned, bf16[32,4096]{1,0:T(8,128)(2,1)S(1)} %odd_a.1.refs_0_, bf16[16,4096]{1,0:T(8,128)(2,1)S(1)} %odd_b.1._.refs_1_, bf16[16,4096]{1,0:T(8,128)(2,1)S(1)} %collective-permute-done.3.refs_2_, bf16[32,4096]{1,0:T(8,128)(2,1)S(1)} %even.1.refs_3_), custom_call_target="tpu_custom_call" | custom-call | flops 11500000 | tf_op jit(solution)/shard_map/odd_near/pallas_call | solution.py:40
  13.7 0.6 %collective-permute-done.4.one = f32[96,256]{1,0:T(8,128)S(1)} collective-permute-done((f32[96,256]{1,0:T(8,128)S(1)}, f32[96,256]{1,0:T(8,128)S(1)}, u32[]{:S(2)}, u32[]{:S(2)}) %collective-permute-start.4) | collective-permute-done | bytes 98336 | tf_op jit(solution)/shard_map/ppermute | solution.py:288
  14.3 1.6 %collective-permute-start.7 = (f32[72,256]{1,0:T(8,128)S(1)}, f32[72,256]{1,0:T(8,128)S(1)}, u32[]{:S(2)}, u32[]{:S(2)}) collective-permute-start(f32[72,256]{1,0:T(8,128)S(1)} %get-tuple-element.45), channel_id=1, source_target_pairs={{0,4},{4,0},{8,12},{12,8},{1,5},{5,1},{9,13},{13,9},{2,6},{6,2},{1... | collective-permute-start | bytes 221192 | tf_op jit(solution)/shard_map/ppermute | solution.py:314
  15.9 1.5 %collective-permute-done.5.refs_0_ = bf16[32,4096]{1,0:T(8,128)(2,1)S(1)} collective-permute-done((bf16[32,4096]{1,0:T(8,128)(2,1)S(1)}, bf16[32,4096]{1,0:T(8,128)(2,1)S(1)}, u32[]{:S(2)}, u32[]{:S(2)}) %collective-permute-start.5) | collective-permute-done | bytes 262176 | tf_op jit(solution)/shard_map/ppermute | solution.py:291
  17.4 0.5 %even_far.1 = f32[32,256]{1,0:T(8,128)S(1)} custom-call(bf16[4096,256]{1,0:T(8,128)(2,1)S(1)} %collective-permute-done.1.turned, bf16[32,4096]{1,0:T(8,128)(2,1)S(1)} %collective-permute-done.5.refs_0_), custom_call_target="tpu_custom_call" | custom-call | flops 11500000 | tf_op jit(solution)/shard_map/even_far/pallas_call | solution.py:40
  17.9 0.0 collective-permute-start.6
  17.9 0.5 %even_near.1.two = f32[32,256]{1,0:T(8,128)S(1)} custom-call(bf16[4096,256]{1,0:T(8,128)(2,1)S(1)} %get-tuple-element.43.turned, bf16[32,4096]{1,0:T(8,128)(2,1)S(1)} %collective-permute-done.5.refs_0_), custom_call_target="tpu_custom_call" | custom-call | flops 11500000 | tf_op jit(solution)/shard_map/even_near/pallas_call | solution.py:40
  18.4 0.4 %collective-permute-done.7.got = f32[72,256]{1,0:T(8,128)S(1)} collective-permute-done((f32[72,256]{1,0:T(8,128)S(1)}, f32[72,256]{1,0:T(8,128)S(1)}, u32[]{:S(2)}, u32[]{:S(2)}) %collective-permute-start.7) | collective-permute-done | bytes 73760 | tf_op jit(solution)/shard_map/ppermute | solution.py:314
  18.8 0.3 %collective-permute-done.6.one = f32[32,256]{1,0:T(8,128)S(1)} collective-permute-done((f32[32,256]{1,0:T(8,128)S(1)}, f32[32,256]{1,0:T(8,128)S(1)}, u32[]{:S(2)}, u32[]{:S(2)}) %collective-permute-start.6) | collective-permute-done | bytes 32800 | tf_op jit(solution)/shard_map/ppermute | solution.py:288
  19.1 2.9 %collective-permute-start.8 = (f32[72,128]{1,0:T(8,128)S(1)}, f32[72,128]{1,0:T(8,128)S(1)}, u32[]{:S(2)}, u32[]{:S(2)}) collective-permute-start(f32[72,128]{1,0:T(8,128)S(1)} %get-tuple-element.50), channel_id=1, source_target_pairs={{0,8},{4,12},{8,0},{12,4},{1,9},{5,13},{9,1},{13,5},{2,10},{6,14},... | collective-permute-start | bytes 110600 | tf_op jit(solution)/shard_map/ppermute | solution.py:328
  22.1 2.0 %collective-permute-done.8.refs_1_ = f32[72,128]{1,0:T(8,128)S(1)} collective-permute-done((f32[72,128]{1,0:T(8,128)S(1)}, f32[72,128]{1,0:T(8,128)S(1)}, u32[]{:S(2)}, u32[]{:S(2)}) %collective-permute-start.8) | collective-permute-done | bytes 36896 | tf_op jit(solution)/shard_map/ppermute | solution.py:328
  24.1 0.6 %finish.1 = f32[32,256]{1,0:T(8,128)} custom-call(f32[72,128]{1,0:T(8,128)S(1)} %get-tuple-element.49.refs_0_, f32[72,128]{1,0:T(8,128)S(1)} %collective-permute-done.8.refs_1_), custom_call_target="tpu_custom_call" | custom-call | flops 13800000 | tf_op jit(solution)/shard_map/finish/pallas_call | solution.py:40
  (4 shorter events, 0.1 us)
Async XLA Ops:
  0.0 2.2 %collective-permute-start = (bf16[32,8192]{1,0:T(8,128)(2,1)}, bf16[32,8192]{1,0:T(8,128)(2,1)S(1)}, u32[]{:S(2)}, u32[]{:S(2)}) collective-permute-start(bf16[32,8192]{1,0:T(8,128)(2,1)} %refs_4_.1), channel_id=1, source_target_pairs={{0,1},{1,0},{2,3},{3,2},{4,5},{5,4},{6,7},{7,6},{8,9},{9,8},{10,11... | collective-permute-start | bytes 1572872 | tf_op jit(solution)/shard_map/ppermute | solution.py:288
  2.2 4.0 %copy-start = (bf16[256,8192]{1,0:T(8,128)(2,1)S(1)}, bf16[256,8192]{1,0:T(8,128)(2,1)}, u32[]{:S(2)}) copy-start(bf16[256,8192]{1,0:T(8,128)(2,1)} %store.1) | copy-start | bytes 12582916
  2.2 8.9 %collective-permute-start.2 = (bf16[16,4096]{1,0:T(8,128)(2,1)S(1)}, bf16[16,4096]{1,0:T(8,128)(2,1)S(1)}, u32[]{:S(2)}, u32[]{:S(2)}) collective-permute-start(bf16[16,4096]{1,0:T(8,128)(2,1)S(1)} %pick.1.refs_0_), channel_id=1, source_target_pairs={{0,2},{1,3},{2,0},{3,1},{4,6},{5,7},{6,4},{7,5},{8,10},{9,11},{10,... | collective-permute-start | bytes 393224 | tf_op jit(solution)/shard_map/ppermute | solution.py:291
  6.1 6.3 %collective-permute-start.3 = (bf16[16,4096]{1,0:T(8,128)(2,1)S(1)}, bf16[16,4096]{1,0:T(8,128)(2,1)S(1)}, u32[]{:S(2)}, u32[]{:S(2)}) collective-permute-start(bf16[16,4096]{1,0:T(8,128)(2,1)S(1)} %odd_b.1._.refs_1_), channel_id=1, source_target_pairs={{0,2},{1,3},{2,0},{3,1},{4,6},{5,7},{6,4},{7,5},{8,10},{9,11},{10,... | collective-permute-start | bytes 393224 | tf_op jit(solution)/shard_map/ppermute | solution.py:291
  7.0 5.4 %collective-permute-start.1 = (bf16[4096,256]{1,0:T(8,128)(2,1)S(1)}, bf16[4096,256]{1,0:T(8,128)(2,1)S(1)}, u32[]{:S(2)}, u32[]{:S(2)}) collective-permute-start(bf16[4096,256]{1,0:T(8,128)(2,1)S(1)} %get-tuple-element.40), channel_id=1, source_target_pairs={{0,1},{1,0},{2,3},{3,2},{4,5},{5,4},{6,7},{7,6},{8,9},{9,8},{10,11... | collective-permute-start | bytes 6291464 | tf_op jit(solution)/shard_map/ppermute | solution.py:288
  8.4 9.0 %collective-permute-start.5 = (bf16[32,4096]{1,0:T(8,128)(2,1)S(1)}, bf16[32,4096]{1,0:T(8,128)(2,1)S(1)}, u32[]{:S(2)}, u32[]{:S(2)}) collective-permute-start(bf16[32,4096]{1,0:T(8,128)(2,1)S(1)} %even.1.refs_3_), channel_id=1, source_target_pairs={{0,2},{1,3},{2,0},{3,1},{4,6},{5,7},{6,4},{7,5},{8,10},{9,11},{10,... | collective-permute-start | bytes 786440 | tf_op jit(solution)/shard_map/ppermute | solution.py:291
  12.9 1.4 %collective-permute-start.4 = (f32[96,256]{1,0:T(8,128)S(1)}, f32[96,256]{1,0:T(8,128)S(1)}, u32[]{:S(2)}, u32[]{:S(2)}) collective-permute-start(f32[96,256]{1,0:T(8,128)S(1)} %odd_far.1), channel_id=1, source_target_pairs={{0,1},{1,0},{2,3},{3,2},{4,5},{5,4},{6,7},{7,6},{8,9},{9,8},{10,11... | collective-permute-start | bytes 294920 | tf_op jit(solution)/shard_map/ppermute | solution.py:288
  14.3 4.4 %collective-permute-start.7 = (f32[72,256]{1,0:T(8,128)S(1)}, f32[72,256]{1,0:T(8,128)S(1)}, u32[]{:S(2)}, u32[]{:S(2)}) collective-permute-start(f32[72,256]{1,0:T(8,128)S(1)} %get-tuple-element.45), channel_id=1, source_target_pairs={{0,4},{4,0},{8,12},{12,8},{1,5},{5,1},{9,13},{13,9},{2,6},{6,2},{1... | collective-permute-start | bytes 221192 | tf_op jit(solution)/shard_map/ppermute | solution.py:314
  17.9 1.2 %collective-permute-start.6 = (f32[32,256]{1,0:T(8,128)S(1)}, f32[32,256]{1,0:T(8,128)S(1)}, u32[]{:S(2)}, u32[]{:S(2)}) collective-permute-start(f32[32,256]{1,0:T(8,128)S(1)} %even_far.1), channel_id=1, source_target_pairs={{0,1},{1,0},{2,3},{3,2},{4,5},{5,4},{6,7},{7,6},{8,9},{9,8},{10,11... | collective-permute-start | bytes 98312 | tf_op jit(solution)/shard_map/ppermute | solution.py:288
  19.1 4.9 %collective-permute-start.8 = (f32[72,128]{1,0:T(8,128)S(1)}, f32[72,128]{1,0:T(8,128)S(1)}, u32[]{:S(2)}, u32[]{:S(2)}) collective-permute-start(f32[72,128]{1,0:T(8,128)S(1)} %get-tuple-element.50), channel_id=1, source_target_pairs={{0,8},{4,12},{8,0},{12,4},{1,9},{5,13},{9,1},{13,5},{2,10},{6,14},... | collective-permute-start | bytes 110600 | tf_op jit(solution)/shard_map/ppermute | solution.py:328

commit v9 on v8

--- a/solution.py
+++ b/solution.py
@@ -196,14 +196,12 @@
     return mm(x, turned[first : first + x.shape[1], :])
 
 
-def theirs_body(store, _, turned, rest, out):
-    core = position()[1]
-    out[...] = turn_store(store, turned, (1 - core) * FLAT)
-    rest[...] = store[:, pl.ds(pl.multiple_of(core * FLAT, FLAT), FLAT)]
-
-
-def ours_body(rest, before, turned, out):
-    out[...] = before[...] + turn_store(rest, turned, 0)
+def theirs_body(store, _, turned, out):
+    out[...] = turn_store(store, turned, (1 - position()[1]) * FLAT)
+
+
+def ours_body(store, before, turned, out):
+    out[...] = before[...] + turn_store(store, turned, position()[1] * FLAT)
 
 
 def woven(pieces, rows):
@@ -297,12 +295,11 @@
     odd_b = precondition("odd_b", (after(own, raw), other), tables, count - ROWS, 1, ROWS, us=ODDB)
     odd_b_came = [hop(odd_b, step) for step in range(1, chips)]
     turned, squares = pltpu.VMEM((FLAT, rows), bf16), pltpu.VMEM((8, rows), f32)
-    outs = [turned, pltpu.VMEM((rows, FLAT), bf16), squares]
-    turned_theirs, rest, part = call(theirs_body, "theirs", outs, [near(store), near(odd_b)], us=0.7)
+    turned_theirs, part = call(theirs_body, "theirs", [turned, squares], [near(store), near(odd_b)], us=0.7)
     far_rows = swap(turned_theirs)
     ours = precondition("even", (after(own, part), other), tables, count, 0, us=EVEN)
     even_came = [hop(ours, step) for step in range(1, chips)]
-    ins = [near(x) for x in (after(rest, ours), part)]
+    ins = [near(x) for x in (after(store, ours), part)]
     turned_ours, squares = call(ours_body, "ours", [turned, squares], ins, us=0.6)
     odd_a = precondition("odd_a", (after(raw, squares), *raw_came), tables, chips * ROWS)
 

time: 24.9 us -> 24.8 us (level)
  transfers between devices with their start and end apart: 9 -> 9, of which waited for: 6 -> 6; matrix products, arithmetic and copies ran while one was open for 0% -> 0% of each run, Pallas kernels for 33% -> 32%
where the time goes in v9:
time: 24.8 us; the launch traced here: 24.7 us
  starting transfers between devices  10.4 us (42%)
  Pallas kernels  8.66 us (35%)
  waiting for transfers between devices  5.46 us (22%)
    pallas_call x15, Pallas kernels, call(): pl.pallas_call(body, out_shape=outs, in_specs=specs or [WHOLE] * len(ins)...  8.66 us
    ppermute x3, starting transfers between devices, hop(): lax.ppermute(x, 'ex', [(e, (e + 2 * step) % exs) for e in range(exs)])  5.06 us
    ppermute x1, starting transfers between devices, local(): lax.ppermute(messages[k // 2], 'dim', [(z, z ^ k) for z in range(dims)])  2.9 us
    ppermute x1, waiting for transfers between devices, local(): lax.ppermute(messages[k // 2], 'dim', [(z, z ^ k) for z in range(dims)])  2.02 us
    ppermute x1, starting transfers between devices, local(): got = lax.ppermute(message, 'dim', [(z, z ^ 1) for z in range(dims)])  1.64 us
    ppermute x4, waiting for transfers between devices, swap(): return lax.ppermute(x, 'ex', across)  1.6 us
    ppermute x3, waiting for transfers between devices, hop(): lax.ppermute(x, 'ex', [(e, (e + 2 * step) % exs) for e in range(exs)])  1.55 us
    ppermute x4, starting transfers between devices, swap(): return lax.ppermute(x, 'ex', across)  0.82 us
  transfers between devices with their start and end apart: 9, of which 6 were waited for; matrix products, arithmetic and copies ran while one was open for 0% of the time, Pallas kernels for 32%

profile of v9, /device:TPU:0, one launch (start us, length us, event | category | flops | bytes accessed | tf_op | source)
XLA Modules:
  0.0 24.7 jit_solution(12164338607371812182)
XLA Ops:
  0.0 0.5 %collective-permute-start = (bf16[32,8192]{1,0:T(8,128)(2,1)}, bf16[32,8192]{1,0:T(8,128)(2,1)S(1)}, u32[]{:S(2)}, u32[]{:S(2)}) collective-permute-start(bf16[32,8192]{1,0:T(8,128)(2,1)} %refs_4_.1), channel_id=1, source_target_pairs={{0,1},{1,0},{2,3},{3,2},{4,5},{5,4},{6,7},{7,6},{8,9},{9,8},{10,11... | collective-permute-start | bytes 1572872 | tf_op jit(solution)/shard_map/ppermute | solution.py:286
  0.5 1.2 %factors.1 = (bf16[64,256]{1,0:T(8,128)(2,1)S(1)}, bf16[64,256]{1,0:T(8,128)(2,1)S(1)}, bf16[256,128]{1,0:T(8,128)(2,1)S(1)}, bf16[256,256]{1,0:T(8,128)(2,1)S(1...) custom-call(f32[2,64,64]{2,1,0:T(8,128)} %refs_0_.1, f32[2,64,64]{2,1,0:T(8,128)} %refs_1_.1, f32[2,64]{1,0:T(2,128)} %refs_2_.1, ...), custom_call_target="tpu_custom_call" | custom-call | flops 27600000 | tf_op jit(solution)/shard_map/factors/pallas_call | solution.py:40
  1.6 0.6 %collective-permute-done.other.refs_1_ = bf16[32,8192]{1,0:T(8,128)(2,1)S(1)} collective-permute-done((bf16[32,8192]{1,0:T(8,128)(2,1)}, bf16[32,8192]{1,0:T(8,128)(2,1)S(1)}, u32[]{:S(2)}, u32[]{:S(2)}) %collective-permute-start) | collective-permute-done | bytes 524320 | tf_op jit(solution)/shard_map/ppermute | solution.py:286
  2.2 0.0 copy-start
  2.2 2.9 %collective-permute-start.2 = (bf16[16,4096]{1,0:T(8,128)(2,1)S(1)}, bf16[16,4096]{1,0:T(8,128)(2,1)S(1)}, u32[]{:S(2)}, u32[]{:S(2)}) collective-permute-start(bf16[16,4096]{1,0:T(8,128)(2,1)S(1)} %pick.1.refs_0_), channel_id=1, source_target_pairs={{0,2},{1,3},{2,0},{3,1},{4,6},{5,7},{6,4},{7,5},{8,10},{9,11},{10,... | collective-permute-start | bytes 393224 | tf_op jit(solution)/shard_map/ppermute | solution.py:289
  5.1 1.0 %odd_b.1._.refs_1_ = bf16[16,4096]{1,0:T(8,128)(2,1)S(1)} custom-call(bf16[32,8192]{1,0:T(8,128)(2,1)S(1)} %get-tuple-element.35.own.refs_0_, bf16[32,8192]{1,0:T(8,128)(2,1)S(1)} %collective-permute-done.other.refs_1_, bf16[64,256]{1,0:T(8,128)(2,1)S(1)} %get-tuple-element.29.refs_2_, bf16[64,256]{1,0:T(8,128)(2,1)S(1)} %get-tuple-element.30.refs_3_, ...), custom_call_target="tpu_custom_call" | custom-call | flops 23000000 | tf_op jit(solution)/shard_map/odd_b/pallas_call | solution.py:40
  6.1 0.1 collective-permute-start.3
  6.2 0.0 copy-done
  6.2 0.6 %theirs.1 = (bf16[4096,256]{1,0:T(8,128)(2,1)S(1)}, f32[8,256]{1,0:T(8,128)S(1)}) custom-call(bf16[256,8192]{1,0:T(8,128)(2,1)S(1)} %copy-done, bf16[16,4096]{1,0:T(8,128)(2,1)S(1)} %odd_b.1._.refs_1_), custom_call_target="tpu_custom_call" | custom-call | flops 16100000 | tf_op jit(solution)/shard_map/theirs/pallas_call | solution.py:40
  6.9 0.1 collective-permute-start.1
  7.0 1.3 %even.1.refs_3_ = bf16[32,4096]{1,0:T(8,128)(2,1)S(1)} custom-call(bf16[32,8192]{1,0:T(8,128)(2,1)S(1)} %get-tuple-element.35.own.refs_0_, bf16[32,8192]{1,0:T(8,128)(2,1)S(1)} %collective-permute-done.other.refs_1_, bf16[64,256]{1,0:T(8,128)(2,1)S(1)} %get-tuple-element.29.refs_2_, bf16[64,256]{1,0:T(8,128)(2,1)S(1)} %get-tuple-element.30.refs_3_, ...), custom_call_target="tpu_custom_call" | custom-call | flops 23000000512 | tf_op jit(solution)/shard_map/even/pallas_call | solution.py:40
  8.3 2.1 %collective-permute-start.5 = (bf16[32,4096]{1,0:T(8,128)(2,1)S(1)}, bf16[32,4096]{1,0:T(8,128)(2,1)S(1)}, u32[]{:S(2)}, u32[]{:S(2)}) collective-permute-start(bf16[32,4096]{1,0:T(8,128)(2,1)S(1)} %even.1.refs_3_), channel_id=1, source_target_pairs={{0,2},{1,3},{2,0},{3,1},{4,6},{5,7},{6,4},{7,5},{8,10},{9,11},{10,... | collective-permute-start | bytes 786440 | tf_op jit(solution)/shard_map/ppermute | solution.py:289
  10.3 0.6 %ours.1 = (bf16[4096,256]{1,0:T(8,128)(2,1)S(1)}, f32[8,256]{1,0:T(8,128)S(1)}) custom-call(bf16[256,8192]{1,0:T(8,128)(2,1)S(1)} %copy-done, f32[8,256]{1,0:T(8,128)S(1)} %get-tuple-element.34.before), custom_call_target="tpu_custom_call" | custom-call | flops 13800000 | tf_op jit(solution)/shard_map/ours/pallas_call | solution.py:40
  11.0 0.0 collective-permute-done.2.refs_1_
  11.0 1.3 %odd_a.1.refs_0_ = bf16[32,4096]{1,0:T(8,128)(2,1)S(1)} custom-call(bf16[16,4096]{1,0:T(8,128)(2,1)S(1)} %pick.1.refs_0_, bf16[16,4096]{1,0:T(8,128)(2,1)S(1)} %collective-permute-done.2.refs_1_, bf16[64,256]{1,0:T(8,128)(2,1)S(1)} %get-tuple-element.29.refs_2_, bf16[64,256]{1,0:T(8,128)(2,1)S(1)} %get-tuple-element.30.refs_3_, ...), custom_call_target="tpu_custom_call" | custom-call | flops 23000000 | tf_op jit(solution)/shard_map/odd_a/pallas_call | solution.py:40
  12.3 0.0 collective-permute-done.3.refs_2_
  12.3 0.0 collective-permute-done.1.turned
  12.3 0.5 %odd_far.1 = f32[96,256]{1,0:T(8,128)S(1)} custom-call(bf16[4096,256]{1,0:T(8,128)(2,1)S(1)} %collective-permute-done.1.turned, bf16[32,4096]{1,0:T(8,128)(2,1)S(1)} %odd_a.1.refs_0_, bf16[16,4096]{1,0:T(8,128)(2,1)S(1)} %odd_b.1._.refs_1_, bf16[16,4096]{1,0:T(8,128)(2,1)S(1)} %collective-permute-done.3.refs_2_, bf16[32,4096]{1,0:T(8,128)(2,1)S(1)} %even.1.refs_3_), custom_call_target="tpu_custom_call" | custom-call | flops 11500000 | tf_op jit(solution)/shard_map/odd_far/pallas_call | solution.py:40
  12.8 0.3 %collective-permute-start.4 = (f32[96,256]{1,0:T(8,128)S(1)}, f32[96,256]{1,0:T(8,128)S(1)}, u32[]{:S(2)}, u32[]{:S(2)}) collective-permute-start(f32[96,256]{1,0:T(8,128)S(1)} %odd_far.1), channel_id=1, source_target_pairs={{0,1},{1,0},{2,3},{3,2},{4,5},{5,4},{6,7},{7,6},{8,9},{9,8},{10,11... | collective-permute-start | bytes 294920 | tf_op jit(solution)/shard_map/ppermute | solution.py:286
  13.1 0.5 %odd_near.1.two = f32[96,256]{1,0:T(8,128)S(1)} custom-call(bf16[4096,256]{1,0:T(8,128)(2,1)S(1)} %get-tuple-element.41.turned, bf16[32,4096]{1,0:T(8,128)(2,1)S(1)} %odd_a.1.refs_0_, bf16[16,4096]{1,0:T(8,128)(2,1)S(1)} %odd_b.1._.refs_1_, bf16[16,4096]{1,0:T(8,128)(2,1)S(1)} %collective-permute-done.3.refs_2_, bf16[32,4096]{1,0:T(8,128)(2,1)S(1)} %even.1.refs_3_), custom_call_target="tpu_custom_call" | custom-call | flops 11500000 | tf_op jit(solution)/shard_map/odd_near/pallas_call | solution.py:40
  13.6 0.6 %collective-permute-done.4.one = f32[96,256]{1,0:T(8,128)S(1)} collective-permute-done((f32[96,256]{1,0:T(8,128)S(1)}, f32[96,256]{1,0:T(8,128)S(1)}, u32[]{:S(2)}, u32[]{:S(2)}) %collective-permute-start.4) | collective-permute-done | bytes 98336 | tf_op jit(solution)/shard_map/ppermute | solution.py:286
  14.2 1.6 %collective-permute-start.7 = (f32[72,256]{1,0:T(8,128)S(1)}, f32[72,256]{1,0:T(8,128)S(1)}, u32[]{:S(2)}, u32[]{:S(2)}) collective-permute-start(f32[72,256]{1,0:T(8,128)S(1)} %get-tuple-element.43), channel_id=1, source_target_pairs={{0,4},{4,0},{8,12},{12,8},{1,5},{5,1},{9,13},{13,9},{2,6},{6,2},{1... | collective-permute-start | bytes 221192 | tf_op jit(solution)/shard_map/ppermute | solution.py:311
  15.8 1.5 %collective-permute-done.5.refs_0_ = bf16[32,4096]{1,0:T(8,128)(2,1)S(1)} collective-permute-done((bf16[32,4096]{1,0:T(8,128)(2,1)S(1)}, bf16[32,4096]{1,0:T(8,128)(2,1)S(1)}, u32[]{:S(2)}, u32[]{:S(2)}) %collective-permute-start.5) | collective-permute-done | bytes 262176 | tf_op jit(solution)/shard_map/ppermute | solution.py:289
  17.4 0.5 %even_far.1 = f32[32,256]{1,0:T(8,128)S(1)} custom-call(bf16[4096,256]{1,0:T(8,128)(2,1)S(1)} %collective-permute-done.1.turned, bf16[32,4096]{1,0:T(8,128)(2,1)S(1)} %collective-permute-done.5.refs_0_), custom_call_target="tpu_custom_call" | custom-call | flops 11500000 | tf_op jit(solution)/shard_map/even_far/pallas_call | solution.py:40
  17.8 0.0 collective-permute-start.6
  17.9 0.5 %even_near.1.two = f32[32,256]{1,0:T(8,128)S(1)} custom-call(bf16[4096,256]{1,0:T(8,128)(2,1)S(1)} %get-tuple-element.41.turned, bf16[32,4096]{1,0:T(8,128)(2,1)S(1)} %collective-permute-done.5.refs_0_), custom_call_target="tpu_custom_call" | custom-call | flops 11500000 | tf_op jit(solution)/shard_map/even_near/pallas_call | solution.py:40
  18.3 0.3 %collective-permute-done.7.got = f32[72,256]{1,0:T(8,128)S(1)} collective-permute-done((f32[72,256]{1,0:T(8,128)S(1)}, f32[72,256]{1,0:T(8,128)S(1)}, u32[]{:S(2)}, u32[]{:S(2)}) %collective-permute-start.7) | collective-permute-done | bytes 73760 | tf_op jit(solution)/shard_map/ppermute | solution.py:311
  18.6 0.4 %collective-permute-done.6.one = f32[32,256]{1,0:T(8,128)S(1)} collective-permute-done((f32[32,256]{1,0:T(8,128)S(1)}, f32[32,256]{1,0:T(8,128)S(1)}, u32[]{:S(2)}, u32[]{:S(2)}) %collective-permute-start.6) | collective-permute-done | bytes 32800 | tf_op jit(solution)/shard_map/ppermute | solution.py:286
  19.1 2.9 %collective-permute-start.8 = (f32[72,128]{1,0:T(8,128)S(1)}, f32[72,128]{1,0:T(8,128)S(1)}, u32[]{:S(2)}, u32[]{:S(2)}) collective-permute-start(f32[72,128]{1,0:T(8,128)S(1)} %get-tuple-element.48), channel_id=1, source_target_pairs={{0,8},{4,12},{8,0},{12,4},{1,9},{5,13},{9,1},{13,5},{2,10},{6,14},... | collective-permute-start | bytes 110600 | tf_op jit(solution)/shard_map/ppermute | solution.py:325
  22.0 2.0 %collective-permute-done.8.refs_1_ = f32[72,128]{1,0:T(8,128)S(1)} collective-permute-done((f32[72,128]{1,0:T(8,128)S(1)}, f32[72,128]{1,0:T(8,128)S(1)}, u32[]{:S(2)}, u32[]{:S(2)}) %collective-permute-start.8) | collective-permute-done | bytes 36896 | tf_op jit(solution)/shard_map/ppermute | solution.py:325
  24.0 0.6 %finish.1 = f32[32,256]{1,0:T(8,128)} custom-call(f32[72,128]{1,0:T(8,128)S(1)} %get-tuple-element.47.refs_0_, f32[72,128]{1,0:T(8,128)S(1)} %collective-permute-done.8.refs_1_), custom_call_target="tpu_custom_call" | custom-call | flops 13800000 | tf_op jit(solution)/shard_map/finish/pallas_call | solution.py:40
  (4 shorter events, 0.1 us)
Async XLA Ops:
  0.0 2.2 %collective-permute-start = (bf16[32,8192]{1,0:T(8,128)(2,1)}, bf16[32,8192]{1,0:T(8,128)(2,1)S(1)}, u32[]{:S(2)}, u32[]{:S(2)}) collective-permute-start(bf16[32,8192]{1,0:T(8,128)(2,1)} %refs_4_.1), channel_id=1, source_target_pairs={{0,1},{1,0},{2,3},{3,2},{4,5},{5,4},{6,7},{7,6},{8,9},{9,8},{10,11... | collective-permute-start | bytes 1572872 | tf_op jit(solution)/shard_map/ppermute | solution.py:286
  2.2 4.0 %copy-start = (bf16[256,8192]{1,0:T(8,128)(2,1)S(1)}, bf16[256,8192]{1,0:T(8,128)(2,1)}, u32[]{:S(2)}) copy-start(bf16[256,8192]{1,0:T(8,128)(2,1)} %store.2) | copy-start | bytes 12582916
  2.2 8.7 %collective-permute-start.2 = (bf16[16,4096]{1,0:T(8,128)(2,1)S(1)}, bf16[16,4096]{1,0:T(8,128)(2,1)S(1)}, u32[]{:S(2)}, u32[]{:S(2)}) collective-permute-start(bf16[16,4096]{1,0:T(8,128)(2,1)S(1)} %pick.1.refs_0_), channel_id=1, source_target_pairs={{0,2},{1,3},{2,0},{3,1},{4,6},{5,7},{6,4},{7,5},{8,10},{9,11},{10,... | collective-permute-start | bytes 393224 | tf_op jit(solution)/shard_map/ppermute | solution.py:289
  6.1 6.1 %collective-permute-start.3 = (bf16[16,4096]{1,0:T(8,128)(2,1)S(1)}, bf16[16,4096]{1,0:T(8,128)(2,1)S(1)}, u32[]{:S(2)}, u32[]{:S(2)}) collective-permute-start(bf16[16,4096]{1,0:T(8,128)(2,1)S(1)} %odd_b.1._.refs_1_), channel_id=1, source_target_pairs={{0,2},{1,3},{2,0},{3,1},{4,6},{5,7},{6,4},{7,5},{8,10},{9,11},{10,... | collective-permute-start | bytes 393224 | tf_op jit(solution)/shard_map/ppermute | solution.py:289
  6.9 5.4 %collective-permute-start.1 = (bf16[4096,256]{1,0:T(8,128)(2,1)S(1)}, bf16[4096,256]{1,0:T(8,128)(2,1)S(1)}, u32[]{:S(2)}, u32[]{:S(2)}) collective-permute-start(bf16[4096,256]{1,0:T(8,128)(2,1)S(1)} %get-tuple-element.38), channel_id=1, source_target_pairs={{0,1},{1,0},{2,3},{3,2},{4,5},{5,4},{6,7},{7,6},{8,9},{9,8},{10,11... | collective-permute-start | bytes 6291464 | tf_op jit(solution)/shard_map/ppermute | solution.py:286
  8.3 9.1 %collective-permute-start.5 = (bf16[32,4096]{1,0:T(8,128)(2,1)S(1)}, bf16[32,4096]{1,0:T(8,128)(2,1)S(1)}, u32[]{:S(2)}, u32[]{:S(2)}) collective-permute-start(bf16[32,4096]{1,0:T(8,128)(2,1)S(1)} %even.1.refs_3_), channel_id=1, source_target_pairs={{0,2},{1,3},{2,0},{3,1},{4,6},{5,7},{6,4},{7,5},{8,10},{9,11},{10,... | collective-permute-start | bytes 786440 | tf_op jit(solution)/shard_map/ppermute | solution.py:289
  12.8 1.4 %collective-permute-start.4 = (f32[96,256]{1,0:T(8,128)S(1)}, f32[96,256]{1,0:T(8,128)S(1)}, u32[]{:S(2)}, u32[]{:S(2)}) collective-permute-start(f32[96,256]{1,0:T(8,128)S(1)} %odd_far.1), channel_id=1, source_target_pairs={{0,1},{1,0},{2,3},{3,2},{4,5},{5,4},{6,7},{7,6},{8,9},{9,8},{10,11... | collective-permute-start | bytes 294920 | tf_op jit(solution)/shard_map/ppermute | solution.py:286
  14.2 4.4 %collective-permute-start.7 = (f32[72,256]{1,0:T(8,128)S(1)}, f32[72,256]{1,0:T(8,128)S(1)}, u32[]{:S(2)}, u32[]{:S(2)}) collective-permute-start(f32[72,256]{1,0:T(8,128)S(1)} %get-tuple-element.43), channel_id=1, source_target_pairs={{0,4},{4,0},{8,12},{12,8},{1,5},{5,1},{9,13},{13,9},{2,6},{6,2},{1... | collective-permute-start | bytes 221192 | tf_op jit(solution)/shard_map/ppermute | solution.py:311
  17.8 1.2 %collective-permute-start.6 = (f32[32,256]{1,0:T(8,128)S(1)}, f32[32,256]{1,0:T(8,128)S(1)}, u32[]{:S(2)}, u32[]{:S(2)}) collective-permute-start(f32[32,256]{1,0:T(8,128)S(1)} %even_far.1), channel_id=1, source_target_pairs={{0,1},{1,0},{2,3},{3,2},{4,5},{5,4},{6,7},{7,6},{8,9},{9,8},{10,11... | collective-permute-start | bytes 98312 | tf_op jit(solution)/shard_map/ppermute | solution.py:286
  19.1 4.9 %collective-permute-start.8 = (f32[72,128]{1,0:T(8,128)S(1)}, f32[72,128]{1,0:T(8,128)S(1)}, u32[]{:S(2)}, u32[]{:S(2)}) collective-permute-start(f32[72,128]{1,0:T(8,128)S(1)} %get-tuple-element.48), channel_id=1, source_target_pairs={{0,8},{4,12},{8,0},{12,4},{1,9},{5,13},{9,1},{13,5},{2,10},{6,14},... | collective-permute-start | bytes 110600 | tf_op jit(solution)/shard_map/ppermute | solution.py:325

commit v10 on v8

--- a/solution.py
+++ b/solution.py
@@ -36,13 +36,14 @@
     return lax.optimization_barrier((x, *others))[0]
 
 
-def call(body, name, outs, ins, scratch=(), us=1.0, specs=None, to=WHOLE):
+def call(body, name, outs, ins, scratch=(), us=1.0, specs=None, to=WHOLE, aliases=()):
     return pl.pallas_call(
         body,
         out_shape=outs,
         in_specs=specs or [WHOLE] * len(ins),
         out_specs=jax.tree.map(lambda _: to, outs, is_leaf=lambda o: hasattr(o, "shape")),
         scratch_shapes=scratch,
+        input_output_aliases=dict(aliases),
         cost_estimate=pl.CostEstimate(flops=int(us * 1.15e9 * SCALE), bytes_accessed=0, transcendentals=0),
         compiler_params=pltpu.CompilerParams(vmem_limit_bytes=40 * 2**20),
         name=name,
@@ -196,14 +197,21 @@
     return mm(x, turned[first : first + x.shape[1], :])
 
 
-def theirs_body(store, _, turned, rest, out):
+def theirs_body(store, _, turned, ours, out):
     core = position()[1]
     out[...] = turn_store(store, turned, (1 - core) * FLAT)
-    rest[...] = store[:, pl.ds(pl.multiple_of(core * FLAT, FLAT), FLAT)]
-
-
-def ours_body(rest, before, turned, out):
-    out[...] = before[...] + turn_store(rest, turned, 0)
+
+    @pl.when(core == 1)
+    def _():
+        out[...] += turn_store(store, ours, FLAT)
+
+
+def ours_body(store, before, _, turned, out):
+    out[...] = before[...]
+
+    @pl.when(position()[1] == 0)
+    def _():
+        out[...] += turn_store(store, turned, 0)
 
 
 def woven(pieces, rows):
@@ -297,13 +305,12 @@
     odd_b = precondition("odd_b", (after(own, raw), other), tables, count - ROWS, 1, ROWS, us=ODDB)
     odd_b_came = [hop(odd_b, step) for step in range(1, chips)]
     turned, squares = pltpu.VMEM((FLAT, rows), bf16), pltpu.VMEM((8, rows), f32)
-    outs = [turned, pltpu.VMEM((rows, FLAT), bf16), squares]
-    turned_theirs, rest, part = call(theirs_body, "theirs", outs, [near(store), near(odd_b)], us=0.7)
+    turned_theirs, turned_ours, part = call(theirs_body, "theirs", [turned, turned, squares], [near(store), near(odd_b)], us=0.7)
     far_rows = swap(turned_theirs)
     ours = precondition("even", (after(own, part), other), tables, count, 0, us=EVEN)
     even_came = [hop(ours, step) for step in range(1, chips)]
-    ins = [near(x) for x in (after(rest, ours), part)]
-    turned_ours, squares = call(ours_body, "ours", [turned, squares], ins, us=0.6)
+    ins = [near(x) for x in (after(store, ours), part, turned_ours)]
+    turned_ours, squares = call(ours_body, "ours", [turned, squares], ins, us=0.6, aliases=[(2, 0)])
     odd_a = precondition("odd_a", (after(raw, squares), *raw_came), tables, chips * ROWS)
 
     odd_b_came = [after(x, odd_a) for x in odd_b_came]

time: 24.9 us -> 24.8 us (level)
    ppermute x4, starting transfers between devices: 0.82 us -> 1.1 us  [swap(): return lax.ppermute(x, 'ex', across)]
    ppermute x3, starting transfers between devices: 5.07 us -> 4.79 us  [hop(): lax.ppermute(x, 'ex', [(e, (e + 2 * step) % exs) for e in range(exs)])]
  transfers between devices with their start and end apart: 9 -> 9, of which waited for: 6 -> 6; matrix products, arithmetic and copies ran while one was open for 0% -> 0% of each run, Pallas kernels for 33% -> 32%
where the time goes in v10:
time: 24.8 us; the launch traced here: 24.7 us
  starting transfers between devices  10.4 us (42%)
  Pallas kernels  8.59 us (35%)
  waiting for transfers between devices  5.52 us (22%)
    pallas_call x15, Pallas kernels, call(): pl.pallas_call(body, out_shape=outs, in_specs=specs or [WHOLE] * len(ins)...  8.59 us
    ppermute x3, starting transfers between devices, hop(): lax.ppermute(x, 'ex', [(e, (e + 2 * step) % exs) for e in range(exs)])  4.79 us
    ppermute x1, starting transfers between devices, local(): lax.ppermute(messages[k // 2], 'dim', [(z, z ^ k) for z in range(dims)])  2.9 us
    ppermute x1, waiting for transfers between devices, local(): lax.ppermute(messages[k // 2], 'dim', [(z, z ^ k) for z in range(dims)])  2.02 us
    ppermute x4, waiting for transfers between devices, swap(): return lax.ppermute(x, 'ex', across)  1.67 us
    ppermute x1, starting transfers between devices, local(): got = lax.ppermute(message, 'dim', [(z, z ^ 1) for z in range(dims)])  1.64 us
    ppermute x3, waiting for transfers between devices, hop(): lax.ppermute(x, 'ex', [(e, (e + 2 * step) % exs) for e in range(exs)])  1.38 us
    ppermute x4, starting transfers between devices, swap(): return lax.ppermute(x, 'ex', across)  1.1 us
  transfers between devices with their start and end apart: 9, of which 6 were waited for; matrix products, arithmetic and copies ran while one was open for 0% of the time, Pallas kernels for 32%

profile of v10, /device:TPU:0, one launch (start us, length us, event | category | flops | bytes accessed | tf_op | source)
XLA Modules:
  0.0 24.7 jit_solution(2168611960909922484)
XLA Ops:
  0.0 0.5 %collective-permute-start = (bf16[32,8192]{1,0:T(8,128)(2,1)}, bf16[32,8192]{1,0:T(8,128)(2,1)S(1)}, u32[]{:S(2)}, u32[]{:S(2)}) collective-permute-start(bf16[32,8192]{1,0:T(8,128)(2,1)} %refs_4_.1), channel_id=1, source_target_pairs={{0,1},{1,0},{2,3},{3,2},{4,5},{5,4},{6,7},{7,6},{8,9},{9,8},{10,11... | collective-permute-start | bytes 1572872 | tf_op jit(solution)/shard_map/ppermute | solution.py:296
  0.5 1.2 %factors.1 = (bf16[64,256]{1,0:T(8,128)(2,1)S(1)}, bf16[64,256]{1,0:T(8,128)(2,1)S(1)}, bf16[256,128]{1,0:T(8,128)(2,1)S(1)}, bf16[256,256]{1,0:T(8,128)(2,1)S(1...) custom-call(f32[2,64,64]{2,1,0:T(8,128)} %refs_0_.1, f32[2,64,64]{2,1,0:T(8,128)} %refs_1_.1, f32[2,64]{1,0:T(2,128)} %refs_2_.1, ...), custom_call_target="tpu_custom_call" | custom-call | flops 27600000 | tf_op jit(solution)/shard_map/factors/pallas_call | solution.py:40
  1.6 0.6 %collective-permute-done.other.refs_1_ = bf16[32,8192]{1,0:T(8,128)(2,1)S(1)} collective-permute-done((bf16[32,8192]{1,0:T(8,128)(2,1)}, bf16[32,8192]{1,0:T(8,128)(2,1)S(1)}, u32[]{:S(2)}, u32[]{:S(2)}) %collective-permute-start) | collective-permute-done | bytes 524320 | tf_op jit(solution)/shard_map/ppermute | solution.py:296
  2.2 0.0 copy-start
  2.2 2.9 %collective-permute-start.2 = (bf16[16,4096]{1,0:T(8,128)(2,1)S(1)}, bf16[16,4096]{1,0:T(8,128)(2,1)S(1)}, u32[]{:S(2)}, u32[]{:S(2)}) collective-permute-start(bf16[16,4096]{1,0:T(8,128)(2,1)S(1)} %pick.1.refs_0_), channel_id=1, source_target_pairs={{0,2},{1,3},{2,0},{3,1},{4,6},{5,7},{6,4},{7,5},{8,10},{9,11},{10,... | collective-permute-start | bytes 393224 | tf_op jit(solution)/shard_map/ppermute | solution.py:299
  5.1 1.0 %odd_b.1._.refs_1_ = bf16[16,4096]{1,0:T(8,128)(2,1)S(1)} custom-call(bf16[32,8192]{1,0:T(8,128)(2,1)S(1)} %get-tuple-element.36.own.refs_0_, bf16[32,8192]{1,0:T(8,128)(2,1)S(1)} %collective-permute-done.other.refs_1_, bf16[64,256]{1,0:T(8,128)(2,1)S(1)} %get-tuple-element.30.refs_2_, bf16[64,256]{1,0:T(8,128)(2,1)S(1)} %get-tuple-element.31.refs_3_, ...), custom_call_target="tpu_custom_call" | custom-call | flops 23000000 | tf_op jit(solution)/shard_map/odd_b/pallas_call | solution.py:40
  6.1 0.1 collective-permute-start.3
  6.2 0.0 copy-done
  6.2 0.6 %theirs.1 = (bf16[4096,256]{1,0:T(8,128)(2,1)S(1)}, bf16[4096,256]{1,0:T(8,128)(2,1)S(1)}, f32[8,256]{1,0:T(8,128)S(1)}) custom-call(bf16[256,8192]{1,0:T(8,128)(2,1)S(1)} %copy-done, bf16[16,4096]{1,0:T(8,128)(2,1)S(1)} %odd_b.1._.refs_1_), custom_call_target="tpu_custom_call" | custom-call | flops 16100000 | tf_op jit(solution)/shard_map/theirs/pallas_call | solution.py:40
  6.9 0.6 %collective-permute-start.1 = (bf16[4096,256]{1,0:T(8,128)(2,1)S(1)}, bf16[4096,256]{1,0:T(8,128)(2,1)S(1)}, u32[]{:S(2)}, u32[]{:S(2)}) collective-permute-start(bf16[4096,256]{1,0:T(8,128)(2,1)S(1)} %get-tuple-element.40), channel_id=1, source_target_pairs={{0,1},{1,0},{2,3},{3,2},{4,5},{5,4},{6,7},{7,6},{8,9},{9,8},{10,11... | collective-permute-start | bytes 6291464 | tf_op jit(solution)/shard_map/ppermute | solution.py:296
  7.4 1.3 %even.1.refs_3_ = bf16[32,4096]{1,0:T(8,128)(2,1)S(1)} custom-call(bf16[32,8192]{1,0:T(8,128)(2,1)S(1)} %get-tuple-element.36.own.refs_0_, bf16[32,8192]{1,0:T(8,128)(2,1)S(1)} %collective-permute-done.other.refs_1_, bf16[64,256]{1,0:T(8,128)(2,1)S(1)} %get-tuple-element.30.refs_2_, bf16[64,256]{1,0:T(8,128)(2,1)S(1)} %get-tuple-element.31.refs_3_, ...), custom_call_target="tpu_custom_call" | custom-call | flops 23000000512 | tf_op jit(solution)/shard_map/even/pallas_call | solution.py:40
  8.7 1.8 %collective-permute-start.5 = (bf16[32,4096]{1,0:T(8,128)(2,1)S(1)}, bf16[32,4096]{1,0:T(8,128)(2,1)S(1)}, u32[]{:S(2)}, u32[]{:S(2)}) collective-permute-start(bf16[32,4096]{1,0:T(8,128)(2,1)S(1)} %even.1.refs_3_), channel_id=1, source_target_pairs={{0,2},{1,3},{2,0},{3,1},{4,6},{5,7},{6,4},{7,5},{8,10},{9,11},{10,... | collective-permute-start | bytes 786440 | tf_op jit(solution)/shard_map/ppermute | solution.py:299
  10.5 0.6 %ours.1 = (bf16[4096,256]{1,0:T(8,128)(2,1)S(1)}, f32[8,256]{1,0:T(8,128)S(1)}) custom-call(bf16[256,8192]{1,0:T(8,128)(2,1)S(1)} %copy-done, f32[8,256]{1,0:T(8,128)S(1)} %get-tuple-element.35.before, bf16[4096,256]{1,0:T(8,128)(2,1)S(1)} %get-tuple-element.38._), custom_call_target="tpu_custom_call", output_to_operand_aliasing={{0}: (2, {})} | custom-call | flops 13800000 | tf_op jit(solution)/shard_map/ours/pallas_call | solution.py:40
  11.2 0.0 collective-permute-done.2.refs_1_
  11.2 1.3 %odd_a.1.refs_0_ = bf16[32,4096]{1,0:T(8,128)(2,1)S(1)} custom-call(bf16[16,4096]{1,0:T(8,128)(2,1)S(1)} %pick.1.refs_0_, bf16[16,4096]{1,0:T(8,128)(2,1)S(1)} %collective-permute-done.2.refs_1_, bf16[64,256]{1,0:T(8,128)(2,1)S(1)} %get-tuple-element.30.refs_2_, bf16[64,256]{1,0:T(8,128)(2,1)S(1)} %get-tuple-element.31.refs_3_, ...), custom_call_target="tpu_custom_call" | custom-call | flops 23000000 | tf_op jit(solution)/shard_map/odd_a/pallas_call | solution.py:40
  12.5 0.0 collective-permute-done.3.refs_2_
  12.5 0.0 collective-permute-done.1.turned
  12.5 0.5 %odd_far.1 = f32[96,256]{1,0:T(8,128)S(1)} custom-call(bf16[4096,256]{1,0:T(8,128)(2,1)S(1)} %collective-permute-done.1.turned, bf16[32,4096]{1,0:T(8,128)(2,1)S(1)} %odd_a.1.refs_0_, bf16[16,4096]{1,0:T(8,128)(2,1)S(1)} %odd_b.1._.refs_1_, bf16[16,4096]{1,0:T(8,128)(2,1)S(1)} %collective-permute-done.3.refs_2_, bf16[32,4096]{1,0:T(8,128)(2,1)S(1)} %even.1.refs_3_), custom_call_target="tpu_custom_call" | custom-call | flops 11500000 | tf_op jit(solution)/shard_map/odd_far/pallas_call | solution.py:40
  13.0 0.1 collective-permute-start.4
  13.0 0.5 %odd_near.1.two = f32[96,256]{1,0:T(8,128)S(1)} custom-call(bf16[4096,256]{1,0:T(8,128)(2,1)S(1)} %get-tuple-element.43.turned, bf16[32,4096]{1,0:T(8,128)(2,1)S(1)} %odd_a.1.refs_0_, bf16[16,4096]{1,0:T(8,128)(2,1)S(1)} %odd_b.1._.refs_1_, bf16[16,4096]{1,0:T(8,128)(2,1)S(1)} %collective-permute-done.3.refs_2_, bf16[32,4096]{1,0:T(8,128)(2,1)S(1)} %even.1.refs_3_), custom_call_target="tpu_custom_call" | custom-call | flops 11500000 | tf_op jit(solution)/shard_map/odd_near/pallas_call | solution.py:40
  13.5 0.8 %collective-permute-done.4.one = f32[96,256]{1,0:T(8,128)S(1)} collective-permute-done((f32[96,256]{1,0:T(8,128)S(1)}, f32[96,256]{1,0:T(8,128)S(1)}, u32[]{:S(2)}, u32[]{:S(2)}) %collective-permute-start.4) | collective-permute-done | bytes 98336 | tf_op jit(solution)/shard_map/ppermute | solution.py:296
  14.4 1.6 %collective-permute-start.7 = (f32[72,256]{1,0:T(8,128)S(1)}, f32[72,256]{1,0:T(8,128)S(1)}, u32[]{:S(2)}, u32[]{:S(2)}) collective-permute-start(f32[72,256]{1,0:T(8,128)S(1)} %get-tuple-element.45), channel_id=1, source_target_pairs={{0,4},{4,0},{8,12},{12,8},{1,5},{5,1},{9,13},{13,9},{2,6},{6,2},{1... | collective-permute-start | bytes 221192 | tf_op jit(solution)/shard_map/ppermute | solution.py:321
  16.0 1.4 %collective-permute-done.5.refs_0_ = bf16[32,4096]{1,0:T(8,128)(2,1)S(1)} collective-permute-done((bf16[32,4096]{1,0:T(8,128)(2,1)S(1)}, bf16[32,4096]{1,0:T(8,128)(2,1)S(1)}, u32[]{:S(2)}, u32[]{:S(2)}) %collective-permute-start.5) | collective-permute-done | bytes 262176 | tf_op jit(solution)/shard_map/ppermute | solution.py:299
  17.4 0.5 %even_far.1 = f32[32,256]{1,0:T(8,128)S(1)} custom-call(bf16[4096,256]{1,0:T(8,128)(2,1)S(1)} %collective-permute-done.1.turned, bf16[32,4096]{1,0:T(8,128)(2,1)S(1)} %collective-permute-done.5.refs_0_), custom_call_target="tpu_custom_call" | custom-call | flops 11500000 | tf_op jit(solution)/shard_map/even_far/pallas_call | solution.py:40
  17.8 0.0 collective-permute-start.6
  17.9 0.5 %even_near.1.two = f32[32,256]{1,0:T(8,128)S(1)} custom-call(bf16[4096,256]{1,0:T(8,128)(2,1)S(1)} %get-tuple-element.43.turned, bf16[32,4096]{1,0:T(8,128)(2,1)S(1)} %collective-permute-done.5.refs_0_), custom_call_target="tpu_custom_call" | custom-call | flops 11500000 | tf_op jit(solution)/shard_map/even_near/pallas_call | solution.py:40
  18.3 0.5 %collective-permute-done.7.got = f32[72,256]{1,0:T(8,128)S(1)} collective-permute-done((f32[72,256]{1,0:T(8,128)S(1)}, f32[72,256]{1,0:T(8,128)S(1)}, u32[]{:S(2)}, u32[]{:S(2)}) %collective-permute-start.7) | collective-permute-done | bytes 73760 | tf_op jit(solution)/shard_map/ppermute | solution.py:321
  18.8 0.3 %collective-permute-done.6.one = f32[32,256]{1,0:T(8,128)S(1)} collective-permute-done((f32[32,256]{1,0:T(8,128)S(1)}, f32[32,256]{1,0:T(8,128)S(1)}, u32[]{:S(2)}, u32[]{:S(2)}) %collective-permute-start.6) | collective-permute-done | bytes 32800 | tf_op jit(solution)/shard_map/ppermute | solution.py:296
  19.1 2.9 %collective-permute-start.8 = (f32[72,128]{1,0:T(8,128)S(1)}, f32[72,128]{1,0:T(8,128)S(1)}, u32[]{:S(2)}, u32[]{:S(2)}) collective-permute-start(f32[72,128]{1,0:T(8,128)S(1)} %get-tuple-element.50), channel_id=1, source_target_pairs={{0,8},{4,12},{8,0},{12,4},{1,9},{5,13},{9,1},{13,5},{2,10},{6,14},... | collective-permute-start | bytes 110600 | tf_op jit(solution)/shard_map/ppermute | solution.py:335
  22.0 2.0 %collective-permute-done.8.refs_1_ = f32[72,128]{1,0:T(8,128)S(1)} collective-permute-done((f32[72,128]{1,0:T(8,128)S(1)}, f32[72,128]{1,0:T(8,128)S(1)}, u32[]{:S(2)}, u32[]{:S(2)}) %collective-permute-start.8) | collective-permute-done | bytes 36896 | tf_op jit(solution)/shard_map/ppermute | solution.py:335
  24.0 0.6 %finish.1 = f32[32,256]{1,0:T(8,128)} custom-call(f32[72,128]{1,0:T(8,128)S(1)} %get-tuple-element.49.refs_0_, f32[72,128]{1,0:T(8,128)S(1)} %collective-permute-done.8.refs_1_), custom_call_target="tpu_custom_call" | custom-call | flops 13800000 | tf_op jit(solution)/shard_map/finish/pallas_call | solution.py:40
  (4 shorter events, 0.1 us)
Async XLA Ops:
  0.0 2.2 %collective-permute-start = (bf16[32,8192]{1,0:T(8,128)(2,1)}, bf16[32,8192]{1,0:T(8,128)(2,1)S(1)}, u32[]{:S(2)}, u32[]{:S(2)}) collective-permute-start(bf16[32,8192]{1,0:T(8,128)(2,1)} %refs_4_.1), channel_id=1, source_target_pairs={{0,1},{1,0},{2,3},{3,2},{4,5},{5,4},{6,7},{7,6},{8,9},{9,8},{10,11... | collective-permute-start | bytes 1572872 | tf_op jit(solution)/shard_map/ppermute | solution.py:296
  2.2 4.0 %copy-start = (bf16[256,8192]{1,0:T(8,128)(2,1)S(1)}, bf16[256,8192]{1,0:T(8,128)(2,1)}, u32[]{:S(2)}) copy-start(bf16[256,8192]{1,0:T(8,128)(2,1)} %store.2) | copy-start | bytes 12582916
  2.2 8.9 %collective-permute-start.2 = (bf16[16,4096]{1,0:T(8,128)(2,1)S(1)}, bf16[16,4096]{1,0:T(8,128)(2,1)S(1)}, u32[]{:S(2)}, u32[]{:S(2)}) collective-permute-start(bf16[16,4096]{1,0:T(8,128)(2,1)S(1)} %pick.1.refs_0_), channel_id=1, source_target_pairs={{0,2},{1,3},{2,0},{3,1},{4,6},{5,7},{6,4},{7,5},{8,10},{9,11},{10,... | collective-permute-start | bytes 393224 | tf_op jit(solution)/shard_map/ppermute | solution.py:299
  6.1 6.3 %collective-permute-start.3 = (bf16[16,4096]{1,0:T(8,128)(2,1)S(1)}, bf16[16,4096]{1,0:T(8,128)(2,1)S(1)}, u32[]{:S(2)}, u32[]{:S(2)}) collective-permute-start(bf16[16,4096]{1,0:T(8,128)(2,1)S(1)} %odd_b.1._.refs_1_), channel_id=1, source_target_pairs={{0,2},{1,3},{2,0},{3,1},{4,6},{5,7},{6,4},{7,5},{8,10},{9,11},{10,... | collective-permute-start | bytes 393224 | tf_op jit(solution)/shard_map/ppermute | solution.py:299
  6.9 5.6 %collective-permute-start.1 = (bf16[4096,256]{1,0:T(8,128)(2,1)S(1)}, bf16[4096,256]{1,0:T(8,128)(2,1)S(1)}, u32[]{:S(2)}, u32[]{:S(2)}) collective-permute-start(bf16[4096,256]{1,0:T(8,128)(2,1)S(1)} %get-tuple-element.40), channel_id=1, source_target_pairs={{0,1},{1,0},{2,3},{3,2},{4,5},{5,4},{6,7},{7,6},{8,9},{9,8},{10,11... | collective-permute-start | bytes 6291464 | tf_op jit(solution)/shard_map/ppermute | solution.py:296
  8.7 8.6 %collective-permute-start.5 = (bf16[32,4096]{1,0:T(8,128)(2,1)S(1)}, bf16[32,4096]{1,0:T(8,128)(2,1)S(1)}, u32[]{:S(2)}, u32[]{:S(2)}) collective-permute-start(bf16[32,4096]{1,0:T(8,128)(2,1)S(1)} %even.1.refs_3_), channel_id=1, source_target_pairs={{0,2},{1,3},{2,0},{3,1},{4,6},{5,7},{6,4},{7,5},{8,10},{9,11},{10,... | collective-permute-start | bytes 786440 | tf_op jit(solution)/shard_map/ppermute | solution.py:299
  13.0 1.4 %collective-permute-start.4 = (f32[96,256]{1,0:T(8,128)S(1)}, f32[96,256]{1,0:T(8,128)S(1)}, u32[]{:S(2)}, u32[]{:S(2)}) collective-permute-start(f32[96,256]{1,0:T(8,128)S(1)} %odd_far.1), channel_id=1, source_target_pairs={{0,1},{1,0},{2,3},{3,2},{4,5},{5,4},{6,7},{7,6},{8,9},{9,8},{10,11... | collective-permute-start | bytes 294920 | tf_op jit(solution)/shard_map/ppermute | solution.py:296
  14.4 4.4 %collective-permute-start.7 = (f32[72,256]{1,0:T(8,128)S(1)}, f32[72,256]{1,0:T(8,128)S(1)}, u32[]{:S(2)}, u32[]{:S(2)}) collective-permute-start(f32[72,256]{1,0:T(8,128)S(1)} %get-tuple-element.45), channel_id=1, source_target_pairs={{0,4},{4,0},{8,12},{12,8},{1,5},{5,1},{9,13},{13,9},{2,6},{6,2},{1... | collective-permute-start | bytes 221192 | tf_op jit(solution)/shard_map/ppermute | solution.py:321
  17.8 1.2 %collective-permute-start.6 = (f32[32,256]{1,0:T(8,128)S(1)}, f32[32,256]{1,0:T(8,128)S(1)}, u32[]{:S(2)}, u32[]{:S(2)}) collective-permute-start(f32[32,256]{1,0:T(8,128)S(1)} %even_far.1), channel_id=1, source_target_pairs={{0,1},{1,0},{2,3},{3,2},{4,5},{5,4},{6,7},{7,6},{8,9},{9,8},{10,11... | collective-permute-start | bytes 98312 | tf_op jit(solution)/shard_map/ppermute | solution.py:296
  19.1 4.9 %collective-permute-start.8 = (f32[72,128]{1,0:T(8,128)S(1)}, f32[72,128]{1,0:T(8,128)S(1)}, u32[]{:S(2)}, u32[]{:S(2)}) collective-permute-start(f32[72,128]{1,0:T(8,128)S(1)} %get-tuple-element.50), channel_id=1, source_target_pairs={{0,8},{4,12},{8,0},{12,4},{1,9},{5,13},{9,1},{13,5},{2,10},{6,14},... | collective-permute-start | bytes 110600 | tf_op jit(solution)/shard_map/ppermute | solution.py:335
